TPU v7x, 32 devices: a whole 2x2x4 slice. The times are simulated.
32 devices in a mesh: grp: 2 (over x), seq: 4 (over z), frm: 4 (over y, core).
Axes of the slice: x: 2, y: 2, z: 4, core: 2. Of those that a mesh axis runs over, the one named last changes fastest.
Arguments:
- residual: bfloat16 [8, 512, 1152], P(('grp', 'frm'), 'seq'), parts along dimension 0, may hold values from -6 to 6
- spatial_query: bfloat16 [8, 512, 1152], P(('grp', 'frm'), 'seq'), parts along dimension 0, may hold values from -6 to 6
- spatial_key: bfloat16 [8, 512, 1152], P(('grp', 'frm'), 'seq'), parts along dimension 0, may hold values from -6 to 6
- spatial_value: bfloat16 [8, 512, 1152], P(('grp', 'frm'), 'seq'), parts along dimension 0, may hold values from -6 to 6
- out_weight: bfloat16 [1152, 1152], replicated, may hold values from -0.1875 to 0.1875
- qkv_weight: bfloat16 [3, 1152, 1152], replicated, may hold values from -0.1875 to 0.1875
- space_gains: float32 [2, 72], replicated, may hold values from 1 to 2
- time_gains: float32 [2, 72], replicated, may hold values from 1 to 2
- cotangent: bfloat16 [8, 512, 1152], P(('grp', 'frm'), 'seq'), parts along dimension 0, may hold values from -6 to 6
Outputs:
- grad_residual: bfloat16 [8, 512, 1152], P(('grp', 'frm'), 'seq'), parts along dimension 0
- grad_query: bfloat16 [8, 512, 1152], P(('grp', 'frm'), 'seq'), parts along dimension 0
- grad_key: bfloat16 [8, 512, 1152], P(('grp', 'frm'), 'seq'), parts along dimension 0
- grad_value: bfloat16 [8, 512, 1152], P(('grp', 'frm'), 'seq'), parts along dimension 0
There are 2 independent parts, one for each index of `grp`. A program takes and returns all parts, laid end to end along the dimension named above; an argument that names none is the same for every part. Nothing has to cross between parts.
All inputs are finite; a program needn't handle non-finite values.
Results may differ from a plain program's by a relative error of at most 0.033.
Values may be sent and summed in bfloat16 or wider, within the bound.
No kernel may reach another device: no remote copies, remote signals or barrier semaphores. Data moves between devices by JAX's collectives and lax.ppermute only.
A program may use at most 128 MiB of HBM per device.

v0:
```python
import jax
import jax.numpy as jnp
from jax import lax
from jax.sharding import PartitionSpec as P

HD = 72


norm_eps = 1e-06
space_forms = ("blhd,bmhd->bhlm", "bhlm,bmhd->blhd", "bhlm,blhd->bmhd")
time_forms = ("lbhd,mbhd->bhlm", "bhlm,mbhd->lbhd", "bhlm,lbhd->mbhd")


def product(form, left, right):
    return jnp.einsum(form, left, right, preferred_element_type=jnp.float32)


def head_norm(tensor):
    widened = tensor.astype(jnp.float32)
    inverse = lax.rsqrt(jnp.mean(widened * widened, axis=-1, keepdims=True) + norm_eps)
    return (widened * inverse, inverse)


def norm_back(upward, normed, inverse, gain):
    scaled = upward * gain
    return inverse * (scaled - normed * jnp.mean(scaled * normed, axis=-1, keepdims=True))


def attend_fwd(query_in, key_in, value_in, gain_pair, form_set):
    query_hat, query_inv = head_norm(query_in)
    key_hat, key_inv = head_norm(key_in)
    query_nrm = (query_hat * gain_pair[0]).astype(jnp.bfloat16)
    key_nrm = (key_hat * gain_pair[1]).astype(jnp.bfloat16)
    factor = query_in.shape[-1] ** (-0.5)
    scores = product(form_set[0], query_nrm, key_nrm) * factor
    expons = jnp.exp(scores)
    shares = expons / jnp.sum(expons, axis=-1, keepdims=True)
    weights = shares.astype(jnp.bfloat16)
    output = product(form_set[1], weights, value_in).astype(jnp.bfloat16)
    stored = (query_hat, key_hat, query_inv, key_inv, query_nrm, key_nrm, shares, weights)
    return (output, stored)


def attend_bwd(stored, upward, value_in, gain_pair, form_set):
    query_hat, key_hat, query_inv, key_inv, query_nrm, key_nrm, shares, weights = stored
    factor = query_hat.shape[-1] ** (-0.5)
    share_grad = product(form_set[0], upward, value_in)
    centre = jnp.sum(shares * share_grad, axis=-1, keepdims=True)
    score_grad = (shares * (share_grad - centre) * factor).astype(jnp.bfloat16)
    query_grad = product(form_set[1], score_grad, key_nrm)
    key_grad = product(form_set[2], score_grad, query_nrm)
    value_grad = product(form_set[2], weights, upward).astype(jnp.bfloat16)
    return (
        norm_back(query_grad, query_hat, query_inv, gain_pair[0]).astype(jnp.bfloat16),
        norm_back(key_grad, key_hat, key_inv, gain_pair[1]).astype(jnp.bfloat16),
        value_grad,
    )


def layer_norm(tokens_in):
    widened = tokens_in.astype(jnp.float32)
    centred = widened - jnp.mean(widened, axis=-1, keepdims=True)
    inverse = lax.rsqrt(jnp.mean(centred * centred, axis=-1, keepdims=True) + norm_eps)
    return (centred * inverse, inverse)


def layer_back(upward, normed, inverse):
    return inverse * (
        upward
        - jnp.mean(upward, axis=-1, keepdims=True)
        - normed * jnp.mean(upward * normed, axis=-1, keepdims=True)
    )


def split_heads(tensor):
    return tensor.reshape(tensor.shape[:-1] + (tensor.shape[-1] // HD, HD))


def merge_heads(tensor):
    return tensor.reshape(tensor.shape[:-2] + (tensor.shape[-2] * tensor.shape[-1],))


def project_three(lowered, qkv_weight):
    query_t = jnp.dot(lowered, qkv_weight[0], preferred_element_type=jnp.float32).astype(
        jnp.bfloat16
    )
    key_t = jnp.dot(lowered, qkv_weight[1], preferred_element_type=jnp.float32).astype(jnp.bfloat16)
    value_t = jnp.dot(lowered, qkv_weight[2], preferred_element_type=jnp.float32).astype(
        jnp.bfloat16
    )
    return (query_t, key_t, value_t)


def project_back(grad_query_t, grad_key_t, grad_value_t, qkv_weight):
    upward = jnp.dot(grad_query_t, qkv_weight[0].T, preferred_element_type=jnp.float32)
    upward = upward + jnp.dot(grad_key_t, qkv_weight[1].T, preferred_element_type=jnp.float32)
    return upward + jnp.dot(grad_value_t, qkv_weight[2].T, preferred_element_type=jnp.float32)


def local(
    residual,
    spatial_query,
    spatial_key,
    spatial_value,
    out_weight,
    qkv_weight,
    space_gains,
    time_gains,
    cotangent,
):
    query_h, key_h, value_h = (
        lax.all_to_all(spatial_query, "seq", split_axis=2, concat_axis=1, tiled=True),
        lax.all_to_all(spatial_key, "seq", split_axis=2, concat_axis=1, tiled=True),
        lax.all_to_all(spatial_value, "seq", split_axis=2, concat_axis=1, tiled=True),
    )
    attended, space_kept = attend_fwd(
        split_heads(query_h), split_heads(key_h), split_heads(value_h), space_gains, space_forms
    )
    returned = lax.all_to_all(merge_heads(attended), "seq", split_axis=1, concat_axis=2, tiled=True)
    mixed = (
        residual.astype(jnp.float32)
        + jnp.dot(returned, out_weight, preferred_element_type=jnp.float32)
    ).astype(jnp.bfloat16)
    normed, inverse = layer_norm(mixed)
    query_t, key_t, value_t = project_three(normed.astype(jnp.bfloat16), qkv_weight)
    query_f, key_f, value_f, upward_f = (
        lax.all_to_all(query_t, "frm", split_axis=2, concat_axis=0, tiled=True),
        lax.all_to_all(key_t, "frm", split_axis=2, concat_axis=0, tiled=True),
        lax.all_to_all(value_t, "frm", split_axis=2, concat_axis=0, tiled=True),
        lax.all_to_all(cotangent, "frm", split_axis=2, concat_axis=0, tiled=True),
    )
    temporal_out, time_kept = attend_fwd(
        split_heads(query_f), split_heads(key_f), split_heads(value_f), time_gains, time_forms
    )
    grads = attend_bwd(
        time_kept, split_heads(upward_f), split_heads(value_f), time_gains, time_forms
    )
    back_query, back_key, back_value = (
        lax.all_to_all(merge_heads(grads[0]), "frm", split_axis=0, concat_axis=2, tiled=True),
        lax.all_to_all(merge_heads(grads[1]), "frm", split_axis=0, concat_axis=2, tiled=True),
        lax.all_to_all(merge_heads(grads[2]), "frm", split_axis=0, concat_axis=2, tiled=True),
    )
    upward = project_back(back_query, back_key, back_value, qkv_weight)
    grad_residual = layer_back(upward, normed, inverse).astype(jnp.bfloat16)
    space_up = jnp.dot(grad_residual, out_weight.T, preferred_element_type=jnp.float32).astype(
        jnp.bfloat16
    )
    up_heads = lax.all_to_all(space_up, "seq", split_axis=2, concat_axis=1, tiled=True)
    space_grads = attend_bwd(
        space_kept, split_heads(up_heads), split_heads(value_h), space_gains, space_forms
    )
    grad_query, grad_key, grad_value = (
        lax.all_to_all(merge_heads(space_grads[0]), "seq", split_axis=1, concat_axis=2, tiled=True),
        lax.all_to_all(merge_heads(space_grads[1]), "seq", split_axis=1, concat_axis=2, tiled=True),
        lax.all_to_all(merge_heads(space_grads[2]), "seq", split_axis=1, concat_axis=2, tiled=True),
    )
    return (grad_residual, grad_query, grad_key, grad_value)


def solution(mesh):
    return jax.shard_map(
        local,
        mesh=mesh,
        in_specs=(
            P(("grp", "frm"), "seq", None),
            P(("grp", "frm"), "seq", None),
            P(("grp", "frm"), "seq", None),
            P(("grp", "frm"), "seq", None),
            P(),
            P(),
            P(),
            P(),
            P(("grp", "frm"), "seq", None),
        ),
        out_specs=(
            P(("grp", "frm"), "seq", None),
            P(("grp", "frm"), "seq", None),
            P(("grp", "frm"), "seq", None),
            P(("grp", "frm"), "seq", None),
        ),
        check_vma=False,
    )
```

profile of v0, /device:TPU:0, one launch (start us, length us, event | category | flops | bytes accessed | tf_op | source)
XLA Modules:
  0.0 384.7 jit_solution(3769090094658111535)
XLA Ops:
  2.9 6.7 %reduce.15 = bf16[1152,128]{1,0:T(8,128)(2,1)S(1)} reduce(bf16[1152,1,128]{2,1,0:T(2,128)(2,1)S(1)} %bitcast.242, bf16[]{:T(256)} %broadcast.287), dimensions={1}, to_apply=%bitcast.192.reduce_sub_computation | reduce | bytes 589826
  10.4 6.7 %all-to-all-start = ((bf16[4,2,18432]{2,1,0:T(2,128)(2,1)}), bf16[4,2,18432]{2,1,0:T(2,128)(2,1)S(1)}, u32[]{:S(2)}, u32[]{:S(2)}) async-start(bf16[4,2,18432]{2,1,0:T(2,128)(2,1)} %reshape.389), calls=%async_computation | async-start | bytes 589824 | tf_op jit(solution)/shard_map/all_to_all | solution.py:112
  18.6 7.5 %reduce.14 = bf16[1152,128]{1,0:T(8,128)(2,1)} reduce(bf16[1152,1,128]{2,1,0:T(2,128)(2,1)S(1)} %bitcast.255, bf16[]{:T(256)} %broadcast.287), dimensions={1}, to_apply=%bitcast.194.reduce_sub_computation | reduce | bytes 589826
  29.3 7.5 %reduce.13 = bf16[1152,128]{1,0:T(8,128)(2,1)} reduce(bf16[1152,1,128]{2,1,0:T(2,128)(2,1)S(1)} %bitcast.256, bf16[]{:T(256)} %broadcast.287), dimensions={1}, to_apply=%bitcast.190.reduce_sub_computation | reduce | bytes 589826
  40.1 7.5 %reduce.17 = bf16[1152,128]{1,0:T(8,128)(2,1)} reduce(bf16[1152,1,128]{2,1,0:T(2,128)(2,1)S(1)} %bitcast.257, bf16[]{:T(256)} %broadcast.287), dimensions={1}, to_apply=%bitcast.188.reduce_sub_computation | reduce | bytes 589826
  49.3 5.1 %all-to-all-start.1 = ((bf16[4,2,18432]{2,1,0:T(2,128)(2,1)}), bf16[4,2,18432]{2,1,0:T(2,128)(2,1)}, u32[]{:S(2)}, u32[]{:S(2)}) async-start(bf16[4,2,18432]{2,1,0:T(2,128)(2,1)} %reshape.391), calls=%async_computation.1 | async-start | bytes 589824 | tf_op jit(solution)/shard_map/all_to_all | solution.py:113
  57.9 5.6 %all-to-all-done.1 = bf16[4,2,18432]{2,1,0:T(2,128)(2,1)} async-done(((bf16[4,2,18432]{2,1,0:T(2,128)(2,1)}), bf16[4,2,18432]{2,1,0:T(2,128)(2,1)}, u32[]{:S(2)}, u32[]{:S(2)}) %all-to-all-start.1) | async-done | bytes 294944 | tf_op jit(solution)/shard_map/all_to_all | solution.py:113
  75.1 4.3 %all-to-all-start.7 = ((bf16[4,2,18432]{2,1,0:T(2,128)(2,1)}), bf16[4,2,18432]{2,1,0:T(2,128)(2,1)}, u32[]{:S(2)}, u32[]{:S(2)}) async-start(bf16[4,2,18432]{2,1,0:T(2,128)(2,1)} %reshape.385), calls=%async_computation.7 | async-start | bytes 589824 | tf_op jit(solution)/shard_map/all_to_all | solution.py:130
  90.1 4.0 %reduce.16 = bf16[512,288]{1,0:T(8,128)(2,1)S(1)} reduce(bf16[512,1,288]{2,1,0:T(2,128)(2,1)} %bitcast.235, bf16[]{:T(256)} %broadcast.287), dimensions={1}, to_apply=%bitcast.196.reduce_sub_computation | reduce | bytes 589826
  95.5 4.3 %all-to-all-start.3 = ((bf16[4,2,18432]{2,1,0:T(2,128)(2,1)}), bf16[4,2,18432]{2,1,0:T(2,128)(2,1)}, u32[]{:S(2)}, u32[]{:S(2)}) async-start(bf16[4,2,18432]{2,1,0:T(2,128)(2,1)} %reshape.393), calls=%async_computation.3 | async-start | bytes 589824 | tf_op jit(solution)/shard_map/all_to_all | solution.py:119
  102.8 7.3 %all-to-all-done.3 = bf16[4,2,18432]{2,1,0:T(2,128)(2,1)} async-done(((bf16[4,2,18432]{2,1,0:T(2,128)(2,1)}), bf16[4,2,18432]{2,1,0:T(2,128)(2,1)}, u32[]{:S(2)}, u32[]{:S(2)}) %all-to-all-start.3) | async-done | bytes 294944 | tf_op jit(solution)/shard_map/all_to_all | solution.py:119
  123.2 7.7 %reduce.19 = bf16[1152,128]{1,0:T(8,128)(2,1)S(1)} reduce(bf16[1152,1,128]{2,1,0:T(2,128)(2,1)} %bitcast.247, bf16[]{:T(256)} %broadcast.287), dimensions={1}, to_apply=%bitcast.200.reduce_sub_computation | reduce | bytes 589826
  131.7 3.9 %all-to-all-start.4 = ((bf16[4,2,18432]{2,1,0:T(2,128)(2,1)}), bf16[4,2,18432]{2,1,0:T(2,128)(2,1)S(1)}, u32[]{:S(2)}, u32[]{:S(2)}) async-start(bf16[4,2,18432]{2,1,0:T(2,128)(2,1)} %reshape.397), calls=%async_computation.4 | async-start | bytes 589824 | tf_op jit(solution)/shard_map/all_to_all | solution.py:127
  140.9 8.4 %reduce.18 = bf16[1152,128]{1,0:T(8,128)(2,1)} reduce(bf16[1152,1,128]{2,1,0:T(2,128)(2,1)} %bitcast.248, bf16[]{:T(256)} %broadcast.287), dimensions={1}, to_apply=%bitcast.198.reduce_sub_computation | reduce | bytes 589826
  160.4 8.4 %reduce.20 = bf16[1152,128]{1,0:T(8,128)(2,1)} reduce(bf16[1152,1,128]{2,1,0:T(2,128)(2,1)} %bitcast.249, bf16[]{:T(256)} %broadcast.287), dimensions={1}, to_apply=%bitcast.202.reduce_sub_computation | reduce | bytes 589826
  178.6 4.3 %all-to-all-start.6 = ((bf16[4,2,18432]{2,1,0:T(2,128)(2,1)}), bf16[4,2,18432]{2,1,0:T(2,128)(2,1)}, u32[]{:S(2)}, u32[]{:S(2)}) async-start(bf16[4,2,18432]{2,1,0:T(2,128)(2,1)} %reshape.399), calls=%async_computation.6 | async-start | bytes 589824 | tf_op jit(solution)/shard_map/all_to_all | solution.py:129
  199.1 4.1 %fusion.99 = f32[128,4,4,4]{2,3,1,0:T(4,128)} fusion(f32[4,128,4,72]{3,0,2,1:T(4,128)} %copy.157, f32[72]{0:T(128)} %get-tuple-element.21, f32[4,128,4]{0,2,1:T(4,128)} %copy.156, f32[4,128,4,72]{3,0,2,1:T(4,128)} %copy.158, f32[72]{0:T(128)} %get-tuple-element.20, f32[4,128,4]{0,2,1:T(4,128)} %copy.153), kind=kOutput, calls=%fused_computation.96 | convolution fusion | flops 2082819 | bytes 1229376 | tf_op jit(solution)/shard_map/div | solution.py:37
  203.3 7.3 %multiply_reduce_fusion.2 = (f32[4,128,4]{0,2,1:T(4,128)}, f32[4,128,4,72]{3,0,2,1:T(4,128)}) fusion(f32[4,128,4,72]{3,0,2,1:T(4,128)} %copy.158, f32[4,128,4]{0,2,1:T(4,128)} %copy.153, f32[72]{0:T(128)S(1)} %copy-done.16, f32[128,4,4,4]{2,3,1,0:T(4,128)} %fusion.99, f32[128,4,4,4]{2,3,1,0:T(4,128)} %convolution_bitcast_fusion.1, ...), kind=kOutput, calls=%fused_computation.68 | convolution fusion | flops 2252803 | bytes 1860160 | tf_op jit(solution)/shard_map/bhlm,mbhd->lbhd/dot_general | solution.py:15
  210.6 6.4 %multiply_reduce_fusion.1 = (f32[4,128,4]{0,2,1:T(4,128)}, f32[4,128,4,72]{3,0,2,1:T(4,128)}) fusion(f32[4,128,4,72]{3,0,2,1:T(4,128)} %copy.157, f32[4,128,4]{0,2,1:T(4,128)S(1)} %copy-done.9, f32[72]{0:T(128)S(1)} %copy-done.17, f32[128,4,4,4]{2,3,1,0:T(4,128)} %fusion.99, f32[128,4,4,4]{2,3,1,0:T(4,128)} %convolution_bitcast_fusion.1, ...), kind=kOutput, calls=%fused_computation.66 | convolution fusion | flops 2252803 | bytes 1860160 | tf_op jit(solution)/shard_map/bhlm,lbhd->mbhd/dot_general | solution.py:15
  218.9 3.9 %multiply_convert_fusion.2 = bf16[4,128,4,72]{3,0,2,1:T(4,128)(2,1)} fusion(f32[4,128,4,72]{3,0,2,1:T(4,128)} %get-tuple-element.31, f32[4,128,4,72]{3,0,2,1:T(4,128)} %copy.158, f32[4,128,4]{0,2,1:T(4,128)} %copy.165, f32[4,128,4]{0,2,1:T(4,128)} %copy.153), kind=kLoop, calls=%fused_computation.67 | loop fusion | flops 737280 | bytes 1490944 | tf_op jit(solution)/shard_map/convert_element_type | solution.py:54
  226.9 3.8 multiply_convert_fusion.1
  242.7 4.1 %all-to-all-start.10 = ((bf16[4,128,288]{1,2,0:T(8,128)(2,1)}), bf16[4,128,288]{1,2,0:T(8,128)(2,1)}, u32[]{:S(2)}, u32[]{:S(2)}) async-start(bf16[4,128,288]{1,2,0:T(8,128)(2,1)} %bitcast.52), calls=%async_computation.10 | async-start | bytes 589824 | tf_op jit(solution)/shard_map/all_to_all | solution.py:141
  263.2 4.3 %fusion.94 = (f32[128]{0:T(128)}, f32[128,1152]{1,0:T(8,128)}) fusion(f32[1,128,1152]{2,1,0:T(8,128)S(1)} %get-tuple-element.27, f32[128]{0:T(128)} %copy-done.13, f32[128]{0:T(128)} %copy-done.12, f32[128,1152]{1,0:T(8,128)} %fusion.7, f32[128,1152]{1,0:T(8,128)} %fusion.11, bf16[128,1152]{0,1:T(8,128)(2,1)S(1)} %bitcast.258, bf16[3,1152,1152]{2,1,0:T(8,128)(2,1)} %param.14), kind=kOutput, calls=%fused_computation.76 | convolution fusion | flops 340623232 | bytes 5309952 | tf_op jit(solution)/shard_map/dot_general | solution.py:95
  273.1 6.7 %reduce.21 = bf16[1152,128]{1,0:T(8,128)(2,1)S(1)} reduce(bf16[1152,1,128]{2,1,0:T(2,128)(2,1)S(1)} %bitcast.253, bf16[]{:T(256)} %broadcast.287), dimensions={1}, to_apply=%bitcast.204.reduce_sub_computation | reduce | bytes 589826
  279.9 12.0 %all_to_all.210 = bf16[4,2,18432]{2,1,0:T(2,128)(2,1)S(1)} all-to-all(bf16[4,2,18432]{2,1,0:T(2,128)(2,1)S(1)} %reshape.401), channel_id=1, replica_groups=mesh['grp'=2,'seq'=4,'frm'=4] {'seq'}, dimensions={0} | all-to-all | bytes 589824 | tf_op jit(solution)/shard_map/all_to_all | solution.py:148
  301.9 4.8 %reduce.24 = bf16[512,288]{1,0:T(8,128)(2,1)} reduce(bf16[512,1,288]{2,1,0:T(2,128)(2,1)} %bitcast.237, bf16[]{:T(256)} %broadcast.287), dimensions={1}, to_apply=%bitcast.210.reduce_sub_computation | reduce | bytes 589826
  312.7 9.7 %multiply_reduce_fusion.4 = (f32[512,4]{0,1:T(4,128)}, f32[1,512,4,72]{1,3,2,0:T(8,128)}) fusion(f32[1,512,4,72]{1,3,2,0:T(8,128)S(1)} %copy-done.2, f32[512,4]{0,1:T(4,128)S(1)} %get-tuple-element.38, f32[72]{0:T(128)} %get-tuple-element.22, f32[4,512,512]{1,2,0:T(8,128)} %fusion.129, f32[4,512]{1,0:T(4,128)} %copy-done.11, f32[4,512,512]{1,2,0:T(8,128)} %copy-done.3, ...), kind=kOutput, calls=%fused_computation.83 | convolution fusion | flops 161464832 | bytes 10191424 | tf_op jit(solution)/shard_map/bhlm,blhd->bmhd/dot_general | solution.py:15
  328.0 4.8 %reduce.23 = bf16[512,288]{1,0:T(8,128)(2,1)} reduce(bf16[512,1,288]{2,1,0:T(2,128)(2,1)} %bitcast.238, bf16[]{:T(256)} %broadcast.287), dimensions={1}, to_apply=%bitcast.208.reduce_sub_computation | reduce | bytes 589826
  335.1 9.7 %multiply_reduce_fusion.5 = (f32[512,4]{0,1:T(4,128)}, f32[1,512,4,72]{1,3,2,0:T(8,128)}) fusion(f32[1,512,4,72]{1,3,2,0:T(8,128)S(1)} %copy-done.1, f32[512,4]{0,1:T(4,128)S(1)} %get-tuple-element.39, f32[72]{0:T(128)} %get-tuple-element.23, f32[4,512,512]{1,2,0:T(8,128)} %fusion.129, f32[4,512]{1,0:T(4,128)} %copy-done.11, f32[4,512,512]{1,2,0:T(8,128)} %copy-done.3, ...), kind=kOutput, calls=%fused_computation.85 | convolution fusion | flops 161464832 | bytes 10191424 | tf_op jit(solution)/shard_map/bhlm,bmhd->blhd/dot_general | solution.py:15
  344.7 5.1 %all-to-all-start.13 = ((bf16[4,2,18432]{2,1,0:T(2,128)(2,1)}), bf16[4,2,18432]{2,1,0:T(2,128)(2,1)}, u32[]{:S(2)}, u32[]{:S(2)}) async-start(bf16[4,2,18432]{2,1,0:T(2,128)(2,1)} %reshape.405), calls=%async_computation.13 | async-start | bytes 589824 | tf_op jit(solution)/shard_map/all_to_all | solution.py:154
  355.1 4.0 %reduce.22 = bf16[512,288]{1,0:T(8,128)(2,1)S(1)} reduce(bf16[512,1,288]{2,1,0:T(2,128)(2,1)} %bitcast.234, bf16[]{:T(256)} %broadcast.287), dimensions={1}, to_apply=%bitcast.206.reduce_sub_computation | reduce | bytes 589826
  360.4 5.1 %all-to-all-start.12 = ((bf16[4,2,18432]{2,1,0:T(2,128)(2,1)}), bf16[4,2,18432]{2,1,0:T(2,128)(2,1)}, u32[]{:S(2)}, u32[]{:S(2)}) async-start(bf16[4,2,18432]{2,1,0:T(2,128)(2,1)} %reshape.403), calls=%async_computation.12 | async-start | bytes 589824 | tf_op jit(solution)/shard_map/all_to_all | solution.py:153
  (176 shorter events, 188.0 us)
Async XLA Ops:
  0.6 115.3 %copy-start = (bf16[1152,1152]{1,0:T(8,128)(2,1)S(1)}, bf16[1152,1152]{1,0:T(8,128)(2,1)}, u32[]{:S(2)}) copy-start(bf16[1152,1152]{1,0:T(8,128)(2,1)} %param.13) | copy-start | bytes 7962628
  10.4 44.0 %copy-start.14 = (f32[2,72]{1,0:T(2,128)S(1)}, f32[2,72]{1,0:T(2,128)}, u32[]{:S(2)}) copy-start(f32[2,72]{1,0:T(2,128)} %param.15) | copy-start | bytes 1732
  10.4 38.9 %all-to-all-start = ((bf16[4,2,18432]{2,1,0:T(2,128)(2,1)}), bf16[4,2,18432]{2,1,0:T(2,128)(2,1)S(1)}, u32[]{:S(2)}, u32[]{:S(2)}) async-start(bf16[4,2,18432]{2,1,0:T(2,128)(2,1)} %reshape.389), calls=%async_computation | async-start | bytes 589824 | tf_op jit(solution)/shard_map/all_to_all | solution.py:112
  49.3 14.2 %all-to-all-start.1 = ((bf16[4,2,18432]{2,1,0:T(2,128)(2,1)}), bf16[4,2,18432]{2,1,0:T(2,128)(2,1)}, u32[]{:S(2)}, u32[]{:S(2)}) async-start(bf16[4,2,18432]{2,1,0:T(2,128)(2,1)} %reshape.391), calls=%async_computation.1 | async-start | bytes 589824 | tf_op jit(solution)/shard_map/all_to_all | solution.py:113
  63.5 11.6 %all-to-all-start.2 = ((bf16[4,2,18432]{2,1,0:T(2,128)(2,1)}), bf16[4,2,18432]{2,1,0:T(2,128)(2,1)S(1)}, u32[]{:S(2)}, u32[]{:S(2)}) async-start(bf16[4,2,18432]{2,1,0:T(2,128)(2,1)} %reshape.387), calls=%async_computation.2 | async-start | bytes 589824 | tf_op jit(solution)/shard_map/all_to_all | solution.py:114
  70.8 13.5 %copy-start.4 = (f32[512,4,72]{0,2,1:T(8,128)S(1)}, f32[512,4,72]{0,2,1:T(8,128)}, u32[]{:S(2)}) copy-start(f32[512,4,72]{0,2,1:T(8,128)} %reshape.373) | copy-start | bytes 1769476
  75.1 20.4 %all-to-all-start.7 = ((bf16[4,2,18432]{2,1,0:T(2,128)(2,1)}), bf16[4,2,18432]{2,1,0:T(2,128)(2,1)}, u32[]{:S(2)}, u32[]{:S(2)}) async-start(bf16[4,2,18432]{2,1,0:T(2,128)(2,1)} %reshape.385), calls=%async_computation.7 | async-start | bytes 589824 | tf_op jit(solution)/shard_map/all_to_all | solution.py:130
  83.5 3.6 copy-start.5
  86.3 1.9 copy-start.3
  86.3 1.9 copy-start.11
  86.3 13.5 %copy-start.15 = (f32[2,72]{1,0:T(2,128)S(1)}, f32[2,72]{1,0:T(2,128)}, u32[]{:S(2)}) copy-start(f32[2,72]{1,0:T(2,128)} %param.16) | copy-start | bytes 1732
  95.5 14.7 %all-to-all-start.3 = ((bf16[4,2,18432]{2,1,0:T(2,128)(2,1)}), bf16[4,2,18432]{2,1,0:T(2,128)(2,1)}, u32[]{:S(2)}, u32[]{:S(2)}) async-start(bf16[4,2,18432]{2,1,0:T(2,128)(2,1)} %reshape.393), calls=%async_computation.3 | async-start | bytes 589824 | tf_op jit(solution)/shard_map/all_to_all | solution.py:119
  117.7 0.5 copy-start.12
  118.2 0.6 copy-start.13
  118.9 0.7 copy-start.10
  131.7 19.3 %all-to-all-start.4 = ((bf16[4,2,18432]{2,1,0:T(2,128)(2,1)}), bf16[4,2,18432]{2,1,0:T(2,128)(2,1)S(1)}, u32[]{:S(2)}, u32[]{:S(2)}) async-start(bf16[4,2,18432]{2,1,0:T(2,128)(2,1)} %reshape.397), calls=%async_computation.4 | async-start | bytes 589824 | tf_op jit(solution)/shard_map/all_to_all | solution.py:127
  151.0 0.7 copy-start.8
  151.7 26.9 %all-to-all-start.5 = ((bf16[4,2,18432]{2,1,0:T(2,128)(2,1)}), bf16[4,2,18432]{2,1,0:T(2,128)(2,1)S(1)}, u32[]{:S(2)}, u32[]{:S(2)}) async-start(bf16[4,2,18432]{2,1,0:T(2,128)(2,1)} %reshape.395), calls=%async_computation.5 | async-start | bytes 589824 | tf_op jit(solution)/shard_map/all_to_all | solution.py:128
  178.6 13.3 %all-to-all-start.6 = ((bf16[4,2,18432]{2,1,0:T(2,128)(2,1)}), bf16[4,2,18432]{2,1,0:T(2,128)(2,1)}, u32[]{:S(2)}, u32[]{:S(2)}) async-start(bf16[4,2,18432]{2,1,0:T(2,128)(2,1)} %reshape.399), calls=%async_computation.6 | async-start | bytes 589824 | tf_op jit(solution)/shard_map/all_to_all | solution.py:129
  199.1 4.1 %copy-start.9 = (f32[4,128,4]{0,2,1:T(4,128)S(1)}, f32[4,128,4]{0,2,1:T(4,128)}, u32[]{:S(2)}) copy-start(f32[4,128,4]{0,2,1:T(4,128)} %copy.156) | copy-start | bytes 24580
  199.1 4.1 %copy-start.16 = (f32[72]{0:T(128)S(1)}, f32[72]{0:T(128)}, u32[]{:S(2)}) copy-start(f32[72]{0:T(128)} %get-tuple-element.20) | copy-start | bytes 868
  199.1 4.1 %copy-start.17 = (f32[72]{0:T(128)S(1)}, f32[72]{0:T(128)}, u32[]{:S(2)}) copy-start(f32[72]{0:T(128)} %get-tuple-element.21) | copy-start | bytes 868
  232.9 9.8 %all-to-all-start.9 = ((bf16[4,128,288]{1,2,0:T(8,128)(2,1)}), bf16[4,128,288]{1,2,0:T(8,128)(2,1)S(1)}, u32[]{:S(2)}, u32[]{:S(2)}) async-start(bf16[4,128,288]{1,2,0:T(8,128)(2,1)} %bitcast.46), calls=%async_computation.9 | async-start | bytes 589824 | tf_op jit(solution)/shard_map/all_to_all | solution.py:140
  242.7 10.5 %all-to-all-start.10 = ((bf16[4,128,288]{1,2,0:T(8,128)(2,1)}), bf16[4,128,288]{1,2,0:T(8,128)(2,1)}, u32[]{:S(2)}, u32[]{:S(2)}) async-start(bf16[4,128,288]{1,2,0:T(8,128)(2,1)} %bitcast.52), calls=%async_computation.10 | async-start | bytes 589824 | tf_op jit(solution)/shard_map/all_to_all | solution.py:141
  253.2 10.0 %all-to-all-start.8 = ((bf16[4,128,288]{1,2,0:T(8,128)(2,1)}), bf16[4,128,288]{1,2,0:T(8,128)(2,1)S(1)}, u32[]{:S(2)}, u32[]{:S(2)}) async-start(bf16[4,128,288]{1,2,0:T(8,128)(2,1)} %bitcast.266), calls=%async_computation.8 | async-start | bytes 589824 | tf_op jit(solution)/shard_map/all_to_all | solution.py:139
  270.7 0.7 copy-start.7
  292.5 3.8 copy-start.6
  296.4 16.3 %copy-start.2 = (f32[1,512,4,72]{1,3,2,0:T(8,128)S(1)}, f32[1,512,4,72]{1,3,2,0:T(8,128)}, u32[]{:S(2)}) copy-start(f32[1,512,4,72]{1,3,2,0:T(8,128)} %reshape.376) | copy-start | bytes 1769476
  308.9 35.8 %all-to-all-start.14 = ((bf16[4,2,18432]{2,1,0:T(2,128)(2,1)}), bf16[4,2,18432]{2,1,0:T(2,128)(2,1)S(1)}, u32[]{:S(2)}, u32[]{:S(2)}) async-start(bf16[4,2,18432]{2,1,0:T(2,128)(2,1)} %reshape.407), calls=%async_computation.14 | async-start | bytes 589824 | tf_op jit(solution)/shard_map/all_to_all | solution.py:155
  322.4 12.7 %copy-start.1 = (f32[1,512,4,72]{1,3,2,0:T(8,128)S(1)}, f32[1,512,4,72]{1,3,2,0:T(8,128)}, u32[]{:S(2)}) copy-start(f32[1,512,4,72]{1,3,2,0:T(8,128)} %reshape.374) | copy-start | bytes 1769476
  344.7 15.7 %all-to-all-start.13 = ((bf16[4,2,18432]{2,1,0:T(2,128)(2,1)}), bf16[4,2,18432]{2,1,0:T(2,128)(2,1)}, u32[]{:S(2)}, u32[]{:S(2)}) async-start(bf16[4,2,18432]{2,1,0:T(2,128)(2,1)} %reshape.405), calls=%async_computation.13 | async-start | bytes 589824 | tf_op jit(solution)/shard_map/all_to_all | solution.py:154
  360.4 17.0 %all-to-all-start.12 = ((bf16[4,2,18432]{2,1,0:T(2,128)(2,1)}), bf16[4,2,18432]{2,1,0:T(2,128)(2,1)}, u32[]{:S(2)}, u32[]{:S(2)}) async-start(bf16[4,2,18432]{2,1,0:T(2,128)(2,1)} %reshape.403), calls=%async_computation.12 | async-start | bytes 589824 | tf_op jit(solution)/shard_map/all_to_all | solution.py:153
where the time goes:
time: 392 us; the launch traced here: 385 us
  local copies, waits for them, and re-layouts  110 us (28%)
  other arithmetic  104 us (27%)
  matrix products  75 us (19%)
  starting transfers between devices  60.6 us (15%)
  waiting for transfers between devices  20.7 us (5%)
  blocking collectives  12 us (3%)
    unnamed x12, other arithmetic  78 us
    unnamed x72, local copies, waits for them, and re-layouts  54.7 us
    dot_general x10, matrix products, product(): return jnp.einsum(form, left, right, preferred_element_type=jnp.float32)  48.2 us
    all_to_all x1, blocking collectives, local(): lax.all_to_all(space_up, 'seq', split_axis=2, concat_axis=1, tiled=True)  12 us
    reshape x4, local copies, waits for them, and re-layouts, merge_heads(): tensor.reshape(tensor.shape[:-2] + (tensor.shape[-2] * tensor.shape[-1],))  10.1 us
    convert_element_type x8, local copies, waits for them, and re-layouts, head_norm(): widened = tensor.astype(jnp.float32)  9.92 us
  transfers between devices with their start and end apart: 14, of which 6 were waited for; matrix products, arithmetic and copies ran while one was open for 46% of the time, Pallas kernels for 0%

commit v1 on v0

v1 whole, which is shorter than its diff:
```python
import functools

import jax
import jax.numpy as jnp
from jax import lax
from jax.experimental import pallas as pl
from jax.experimental.pallas import tpu as pltpu
from jax.sharding import PartitionSpec as P

HD = 72
EPS = 1e-06
F32 = jnp.float32
BF16 = jnp.bfloat16
LANES = 128
VMEM_LIMIT = 56 * 1024 * 1024

PARAMS = pltpu.CompilerParams(vmem_limit_bytes=VMEM_LIMIT)


def dot(left, right, dims):
    return lax.dot_general(left, right, (dims, ((), ())), preferred_element_type=F32)


def rounded(value):
    return value.astype(BF16).astype(F32)


def head_norm(tensor):
    inverse = lax.rsqrt(jnp.mean(tensor * tensor, axis=-2, keepdims=True) + EPS)
    return (tensor * inverse, inverse)


def norm_back(upward, hat, inverse, gain):
    scaled = upward * gain
    return inverse * (scaled - hat * jnp.mean(scaled * hat, axis=-2, keepdims=True))


def exchange_lanes(blocks, width):
    count = len(blocks)
    group = lax.broadcasted_iota(jnp.int32, blocks[0].shape, 1) // width
    results = []
    for a in range(count):
        result = None
        for b in range(count):
            shift = (width * (b - a)) % (width * count)
            moved = blocks[b] if shift == 0 else pltpu.roll(blocks[b], shift, 1)
            result = moved if result is None else jnp.where(group == b, moved, result)
        results.append(result)
    return results


def is_dense(rows, parts):
    return rows % (8 * parts) == 0


def pack(tile, parts):
    rows, width = tile.shape[0], tile.shape[1] // parts
    if is_dense(rows, parts):
        own = rows // parts
        return exchange_lanes([tile[b * own : (b + 1) * own] for b in range(parts)], width)
    return [tile[:, b * width : (b + 1) * width] for b in range(parts)]


def unpack(blocks):
    parts = len(blocks)
    if blocks[0].shape[1] * parts == LANES:
        return jnp.concatenate(blocks, axis=1)
    return jnp.concatenate(exchange_lanes(blocks, blocks[0].shape[1] // parts), axis=0)


def block_shape(rows, parts):
    if is_dense(rows, parts):
        return (rows // parts, LANES)
    return (rows, LANES // parts)


def turn_kernel(axis, q_ref, k_ref, v_ref, *rest):
    out_refs, held = rest[:-1], rest[-1]
    count = len(out_refs)
    rows = out_refs[0].shape[1]
    me = lax.axis_index(axis)
    for n, ref in enumerate((q_ref, k_ref, v_ref)):
        held[n] = ref[...].astype(F32).T.astype(BF16)
    for s in range(count):
        start = pl.multiple_of((me ^ s) * rows, rows)
        out_refs[s][...] = held[:, pl.ds(start, rows), :]


def turn(axis, count, arrays):
    tokens, width = arrays[0].shape
    return pl.pallas_call(
        functools.partial(turn_kernel, axis),
        out_shape=[jax.ShapeDtypeStruct((3, width // count, tokens), BF16)] * count,
        scratch_shapes=[pltpu.VMEM((3, width, tokens), BF16)],
        compiler_params=PARAMS,
        name="turn",
    )(*arrays)


def unturn_kernel(axis, *refs):
    count = len(refs) - 4
    in_refs, out_refs, held = refs[:count], refs[count:-1], refs[-1]
    rows = in_refs[0].shape[1]
    me = lax.axis_index(axis)
    for s in range(count):
        start = pl.multiple_of((me ^ s) * rows, rows)
        held[:, pl.ds(start, rows), :] = in_refs[s][...]
    for n, ref in enumerate(out_refs):
        ref[...] = held[n].astype(F32).T.astype(BF16)


def unturn(axis, arrays):
    count = len(arrays)
    _, rows, tokens = arrays[0].shape
    return pl.pallas_call(
        functools.partial(unturn_kernel, axis),
        out_shape=[jax.ShapeDtypeStruct((tokens, rows * count), BF16)] * 3,
        scratch_shapes=[pltpu.VMEM((3, rows * count, tokens), BF16)],
        compiler_params=PARAMS,
        name="unturn",
    )(*arrays)


def gather_part(refs, part):
    return jnp.concatenate([ref[part].astype(F32) for ref in refs], axis=1)


def space_fwd_kernel(axis, parts, gain_ref, *refs):
    in_refs, out_ref, held = refs[:-2], refs[-2], refs[-1]
    count = len(in_refs)
    rows = in_refs[0].shape[1]
    me = lax.axis_index(axis)
    query, key, value = (gather_part(in_refs, n) for n in range(3))
    factor = HD ** (-0.5)
    for h in range(rows // HD):
        cut = slice(h * HD, (h + 1) * HD)
        query_nrm = (head_norm(query[cut])[0] * gain_ref[0]).astype(BF16)
        key_nrm = (head_norm(key[cut])[0] * gain_ref[1]).astype(BF16)
        scores = dot(key_nrm, query_nrm, ((0,), (0,)))
        expons = jnp.exp(scores * factor)
        total = jnp.sum(expons, axis=0, keepdims=True)
        attended = dot(value[cut].astype(BF16), expons.astype(BF16), ((1,), (0,)))
        held[cut, :] = attended * (1.0 / total)
    for s in range(count):
        blocks = pack(held[:, s * LANES : (s + 1) * LANES], parts)
        for f, block in enumerate(blocks):
            out_ref[(me ^ s) * parts + f] = block.astype(BF16)


def space_fwd(axis, parts, gains, arrays):
    count = len(arrays)
    _, rows, tokens = arrays[0].shape
    return pl.pallas_call(
        functools.partial(space_fwd_kernel, axis, parts),
        out_shape=jax.ShapeDtypeStruct((count * parts,) + block_shape(rows, parts), BF16),
        scratch_shapes=[pltpu.VMEM((rows, count * tokens), F32)],
        compiler_params=PARAMS,
        name="space_fwd",
    )(gains, *arrays)


def space_bwd_kernel(axis, parts, gain_ref, up_ref, *refs):
    count = (len(refs) - 1) // 2
    in_refs, out_refs, held = refs[:count], refs[count:-1], refs[-1]
    rows = in_refs[0].shape[1]
    me = lax.axis_index(axis)
    for s in range(count):
        blocks = [up_ref[(me ^ s) * parts + f].astype(F32) for f in range(parts)]
        held[:, s * LANES : (s + 1) * LANES] = unpack(blocks)
    query, key, value = (gather_part(in_refs, n) for n in range(3))
    factor = HD ** (-0.5)
    grads = []
    for h in range(rows // HD):
        cut = slice(h * HD, (h + 1) * HD)
        query_hat, query_inv = head_norm(query[cut])
        key_hat, key_inv = head_norm(key[cut])
        query_nrm = (query_hat * gain_ref[0]).astype(BF16)
        key_nrm = (key_hat * gain_ref[1]).astype(BF16)
        up = held[cut, :].astype(BF16)
        scores = dot(key_nrm, query_nrm, ((0,), (0,)))
        expons = jnp.exp(scores * factor)
        shares = expons * (1.0 / jnp.sum(expons, axis=0, keepdims=True))
        share_grad = dot(value[cut].astype(BF16), up, ((0,), (0,)))
        centre = jnp.sum(shares * share_grad, axis=0, keepdims=True)
        score_grad = (shares * (share_grad - centre) * factor).astype(BF16)
        query_grad = dot(key_nrm, score_grad, ((1,), (0,)))
        key_grad = dot(query_nrm, score_grad, ((1,), (1,)))
        value_grad = dot(up, shares.astype(BF16), ((1,), (1,)))
        grads.append(
            (
                norm_back(query_grad, query_hat, query_inv, gain_ref[0]),
                norm_back(key_grad, key_hat, key_inv, gain_ref[1]),
                value_grad,
            )
        )
    for n in range(3):
        whole = jnp.concatenate([grad[n] for grad in grads], axis=0).astype(BF16)
        for s in range(count):
            out_refs[s][n] = whole[:, s * LANES : (s + 1) * LANES]


def space_bwd(axis, parts, gains, up, arrays):
    count = len(arrays)
    _, rows, tokens = arrays[0].shape
    return pl.pallas_call(
        functools.partial(space_bwd_kernel, axis, parts),
        out_shape=[jax.ShapeDtypeStruct((3, rows, tokens), BF16)] * count,
        scratch_shapes=[pltpu.VMEM((rows, count * tokens), F32)],
        compiler_params=PARAMS,
        name="space_bwd",
    )(gains, up, *arrays)


def time_head(query_in, key_in, value, upward, query_gain, key_gain, parts):
    width = LANES // parts
    factor = HD ** (-0.5)
    query_hat, query_inv = head_norm(query_in)
    key_hat, key_inv = head_norm(key_in)
    query_nrm = rounded(query_hat * query_gain)
    key_nrm = rounded(key_hat * key_gain)

    def turned(tensor, r):
        shift = (r * width) % LANES
        return tensor if shift == 0 else pltpu.roll(tensor, shift, 1)

    keys = [turned(key_nrm, r) for r in range(parts)]
    expons = [jnp.exp(jnp.sum(query_nrm * keys[r], axis=0, keepdims=True) * factor) for r in range(parts)]
    scale = 1.0 / functools.reduce(jnp.add, expons)
    shares = [expon * scale for expon in expons]
    share_grads = [jnp.sum(upward * turned(value, r), axis=0, keepdims=True) for r in range(parts)]
    centre = functools.reduce(jnp.add, [a * b for a, b in zip(shares, share_grads)])
    score_grads = [rounded(shares[r] * (share_grads[r] - centre) * factor) for r in range(parts)]
    query_grad = functools.reduce(jnp.add, [score_grads[r] * keys[r] for r in range(parts)])
    key_grad = functools.reduce(jnp.add, [turned(score_grads[r] * query_nrm, -r) for r in range(parts)])
    value_grad = functools.reduce(jnp.add, [turned(rounded(shares[r]) * upward, -r) for r in range(parts)])
    return (
        norm_back(query_grad, query_hat, query_inv, query_gain),
        norm_back(key_grad, key_hat, key_inv, key_gain),
        value_grad,
    )


def middle_kernel(
    count,
    parts,
    att_ref,
    res_ref,
    cot_ref,
    gain_ref,
    ow_hbm,
    qw_hbm,
    gr_ref,
    up_ref,
    ow_ref,
    qw_ref,
    att_s,
    low_s,
    cot_s,
    qkv_s,
    grad_s,
    sems,
):
    width = ow_ref.shape[0]
    rows = width // count
    copies = [pltpu.make_async_copy(ow_hbm, ow_ref, sems.at[0])]
    copies += [pltpu.make_async_copy(qw_hbm.at[n], qw_ref.at[n], sems.at[1 + n]) for n in range(3)]
    for copy in copies:
        copy.start()
    for z in range(count):
        att_s[z * rows : (z + 1) * rows, :] = unpack(
            [att_ref[z * parts + f].astype(F32) for f in range(parts)]
        )
    attended = att_s[...].T.astype(BF16)
    cot_s[...] = cot_ref[...].reshape(LANES, width).astype(F32).T
    copies[0].wait()
    mixed = rounded(
        res_ref[...].reshape(LANES, width).astype(F32) + dot(attended, ow_ref[...], ((1,), (0,)))
    )
    centred = mixed - jnp.mean(mixed, axis=1, keepdims=True)
    inverse = lax.rsqrt(jnp.mean(centred * centred, axis=1, keepdims=True) + EPS)
    normed = centred * inverse
    low_s[...] = normed
    lowered = normed.astype(BF16)
    for n in range(3):
        copies[1 + n].wait()
        product = rounded(dot(lowered, qw_ref[n], ((1,), (0,))))
        qkv_s[n] = product.T
    for h in range(width // HD):
        cut = slice(h * HD, (h + 1) * HD)
        grads = time_head(
            qkv_s[0, cut], qkv_s[1, cut], qkv_s[2, cut], cot_s[cut], gain_ref[0], gain_ref[1], parts
        )
        for n in range(3):
            grad_s[n, cut] = grads[n]
    upward = dot(qw_ref[0], grad_s[0].astype(BF16), ((1,), (0,)))
    upward = upward + dot(qw_ref[1], grad_s[1].astype(BF16), ((1,), (0,)))
    upward = upward + dot(qw_ref[2], grad_s[2].astype(BF16), ((1,), (0,)))
    upward = upward.T
    grad = inverse * (
        upward
        - jnp.mean(upward, axis=1, keepdims=True)
        - low_s[...] * jnp.mean(upward * low_s[...], axis=1, keepdims=True)
    )
    grad = grad.astype(BF16)
    gr_ref[...] = grad.reshape(gr_ref.shape)
    att_s[...] = dot(ow_ref[...], grad, ((1,), (1,)))
    for z in range(count):
        for f, block in enumerate(pack(att_s[z * rows : (z + 1) * rows, :], parts)):
            up_ref[z * parts + f] = block.astype(BF16)


def middle(count, parts, att, res, cot, gains, out_weight, qkv_weight):
    width = out_weight.shape[0]
    vmem = pl.BlockSpec(memory_space=pltpu.VMEM)
    hbm = pl.BlockSpec(memory_space=pl.ANY)
    return pl.pallas_call(
        functools.partial(middle_kernel, count, parts),
        out_shape=[
            jax.ShapeDtypeStruct(res.shape, BF16),
            jax.ShapeDtypeStruct(att.shape, BF16),
        ],
        in_specs=[vmem, vmem, vmem, vmem, hbm, hbm],
        out_specs=[vmem, vmem],
        scratch_shapes=[
            pltpu.VMEM(out_weight.shape, BF16),
            pltpu.VMEM(qkv_weight.shape, BF16),
            pltpu.VMEM((width, LANES), F32),
            pltpu.VMEM((LANES, width), F32),
            pltpu.VMEM((width, LANES), F32),
            pltpu.VMEM((3, width, LANES), F32),
            pltpu.VMEM((3, width, LANES), F32),
            pltpu.SemaphoreType.DMA((4,)),
        ],
        compiler_params=PARAMS,
        name="middle",
    )(att, res, cot, gains, out_weight, qkv_weight)


def swap(array, axis, count, s):
    if s == 0:
        return array
    return lax.ppermute(array, axis, [(n, n ^ s) for n in range(count)])


def local(
    count,
    parts,
    residual,
    spatial_query,
    spatial_key,
    spatial_value,
    out_weight,
    qkv_weight,
    space_gains,
    time_gains,
    cotangent,
):
    tokens, width = residual.shape[1:]
    wide_space = jnp.broadcast_to(space_gains[:, :, None], space_gains.shape + (1,))
    wide_time = jnp.broadcast_to(time_gains[:, :, None], time_gains.shape + (1,))
    own = turn("seq", count, (spatial_query[0], spatial_key[0], spatial_value[0]))
    held = [swap(own[s], "seq", count, s) for s in range(count)]
    frames = (parts, tokens // parts, width)
    res = lax.all_to_all(residual.reshape(frames), "frm", 0, 0, tiled=True)
    cot = lax.all_to_all(cotangent.reshape(frames), "frm", 0, 0, tiled=True)
    sent = space_fwd("seq", parts, wide_space, held)
    att = lax.all_to_all(sent, ("seq", "frm"), 0, 0, tiled=True)
    grad, up = middle(count, parts, att, res, cot, wide_time, out_weight, qkv_weight)
    up = lax.all_to_all(up, ("seq", "frm"), 0, 0, tiled=True)
    grad = lax.all_to_all(grad, "frm", 0, 0, tiled=True)
    grads = space_bwd("seq", parts, wide_space, up, held)
    back = [swap(grads[s], "seq", count, s) for s in range(count)]
    outs = unturn("seq", back)
    return (grad.reshape(residual.shape),) + tuple(out[None] for out in outs)


def solution(mesh):
    tokens = P(("grp", "frm"), "seq", None)
    return jax.shard_map(
        functools.partial(local, mesh.shape["seq"], mesh.shape["frm"]),
        mesh=mesh,
        in_specs=(tokens, tokens, tokens, tokens, P(), P(), P(), P(), tokens),
        out_specs=(tokens, tokens, tokens, tokens),
        check_vma=False,
    )
```

time: 392 us -> 114 us (0.29)
  the two profiles are of different devices: /device:TPU:0 before, /device:TPU:8 now
where the time goes in v1:
time: 114 us; the launch traced here: 113 us
  waiting for transfers between devices  42.7 us (37%)
  Pallas kernels  26.7 us (23%)
  starting transfers between devices  23 us (20%)
  blocking collectives  14.8 us (13%)
  local copies, waits for them, and re-layouts  5.65 us (5%)
    ppermute x6, waiting for transfers between devices, swap(): return lax.ppermute(array, axis, [(n, n ^ s) for n in range(count)])  34.8 us
    all_to_all x1, blocking collectives, local(): up = lax.all_to_all(up, ('seq', 'frm'), 0, 0, tiled=True)  14.8 us
    pallas_call x1, Pallas kernels, middle(): pl.pallas_call(functools.partial(middle_kernel, count, parts), out_shape=...  11.7 us
    all_to_all x1, waiting for transfers between devices, local(): att = lax.all_to_all(sent, ('seq', 'frm'), 0, 0, tiled=True)  7.4 us
    ppermute x6, starting transfers between devices, swap(): return lax.ppermute(array, axis, [(n, n ^ s) for n in range(count)])  6.98 us
    pallas_call x1, Pallas kernels, space_bwd(): pl.pallas_call(functools.partial(space_bwd_kernel, axis, parts), out_shap...  6.46 us
    all_to_all x1, starting transfers between devices, local(): att = lax.all_to_all(sent, ('seq', 'frm'), 0, 0, tiled=True)  5.43 us
    pallas_call x1, Pallas kernels, space_fwd(): pl.pallas_call(functools.partial(space_fwd_kernel, axis, parts), out_shap...  3.82 us
  transfers between devices with their start and end apart: 10, of which 8 were waited for; matrix products, arithmetic and copies ran while one was open for 3% of the time, Pallas kernels for 11%

profile of v1, /device:TPU:8, one launch (start us, length us, event | category | flops | bytes accessed | tf_op | source)
XLA Modules:
  0.0 113.5 jit_solution(4958751296555425807)
XLA Ops:
  0.6 3.5 %all-to-all-start.1 = ((bf16[4,32,1152]{2,1,0:T(8,128)(2,1)}), bf16[4,32,1152]{2,1,0:T(8,128)(2,1)S(1)}, u32[]{:S(2)}, u32[]{:S(2)}) async-start(bf16[4,32,1152]{2,1,0:T(8,128)(2,1)} %bitcast.15), calls=%async_computation.1 | async-start | bytes 589824 | tf_op jit(solution)/shard_map/all_to_all | solution.py:364
  4.1 2.4 %turn.1 = (bf16[3,288,128]{2,1,0:T(8,128)(2,1)}, bf16[3,288,128]{2,1,0:T(8,128)(2,1)}, bf16[3,288,128]{2,1,0:T(8,128)(2,1)}, bf16[3,288,128]{2,1,0:T(8,128)(2,1)}) custom-call(bf16[128,1152]{1,0:T(8,128)(2,1)} %bitcast.12, bf16[128,1152]{1,0:T(8,128)(2,1)} %bitcast.13, bf16[128,1152]{1,0:T(8,128)(2,1)} %bitcast.14), custom_call_target="tpu_custom_call" | custom-call | tf_op jit(solution)/shard_map/turn/pallas_call | solution.py:91
  6.5 0.0 collective-permute-start
  6.5 3.0 %collective-permute-start.1 = (bf16[3,288,128]{2,1,0:T(8,128)(2,1)}, bf16[3,288,128]{2,1,0:T(8,128)(2,1)S(1)}, u32[]{:S(2)}, u32[]{:S(2)}) collective-permute-start(bf16[3,288,128]{2,1,0:T(8,128)(2,1)} %get-tuple-element.19), channel_id=1, source_target_pairs={{0,8},{4,12},{8,0},{12,4},{1,9},{5,13},{9,1},{13,5},{2,10},{6,14},... | collective-permute-start | bytes 663560 | tf_op jit(solution)/shard_map/ppermute | solution.py:342
  9.5 0.5 collective-permute-start.2
  10.0 0.5 all-to-all-done.1.res_ref
  10.5 3.5 %all-to-all-start.2 = ((bf16[4,32,1152]{2,1,0:T(8,128)(2,1)}), bf16[4,32,1152]{2,1,0:T(8,128)(2,1)S(1)}, u32[]{:S(2)}, u32[]{:S(2)}) async-start(bf16[4,32,1152]{2,1,0:T(8,128)(2,1)} %bitcast.16), calls=%async_computation.2 | async-start | bytes 589824 | tf_op jit(solution)/shard_map/all_to_all | solution.py:365
  13.9 1.4 %copy.13.gain_ref = f32[2,72,1]{2,1,0:T(8,128)} copy(f32[2,72,1]{1,0,2:T(2,128)} %bitcast.17) | data formatting | bytes 1152 | tf_op jit(solution)/shard_map/broadcast_in_dim | solution.py:359
  15.3 1.4 %collective-permute-done.refs_1_ = bf16[3,288,128]{2,1,0:T(8,128)(2,1)S(1)} collective-permute-done((bf16[3,288,128]{2,1,0:T(8,128)(2,1)}, bf16[3,288,128]{2,1,0:T(8,128)(2,1)S(1)}, u32[]{:S(2)}, u32[]{:S(2)}) %collective-permute-start) | collective-permute-done | bytes 221216 | tf_op jit(solution)/shard_map/ppermute | solution.py:342
  16.7 8.4 %collective-permute-done.1.refs_2_ = bf16[3,288,128]{2,1,0:T(8,128)(2,1)S(1)} collective-permute-done((bf16[3,288,128]{2,1,0:T(8,128)(2,1)}, bf16[3,288,128]{2,1,0:T(8,128)(2,1)S(1)}, u32[]{:S(2)}, u32[]{:S(2)}) %collective-permute-start.1) | collective-permute-done | bytes 221216 | tf_op jit(solution)/shard_map/ppermute | solution.py:342
  25.2 4.8 %collective-permute-done.2.refs_3_ = bf16[3,288,128]{2,1,0:T(8,128)(2,1)S(1)} collective-permute-done((bf16[3,288,128]{2,1,0:T(8,128)(2,1)}, bf16[3,288,128]{2,1,0:T(8,128)(2,1)S(1)}, u32[]{:S(2)}, u32[]{:S(2)}) %collective-permute-start.2) | collective-permute-done | bytes 221216 | tf_op jit(solution)/shard_map/ppermute | solution.py:342
  30.0 0.7 copy-done.5
  30.6 3.8 %space_fwd.1 = bf16[16,72,128]{2,1,0:T(8,128)(2,1)} custom-call(f32[2,72,1]{2,1,0:T(8,128)} %copy.13.gain_ref, bf16[3,288,128]{2,1,0:T(8,128)(2,1)} %get-tuple-element.17.refs_0_, bf16[3,288,128]{2,1,0:T(8,128)(2,1)} %copy-done.3, bf16[3,288,128]{2,1,0:T(8,128)(2,1)} %copy-done.4, bf16[3,288,128]{2,1,0:T(8,128)(2,1)} %copy-done.5), custom_call_target="tpu_custom_call" | custom-call | tf_op jit(solution)/shard_map/space_fwd/pallas_call | solution.py:153
  34.5 0.0 all-to-all-done.2.cot_ref
  34.5 5.4 %all-to-all-start = ((bf16[16,72,128]{2,1,0:T(8,128)(2,1)}), bf16[16,72,128]{2,1,0:T(8,128)(2,1)S(1)}, u32[]{:S(2)}, u32[]{:S(2)}) async-start(bf16[16,72,128]{2,1,0:T(8,128)(2,1)} %space_fwd.1), calls=%async_computation | async-start | bytes 589824 | tf_op jit(solution)/shard_map/all_to_all | solution.py:367
  39.9 1.4 %copy.14.gain_ref = f32[2,72,1]{2,1,0:T(8,128)} copy(f32[2,72,1]{1,0,2:T(2,128)} %bitcast.18) | data formatting | bytes 1152 | tf_op jit(solution)/shard_map/broadcast_in_dim | solution.py:360
  41.3 7.4 %all-to-all-done.att_ref = bf16[16,72,128]{2,1,0:T(8,128)(2,1)S(1)} async-done(((bf16[16,72,128]{2,1,0:T(8,128)(2,1)}), bf16[16,72,128]{2,1,0:T(8,128)(2,1)S(1)}, u32[]{:S(2)}, u32[]{:S(2)}) %all-to-all-start) | async-done | bytes 294944 | tf_op jit(solution)/shard_map/all_to_all | solution.py:367
  48.7 0.7 copy-done.2
  49.4 11.7 %middle.1 = (bf16[4,32,1152]{2,1,0:T(8,128)(2,1)}, bf16[16,72,128]{2,1,0:T(8,128)(2,1)}) custom-call(bf16[16,72,128]{2,1,0:T(8,128)(2,1)} %copy-done.2, bf16[4,32,1152]{2,1,0:T(8,128)(2,1)} %copy-done, bf16[4,32,1152]{2,1,0:T(8,128)(2,1)} %copy-done.1, f32[2,72,1]{2,1,0:T(8,128)} %copy.14.gain_ref, bf16[1152,1152]{1,0:T(8,128)(2,1)} %ow_hbm.1, ...), custom_call_target="tpu_custom_call" | custom-call | tf_op jit(solution)/shard_map/middle/pallas_call | solution.py:316
  61.1 14.8 %all_to_all.25.up_ref = bf16[16,72,128]{2,1,0:T(8,128)(2,1)} all-to-all(bf16[16,72,128]{2,1,0:T(8,128)(2,1)} %get-tuple-element.22), channel_id=1, replica_groups=mesh['grp'=2,'seq'=4,'frm'=4] {'seq','frm'}, dimensions={0} | all-to-all | bytes 589824 | tf_op jit(solution)/shard_map/all_to_all | solution.py:369
  75.8 3.6 %all-to-all-start.3 = ((bf16[4,32,1152]{2,1,0:T(8,128)(2,1)}), bf16[4,32,1152]{2,1,0:T(8,128)(2,1)S(1)}, u32[]{:S(2)}, u32[]{:S(2)}) async-start(bf16[4,32,1152]{2,1,0:T(8,128)(2,1)} %get-tuple-element.21), calls=%async_computation.3 | async-start | bytes 589824 | tf_op jit(solution)/shard_map/all_to_all | solution.py:370
  79.5 6.5 %space_bwd.1 = (bf16[3,288,128]{2,1,0:T(8,128)(2,1)}, bf16[3,288,128]{2,1,0:T(8,128)(2,1)}, bf16[3,288,128]{2,1,0:T(8,128)(2,1)}, bf16[3,288,128]{2,1,0:T(8,128)(2,1)}) custom-call(f32[2,72,1]{2,1,0:T(8,128)} %copy.13.gain_ref, bf16[16,72,128]{2,1,0:T(8,128)(2,1)} %all_to_all.25.up_ref, bf16[3,288,128]{2,1,0:T(8,128)(2,1)} %get-tuple-element.17.refs_0_, ...), custom_call_target="tpu_custom_call" | custom-call | tf_op jit(solution)/shard_map/space_bwd/pallas_call | solution.py:205
  85.9 1.9 %collective-permute-start.3 = (bf16[3,288,128]{2,1,0:T(8,128)(2,1)}, bf16[3,288,128]{2,1,0:T(8,128)(2,1)S(1)}, u32[]{:S(2)}, u32[]{:S(2)}) collective-permute-start(bf16[3,288,128]{2,1,0:T(8,128)(2,1)} %get-tuple-element.24), channel_id=1, source_target_pairs={{0,4},{4,0},{8,12},{12,8},{1,5},{5,1},{9,13},{13,9},{2,6},{6,2},{1... | collective-permute-start | bytes 663560 | tf_op jit(solution)/shard_map/ppermute | solution.py:342
  87.8 1.2 %collective-permute-start.4 = (bf16[3,288,128]{2,1,0:T(8,128)(2,1)}, bf16[3,288,128]{2,1,0:T(8,128)(2,1)S(1)}, u32[]{:S(2)}, u32[]{:S(2)}) collective-permute-start(bf16[3,288,128]{2,1,0:T(8,128)(2,1)} %get-tuple-element.25), channel_id=1, source_target_pairs={{0,8},{4,12},{8,0},{12,4},{1,9},{5,13},{9,1},{13,5},{2,10},{6,14},... | collective-permute-start | bytes 663560 | tf_op jit(solution)/shard_map/ppermute | solution.py:342
  89.0 0.4 collective-permute-start.5
  89.4 0.0 all-to-all-done.3
  89.4 8.1 %collective-permute-done.3.refs_1_ = bf16[3,288,128]{2,1,0:T(8,128)(2,1)S(1)} collective-permute-done((bf16[3,288,128]{2,1,0:T(8,128)(2,1)}, bf16[3,288,128]{2,1,0:T(8,128)(2,1)S(1)}, u32[]{:S(2)}, u32[]{:S(2)}) %collective-permute-start.3) | collective-permute-done | bytes 221216 | tf_op jit(solution)/shard_map/ppermute | solution.py:342
  97.5 7.2 %collective-permute-done.4.refs_2_ = bf16[3,288,128]{2,1,0:T(8,128)(2,1)S(1)} collective-permute-done((bf16[3,288,128]{2,1,0:T(8,128)(2,1)}, bf16[3,288,128]{2,1,0:T(8,128)(2,1)S(1)}, u32[]{:S(2)}, u32[]{:S(2)}) %collective-permute-start.4) | collective-permute-done | bytes 221216 | tf_op jit(solution)/shard_map/ppermute | solution.py:342
  104.7 5.0 %collective-permute-done.5.refs_3_ = bf16[3,288,128]{2,1,0:T(8,128)(2,1)S(1)} collective-permute-done((bf16[3,288,128]{2,1,0:T(8,128)(2,1)}, bf16[3,288,128]{2,1,0:T(8,128)(2,1)S(1)}, u32[]{:S(2)}, u32[]{:S(2)}) %collective-permute-start.5) | collective-permute-done | bytes 221216 | tf_op jit(solution)/shard_map/ppermute | solution.py:342
  109.7 0.7 copy-done.8
  110.3 2.4 %unturn.1 = (bf16[128,1152]{1,0:T(8,128)(2,1)}, bf16[128,1152]{1,0:T(8,128)(2,1)}, bf16[128,1152]{1,0:T(8,128)(2,1)}) custom-call(bf16[3,288,128]{2,1,0:T(8,128)(2,1)} %get-tuple-element.23.refs_0_, bf16[3,288,128]{2,1,0:T(8,128)(2,1)} %copy-done.6, bf16[3,288,128]{2,1,0:T(8,128)(2,1)} %copy-done.7, bf16[3,288,128]{2,1,0:T(8,128)(2,1)} %copy-done.8), custom_call_target="tpu_custom_call" | custom-call | tf_op jit(solution)/shard_map/unturn/pallas_call | solution.py:115
  112.8 0.7 copy.17
  (15 shorter events, 0.0 us)
Async XLA Ops:
  0.6 9.8 %all-to-all-start.1 = ((bf16[4,32,1152]{2,1,0:T(8,128)(2,1)}), bf16[4,32,1152]{2,1,0:T(8,128)(2,1)S(1)}, u32[]{:S(2)}, u32[]{:S(2)}) async-start(bf16[4,32,1152]{2,1,0:T(8,128)(2,1)} %bitcast.15), calls=%async_computation.1 | async-start | bytes 589824 | tf_op jit(solution)/shard_map/all_to_all | solution.py:364
  6.5 10.2 %collective-permute-start = (bf16[3,288,128]{2,1,0:T(8,128)(2,1)}, bf16[3,288,128]{2,1,0:T(8,128)(2,1)S(1)}, u32[]{:S(2)}, u32[]{:S(2)}) collective-permute-start(bf16[3,288,128]{2,1,0:T(8,128)(2,1)} %get-tuple-element.18), channel_id=1, source_target_pairs={{0,4},{4,0},{8,12},{12,8},{1,5},{5,1},{9,13},{13,9},{2,6},{6,2},{1... | collective-permute-start | bytes 663560 | tf_op jit(solution)/shard_map/ppermute | solution.py:342
  6.5 18.7 %collective-permute-start.1 = (bf16[3,288,128]{2,1,0:T(8,128)(2,1)}, bf16[3,288,128]{2,1,0:T(8,128)(2,1)S(1)}, u32[]{:S(2)}, u32[]{:S(2)}) collective-permute-start(bf16[3,288,128]{2,1,0:T(8,128)(2,1)} %get-tuple-element.19), channel_id=1, source_target_pairs={{0,8},{4,12},{8,0},{12,4},{1,9},{5,13},{9,1},{13,5},{2,10},{6,14},... | collective-permute-start | bytes 663560 | tf_op jit(solution)/shard_map/ppermute | solution.py:342
  9.5 20.4 %collective-permute-start.2 = (bf16[3,288,128]{2,1,0:T(8,128)(2,1)}, bf16[3,288,128]{2,1,0:T(8,128)(2,1)S(1)}, u32[]{:S(2)}, u32[]{:S(2)}) collective-permute-start(bf16[3,288,128]{2,1,0:T(8,128)(2,1)} %get-tuple-element.20), channel_id=1, source_target_pairs={{0,12},{4,8},{8,4},{12,0},{1,13},{5,9},{9,5},{13,1},{2,14},{6,10},... | collective-permute-start | bytes 663560 | tf_op jit(solution)/shard_map/ppermute | solution.py:342
  10.5 38.3 %copy-start = (bf16[4,32,1152]{2,1,0:T(8,128)(2,1)}, bf16[4,32,1152]{2,1,0:T(8,128)(2,1)S(1)}, u32[]{:S(2)}) copy-start(bf16[4,32,1152]{2,1,0:T(8,128)(2,1)S(1)} %all-to-all-done.1.res_ref) | copy-start | bytes 884740
  10.5 24.0 %all-to-all-start.2 = ((bf16[4,32,1152]{2,1,0:T(8,128)(2,1)}), bf16[4,32,1152]{2,1,0:T(8,128)(2,1)S(1)}, u32[]{:S(2)}, u32[]{:S(2)}) async-start(bf16[4,32,1152]{2,1,0:T(8,128)(2,1)} %bitcast.16), calls=%async_computation.2 | async-start | bytes 589824 | tf_op jit(solution)/shard_map/all_to_all | solution.py:365
  16.7 13.2 %copy-start.3 = (bf16[3,288,128]{2,1,0:T(8,128)(2,1)}, bf16[3,288,128]{2,1,0:T(8,128)(2,1)S(1)}, u32[]{:S(2)}) copy-start(bf16[3,288,128]{2,1,0:T(8,128)(2,1)S(1)} %collective-permute-done.refs_1_) | copy-start | bytes 663556
  25.2 4.8 %copy-start.4 = (bf16[3,288,128]{2,1,0:T(8,128)(2,1)}, bf16[3,288,128]{2,1,0:T(8,128)(2,1)S(1)}, u32[]{:S(2)}) copy-start(bf16[3,288,128]{2,1,0:T(8,128)(2,1)S(1)} %collective-permute-done.1.refs_2_) | copy-start | bytes 663556
  30.0 0.7 copy-start.5
  34.5 14.3 %copy-start.1 = (bf16[4,32,1152]{2,1,0:T(8,128)(2,1)}, bf16[4,32,1152]{2,1,0:T(8,128)(2,1)S(1)}, u32[]{:S(2)}) copy-start(bf16[4,32,1152]{2,1,0:T(8,128)(2,1)S(1)} %all-to-all-done.2.cot_ref) | copy-start | bytes 884740
  34.5 14.2 %all-to-all-start = ((bf16[16,72,128]{2,1,0:T(8,128)(2,1)}), bf16[16,72,128]{2,1,0:T(8,128)(2,1)S(1)}, u32[]{:S(2)}, u32[]{:S(2)}) async-start(bf16[16,72,128]{2,1,0:T(8,128)(2,1)} %space_fwd.1), calls=%async_computation | async-start | bytes 589824 | tf_op jit(solution)/shard_map/all_to_all | solution.py:367
  48.7 0.7 copy-start.2
  75.8 13.6 %all-to-all-start.3 = ((bf16[4,32,1152]{2,1,0:T(8,128)(2,1)}), bf16[4,32,1152]{2,1,0:T(8,128)(2,1)S(1)}, u32[]{:S(2)}, u32[]{:S(2)}) async-start(bf16[4,32,1152]{2,1,0:T(8,128)(2,1)} %get-tuple-element.21), calls=%async_computation.3 | async-start | bytes 589824 | tf_op jit(solution)/shard_map/all_to_all | solution.py:370
  85.9 11.6 %collective-permute-start.3 = (bf16[3,288,128]{2,1,0:T(8,128)(2,1)}, bf16[3,288,128]{2,1,0:T(8,128)(2,1)S(1)}, u32[]{:S(2)}, u32[]{:S(2)}) collective-permute-start(bf16[3,288,128]{2,1,0:T(8,128)(2,1)} %get-tuple-element.24), channel_id=1, source_target_pairs={{0,4},{4,0},{8,12},{12,8},{1,5},{5,1},{9,13},{13,9},{2,6},{6,2},{1... | collective-permute-start | bytes 663560 | tf_op jit(solution)/shard_map/ppermute | solution.py:342
  87.8 16.8 %collective-permute-start.4 = (bf16[3,288,128]{2,1,0:T(8,128)(2,1)}, bf16[3,288,128]{2,1,0:T(8,128)(2,1)S(1)}, u32[]{:S(2)}, u32[]{:S(2)}) collective-permute-start(bf16[3,288,128]{2,1,0:T(8,128)(2,1)} %get-tuple-element.25), channel_id=1, source_target_pairs={{0,8},{4,12},{8,0},{12,4},{1,9},{5,13},{9,1},{13,5},{2,10},{6,14},... | collective-permute-start | bytes 663560 | tf_op jit(solution)/shard_map/ppermute | solution.py:342
  89.0 20.6 %collective-permute-start.5 = (bf16[3,288,128]{2,1,0:T(8,128)(2,1)}, bf16[3,288,128]{2,1,0:T(8,128)(2,1)S(1)}, u32[]{:S(2)}, u32[]{:S(2)}) collective-permute-start(bf16[3,288,128]{2,1,0:T(8,128)(2,1)} %get-tuple-element.26), channel_id=1, source_target_pairs={{0,12},{4,8},{8,4},{12,0},{1,13},{5,9},{9,5},{13,1},{2,14},{6,10},... | collective-permute-start | bytes 663560 | tf_op jit(solution)/shard_map/ppermute | solution.py:342
  97.5 12.1 %copy-start.6 = (bf16[3,288,128]{2,1,0:T(8,128)(2,1)}, bf16[3,288,128]{2,1,0:T(8,128)(2,1)S(1)}, u32[]{:S(2)}) copy-start(bf16[3,288,128]{2,1,0:T(8,128)(2,1)S(1)} %collective-permute-done.3.refs_1_) | copy-start | bytes 663556
  104.7 5.0 %copy-start.7 = (bf16[3,288,128]{2,1,0:T(8,128)(2,1)}, bf16[3,288,128]{2,1,0:T(8,128)(2,1)S(1)}, u32[]{:S(2)}) copy-start(bf16[3,288,128]{2,1,0:T(8,128)(2,1)S(1)} %collective-permute-done.4.refs_2_) | copy-start | bytes 663556
  109.7 0.7 copy-start.8

commit v2 on v1

--- a/solution.py
+++ b/solution.py
@@ -15,6 +15,10 @@
 VMEM_LIMIT = 56 * 1024 * 1024
 
 PARAMS = pltpu.CompilerParams(vmem_limit_bytes=VMEM_LIMIT)
+
+
+def cost(micros):
+    return pl.CostEstimate(flops=int(micros * 1e9), bytes_accessed=0, transcendentals=0)
 
 
 def dot(left, right, dims):
@@ -49,6 +53,14 @@
     return results
 
 
+def column(row):
+    size = row.shape[1]
+    here = lax.broadcasted_iota(jnp.int32, (size, size), 0) == lax.broadcasted_iota(
+        jnp.int32, (size, size), 1
+    )
+    return jnp.sum(jnp.where(here, row, 0.0), axis=1, keepdims=True)
+
+
 def is_dense(rows, parts):
     return rows % (8 * parts) == 0
 
@@ -74,55 +86,68 @@
     return (rows, LANES // parts)
 
 
-def turn_kernel(axis, q_ref, k_ref, v_ref, *rest):
+def turn_kernel(axis, q_ref, k_ref, v_ref, res_ref, cot_ref, both_ref, *rest):
     out_refs, held = rest[:-1], rest[-1]
-    count = len(out_refs)
     rows = out_refs[0].shape[1]
+    parts, _, own, width = both_ref.shape
     me = lax.axis_index(axis)
+    for n, ref in enumerate((res_ref, cot_ref)):
+        both_ref[:, n] = ref[...].reshape(parts, own, width)
     for n, ref in enumerate((q_ref, k_ref, v_ref)):
-        held[n] = ref[...].astype(F32).T.astype(BF16)
-    for s in range(count):
+        held[n] = ref[...].T
+    for s, ref in enumerate(out_refs):
         start = pl.multiple_of((me ^ s) * rows, rows)
-        out_refs[s][...] = held[:, pl.ds(start, rows), :]
-
-
-def turn(axis, count, arrays):
+        ref[...] = held[:, pl.ds(start, rows), :]
+
+
+def turn(axis, count, parts, arrays, frames):
     tokens, width = arrays[0].shape
-    return pl.pallas_call(
+    outs = pl.pallas_call(
         functools.partial(turn_kernel, axis),
-        out_shape=[jax.ShapeDtypeStruct((3, width // count, tokens), BF16)] * count,
+        out_shape=[jax.ShapeDtypeStruct((parts, 2, tokens // parts, width), BF16)]
+        + [jax.ShapeDtypeStruct((3, width // count, tokens), BF16)] * count,
         scratch_shapes=[pltpu.VMEM((3, width, tokens), BF16)],
         compiler_params=PARAMS,
+        cost_estimate=cost(3),
         name="turn",
-    )(*arrays)
-
-
-def unturn_kernel(axis, *refs):
-    count = len(refs) - 4
-    in_refs, out_refs, held = refs[:count], refs[count:-1], refs[-1]
+    )(*arrays, *frames)
+    return outs[0], outs[1:]
+
+
+def unturn_kernel(axis, grad_ref, *refs):
+    in_refs, out_refs, grad_out, held = refs[:-5], refs[-5:-2], refs[-2], refs[-1]
     rows = in_refs[0].shape[1]
     me = lax.axis_index(axis)
-    for s in range(count):
+    grad_out[...] = grad_ref[...]
+    for s, ref in enumerate(in_refs):
         start = pl.multiple_of((me ^ s) * rows, rows)
-        held[:, pl.ds(start, rows), :] = in_refs[s][...]
+        held[:, pl.ds(start, rows), :] = ref[...]
     for n, ref in enumerate(out_refs):
-        ref[...] = held[n].astype(F32).T.astype(BF16)
-
-
-def unturn(axis, arrays):
-    count = len(arrays)
-    _, rows, tokens = arrays[0].shape
+        ref[...] = held[n].T
+
+
+def unturn(axis, grad, blocks):
+    count = len(blocks)
+    _, rows, tokens = blocks[0].shape
     return pl.pallas_call(
         functools.partial(unturn_kernel, axis),
-        out_shape=[jax.ShapeDtypeStruct((tokens, rows * count), BF16)] * 3,
+        out_shape=[jax.ShapeDtypeStruct((tokens, rows * count), BF16)] * 4,
         scratch_shapes=[pltpu.VMEM((3, rows * count, tokens), BF16)],
         compiler_params=PARAMS,
+        cost_estimate=cost(3),
         name="unturn",
-    )(*arrays)
+    )(grad, *blocks)
 
 
 def gather_part(refs, part):
     return jnp.concatenate([ref[part].astype(F32) for ref in refs], axis=1)
+
+
+def head_expons(query, key, query_gain, key_gain):
+    query_nrm = (head_norm(query)[0] * query_gain).astype(BF16)
+    key_nrm = (head_norm(key)[0] * key_gain).astype(BF16)
+    expons = jnp.exp(dot(key_nrm, query_nrm, ((0,), (0,))) * (HD ** (-0.5)))
+    return expons, 1.0 / jnp.sum(expons, axis=0, keepdims=True)
 
 
 def space_fwd_kernel(axis, parts, gain_ref, *refs):
@@ -131,16 +156,12 @@
     rows = in_refs[0].shape[1]
     me = lax.axis_index(axis)
     query, key, value = (gather_part(in_refs, n) for n in range(3))
-    factor = HD ** (-0.5)
+    query_gain, key_gain = (column(gain_ref[n : n + 1]) for n in range(2))
     for h in range(rows // HD):
         cut = slice(h * HD, (h + 1) * HD)
-        query_nrm = (head_norm(query[cut])[0] * gain_ref[0]).astype(BF16)
-        key_nrm = (head_norm(key[cut])[0] * gain_ref[1]).astype(BF16)
-        scores = dot(key_nrm, query_nrm, ((0,), (0,)))
-        expons = jnp.exp(scores * factor)
-        total = jnp.sum(expons, axis=0, keepdims=True)
+        expons, scale = head_expons(query[cut], key[cut], query_gain, key_gain)
         attended = dot(value[cut].astype(BF16), expons.astype(BF16), ((1,), (0,)))
-        held[cut, :] = attended * (1.0 / total)
+        held[cut, :] = attended * scale
     for s in range(count):
         blocks = pack(held[:, s * LANES : (s + 1) * LANES], parts)
         for f, block in enumerate(blocks):
@@ -155,11 +176,34 @@
         out_shape=jax.ShapeDtypeStruct((count * parts,) + block_shape(rows, parts), BF16),
         scratch_shapes=[pltpu.VMEM((rows, count * tokens), F32)],
         compiler_params=PARAMS,
+        cost_estimate=cost(4),
         name="space_fwd",
     )(gains, *arrays)
 
 
-def space_bwd_kernel(axis, parts, gain_ref, up_ref, *refs):
+def space_weights_kernel(gain_ref, *refs):
+    in_refs, weight_ref = refs[:-1], refs[-1]
+    query, key = (gather_part(in_refs, n) for n in range(2))
+    query_gain, key_gain = (column(gain_ref[n : n + 1]) for n in range(2))
+    for h in range(weight_ref.shape[0]):
+        cut = slice(h * HD, (h + 1) * HD)
+        expons, scale = head_expons(query[cut], key[cut], query_gain, key_gain)
+        weight_ref[h] = (expons * scale).astype(BF16)
+
+
+def space_weights(gains, arrays):
+    count = len(arrays)
+    _, rows, tokens = arrays[0].shape
+    return pl.pallas_call(
+        space_weights_kernel,
+        out_shape=jax.ShapeDtypeStruct((rows // HD, count * tokens, count * tokens), BF16),
+        compiler_params=PARAMS,
+        cost_estimate=cost(8),
+        name="space_weights",
+    )(gains, *arrays)
+
+
+def space_bwd_kernel(axis, parts, gain_ref, weight_ref, up_ref, *refs):
     count = (len(refs) - 1) // 2
     in_refs, out_refs, held = refs[:count], refs[count:-1], refs[-1]
     rows = in_refs[0].shape[1]
@@ -168,28 +212,28 @@
         blocks = [up_ref[(me ^ s) * parts + f].astype(F32) for f in range(parts)]
         held[:, s * LANES : (s + 1) * LANES] = unpack(blocks)
     query, key, value = (gather_part(in_refs, n) for n in range(3))
+    query_gain, key_gain = (column(gain_ref[n : n + 1]) for n in range(2))
     factor = HD ** (-0.5)
     grads = []
     for h in range(rows // HD):
         cut = slice(h * HD, (h + 1) * HD)
         query_hat, query_inv = head_norm(query[cut])
         key_hat, key_inv = head_norm(key[cut])
-        query_nrm = (query_hat * gain_ref[0]).astype(BF16)
-        key_nrm = (key_hat * gain_ref[1]).astype(BF16)
+        query_nrm = (query_hat * query_gain).astype(BF16)
+        key_nrm = (key_hat * key_gain).astype(BF16)
         up = held[cut, :].astype(BF16)
-        scores = dot(key_nrm, query_nrm, ((0,), (0,)))
-        expons = jnp.exp(scores * factor)
-        shares = expons * (1.0 / jnp.sum(expons, axis=0, keepdims=True))
+        weights = weight_ref[h]
+        shares = weights.astype(F32)
         share_grad = dot(value[cut].astype(BF16), up, ((0,), (0,)))
         centre = jnp.sum(shares * share_grad, axis=0, keepdims=True)
         score_grad = (shares * (share_grad - centre) * factor).astype(BF16)
         query_grad = dot(key_nrm, score_grad, ((1,), (0,)))
         key_grad = dot(query_nrm, score_grad, ((1,), (1,)))
-        value_grad = dot(up, shares.astype(BF16), ((1,), (1,)))
+        value_grad = dot(up, weights, ((1,), (1,)))
         grads.append(
             (
-                norm_back(query_grad, query_hat, query_inv, gain_ref[0]),
-                norm_back(key_grad, key_hat, key_inv, gain_ref[1]),
+                norm_back(query_grad, query_hat, query_inv, query_gain),
+                norm_back(key_grad, key_hat, key_inv, key_gain),
                 value_grad,
             )
         )
@@ -199,7 +243,7 @@
             out_refs[s][n] = whole[:, s * LANES : (s + 1) * LANES]
 
 
-def space_bwd(axis, parts, gains, up, arrays):
+def space_bwd(axis, parts, gains, weights, up, arrays):
     count = len(arrays)
     _, rows, tokens = arrays[0].shape
     return pl.pallas_call(
@@ -207,8 +251,9 @@
         out_shape=[jax.ShapeDtypeStruct((3, rows, tokens), BF16)] * count,
         scratch_shapes=[pltpu.VMEM((rows, count * tokens), F32)],
         compiler_params=PARAMS,
+        cost_estimate=cost(6),
         name="space_bwd",
-    )(gains, up, *arrays)
+    )(gains, weights, up, *arrays)
 
 
 def time_head(query_in, key_in, value, upward, query_gain, key_gain, parts):
@@ -244,8 +289,7 @@
     count,
     parts,
     att_ref,
-    res_ref,
-    cot_ref,
+    pair_ref,
     gain_ref,
     ow_hbm,
     qw_hbm,
@@ -271,10 +315,10 @@
             [att_ref[z * parts + f].astype(F32) for f in range(parts)]
         )
     attended = att_s[...].T.astype(BF16)
-    cot_s[...] = cot_ref[...].reshape(LANES, width).astype(F32).T
+    cot_s[...] = pair_ref[:, 1].reshape(LANES, width).astype(F32).T
     copies[0].wait()
     mixed = rounded(
-        res_ref[...].reshape(LANES, width).astype(F32) + dot(attended, ow_ref[...], ((1,), (0,)))
+        pair_ref[:, 0].reshape(LANES, width).astype(F32) + dot(attended, ow_ref[...], ((1,), (0,)))
     )
     centred = mixed - jnp.mean(mixed, axis=1, keepdims=True)
     inverse = lax.rsqrt(jnp.mean(centred * centred, axis=1, keepdims=True) + EPS)
@@ -285,10 +329,11 @@
         copies[1 + n].wait()
         product = rounded(dot(lowered, qw_ref[n], ((1,), (0,))))
         qkv_s[n] = product.T
+    query_gain, key_gain = (column(gain_ref[n : n + 1]) for n in range(2))
     for h in range(width // HD):
         cut = slice(h * HD, (h + 1) * HD)
         grads = time_head(
-            qkv_s[0, cut], qkv_s[1, cut], qkv_s[2, cut], cot_s[cut], gain_ref[0], gain_ref[1], parts
+            qkv_s[0, cut], qkv_s[1, cut], qkv_s[2, cut], cot_s[cut], query_gain, key_gain, parts
         )
         for n in range(3):
             grad_s[n, cut] = grads[n]
@@ -309,17 +354,17 @@
             up_ref[z * parts + f] = block.astype(BF16)
 
 
-def middle(count, parts, att, res, cot, gains, out_weight, qkv_weight):
+def middle(count, parts, att, pair, gains, out_weight, qkv_weight):
     width = out_weight.shape[0]
     vmem = pl.BlockSpec(memory_space=pltpu.VMEM)
     hbm = pl.BlockSpec(memory_space=pl.ANY)
     return pl.pallas_call(
         functools.partial(middle_kernel, count, parts),
         out_shape=[
-            jax.ShapeDtypeStruct(res.shape, BF16),
+            jax.ShapeDtypeStruct((pair.shape[0],) + pair.shape[2:], BF16),
             jax.ShapeDtypeStruct(att.shape, BF16),
         ],
-        in_specs=[vmem, vmem, vmem, vmem, hbm, hbm],
+        in_specs=[vmem, vmem, vmem, hbm, hbm],
         out_specs=[vmem, vmem],
         scratch_shapes=[
             pltpu.VMEM(out_weight.shape, BF16),
@@ -332,8 +377,9 @@
             pltpu.SemaphoreType.DMA((4,)),
         ],
         compiler_params=PARAMS,
+        cost_estimate=cost(10),
         name="middle",
-    )(att, res, cot, gains, out_weight, qkv_weight)
+    )(att, pair, gains, out_weight, qkv_weight)
 
 
 def swap(array, axis, count, s):
@@ -356,22 +402,30 @@
     cotangent,
 ):
     tokens, width = residual.shape[1:]
-    wide_space = jnp.broadcast_to(space_gains[:, :, None], space_gains.shape + (1,))
-    wide_time = jnp.broadcast_to(time_gains[:, :, None], time_gains.shape + (1,))
-    own = turn("seq", count, (spatial_query[0], spatial_key[0], spatial_value[0]))
+    both, own = turn(
+        "seq",
+        count,
+        parts,
+        (spatial_query[0], spatial_key[0], spatial_value[0]),
+        (residual[0], cotangent[0]),
+    )
     held = [swap(own[s], "seq", count, s) for s in range(count)]
-    frames = (parts, tokens // parts, width)
-    res = lax.all_to_all(residual.reshape(frames), "frm", 0, 0, tiled=True)
-    cot = lax.all_to_all(cotangent.reshape(frames), "frm", 0, 0, tiled=True)
-    sent = space_fwd("seq", parts, wide_space, held)
+    both = lax.all_to_all(both, "frm", 0, 0, tiled=True)
+    sent = space_fwd("seq", parts, space_gains, held)
     att = lax.all_to_all(sent, ("seq", "frm"), 0, 0, tiled=True)
-    grad, up = middle(count, parts, att, res, cot, wide_time, out_weight, qkv_weight)
+    late = lax.optimization_barrier((sent, *held))[1:]
+    weights = space_weights(space_gains, late)
+    att, both, weights = lax.optimization_barrier((att, both, weights))
+    grad, up = middle(count, parts, att, both, time_gains, out_weight, qkv_weight)
     up = lax.all_to_all(up, ("seq", "frm"), 0, 0, tiled=True)
+    grads = space_bwd("seq", parts, space_gains, weights, up, held)
+    back = [swap(grads[s], "seq", count, s) for s in range(count)]
+    grad, _ = lax.optimization_barrier((grad, back[1]))
     grad = lax.all_to_all(grad, "frm", 0, 0, tiled=True)
-    grads = space_bwd("seq", parts, wide_space, up, held)
-    back = [swap(grads[s], "seq", count, s) for s in range(count)]
-    outs = unturn("seq", back)
-    return (grad.reshape(residual.shape),) + tuple(out[None] for out in outs)
+    grad_query, grad_key, grad_value, grad = unturn(
+        "seq", grad.reshape((tokens, width)), back
+    )
+    return (grad[None], grad_query[None], grad_key[None], grad_value[None])
 
 
 def solution(mesh):

time: 114 us -> 106 us (0.930)
  waiting for transfers between devices: 42.7 us -> 37.3 us
  Pallas kernels: 26.7 us -> 31.1 us
  starting transfers between devices: 23 us -> 19.2 us
  local copies, waits for them, and re-layouts: 5.65 us -> 2.2 us
    pallas_call x0 -> x1, Pallas kernels: none -> 4.11 us  [space_weights(): pl.pallas_call(space_weights_kernel, out_shape=jax.ShapeDtypeStruct((rows...]
    all_to_all x2 -> x1, starting transfers between devices: 6.91 us -> 3.48 us  [local(): both = lax.all_to_all(both, 'frm', 0, 0, tiled=True)]
    broadcast_in_dim x2 -> x0, local copies, waits for them, and re-layouts: 2.84 us -> none  [the longest x1 1.42 us: local(): space_gains[:, :, None]]
    all_to_all x1, waiting for transfers between devices: 7.4 us -> 4.7 us  [local(): att = lax.all_to_all(sent, ('seq', 'frm'), 0, 0, tiled=True)]
    ppermute x6, waiting for transfers between devices: 34.8 us -> 32.6 us  [swap(): return lax.ppermute(array, axis, [(n, n ^ s) for n in range(count)])]
    unnamed x19 -> x18, local copies, waits for them, and re-layouts: 2.81 us -> 2.2 us
  transfers between devices with their start and end apart: 10 -> 9, of which waited for: 8 -> 7; matrix products, arithmetic and copies ran while one was open for 3% -> 0% of each run, Pallas kernels for 11% -> 8%
where the time goes in v2:
time: 106 us; the launch traced here: 105 us
  waiting for transfers between devices  37.3 us (35%)
  Pallas kernels  31.1 us (29%)
  starting transfers between devices  19.2 us (18%)
  blocking collectives  14.7 us (14%)
  local copies, waits for them, and re-layouts  2.2 us (2%)
    ppermute x6, waiting for transfers between devices, swap(): return lax.ppermute(array, axis, [(n, n ^ s) for n in range(count)])  32.6 us
    all_to_all x1, blocking collectives, local(): up = lax.all_to_all(up, ('seq', 'frm'), 0, 0, tiled=True)  14.7 us
    pallas_call x1, Pallas kernels, middle(): pl.pallas_call(functools.partial(middle_kernel, count, parts), out_shape=...  11.6 us
    ppermute x6, starting transfers between devices, swap(): return lax.ppermute(array, axis, [(n, n ^ s) for n in range(count)])  6.98 us
    pallas_call x1, Pallas kernels, space_bwd(): pl.pallas_call(functools.partial(space_bwd_kernel, axis, parts), out_shap...  6.29 us
    all_to_all x1, starting transfers between devices, local(): att = lax.all_to_all(sent, ('seq', 'frm'), 0, 0, tiled=True)  5.29 us
    all_to_all x1, waiting for transfers between devices, local(): att = lax.all_to_all(sent, ('seq', 'frm'), 0, 0, tiled=True)  4.7 us
    pallas_call x1, Pallas kernels, space_weights(): pl.pallas_call(space_weights_kernel, out_shape=jax.ShapeDtypeStruct((rows...  4.11 us
  transfers between devices with their start and end apart: 9, of which 7 were waited for; matrix products, arithmetic and copies ran while one was open for 0% of the time, Pallas kernels for 8%

profile of v2, /device:TPU:8, one launch (start us, length us, event | category | flops | bytes accessed | tf_op | source)
XLA Modules:
  0.0 105.2 jit_solution(1610347307918508078)
XLA Ops:
  0.6 2.8 %turn.1 = (bf16[4,2,32,1152]{3,2,1,0:T(8,128)(2,1)}, bf16[3,288,128]{2,1,0:T(8,128)(2,1)}, bf16[3,288,128]{2,1,0:T(8,128)(2,1)}, bf16[3,288,128]{2,1,0:T(8,128)(2,1)}, bf16[3,288,128]{2,1,0:T(8,128)(2,1)}) custom-call(bf16[128,1152]{1,0:T(8,128)(2,1)} %bitcast.11, bf16[128,1152]{1,0:T(8,128)(2,1)} %bitcast.12, bf16[128,1152]{1,0:T(8,128)(2,1)} %bitcast.13, ...), custom_call_target="tpu_custom_call" | custom-call | flops 3000000000 | tf_op jit(solution)/shard_map/turn/pallas_call | solution.py:105
  3.4 0.0 collective-permute-start
  3.4 3.0 %collective-permute-start.1 = (bf16[3,288,128]{2,1,0:T(8,128)(2,1)}, bf16[3,288,128]{2,1,0:T(8,128)(2,1)S(1)}, u32[]{:S(2)}, u32[]{:S(2)}) collective-permute-start(bf16[3,288,128]{2,1,0:T(8,128)(2,1)} %get-tuple-element.29), channel_id=1, source_target_pairs={{0,8},{4,12},{8,0},{12,4},{1,9},{5,13},{9,1},{13,5},{2,10},{6,14},... | collective-permute-start | bytes 663560 | tf_op jit(solution)/shard_map/ppermute | solution.py:388
  6.4 0.5 collective-permute-start.2
  6.9 3.5 %all-to-all-start.1 = ((bf16[4,2,32,1152]{3,2,1,0:T(8,128)(2,1)}), bf16[4,2,32,1152]{3,2,1,0:T(8,128)(2,1)S(1)}, u32[]{:S(2)}, u32[]{:S(2)}) async-start(bf16[4,2,32,1152]{3,2,1,0:T(8,128)(2,1)} %get-tuple-element.31), calls=%async_computation.1 | async-start | bytes 1179648 | tf_op jit(solution)/shard_map/all_to_all | solution.py:413
  10.4 2.3 %collective-permute-done.refs_1_ = bf16[3,288,128]{2,1,0:T(8,128)(2,1)S(1)} collective-permute-done((bf16[3,288,128]{2,1,0:T(8,128)(2,1)}, bf16[3,288,128]{2,1,0:T(8,128)(2,1)S(1)}, u32[]{:S(2)}, u32[]{:S(2)}) %collective-permute-start) | collective-permute-done | bytes 221216 | tf_op jit(solution)/shard_map/ppermute | solution.py:388
  12.7 9.4 %collective-permute-done.1.refs_2_ = bf16[3,288,128]{2,1,0:T(8,128)(2,1)S(1)} collective-permute-done((bf16[3,288,128]{2,1,0:T(8,128)(2,1)}, bf16[3,288,128]{2,1,0:T(8,128)(2,1)S(1)}, u32[]{:S(2)}, u32[]{:S(2)}) %collective-permute-start.1) | collective-permute-done | bytes 221216 | tf_op jit(solution)/shard_map/ppermute | solution.py:388
  22.1 4.1 %collective-permute-done.2.refs_3_ = bf16[3,288,128]{2,1,0:T(8,128)(2,1)S(1)} collective-permute-done((bf16[3,288,128]{2,1,0:T(8,128)(2,1)}, bf16[3,288,128]{2,1,0:T(8,128)(2,1)S(1)}, u32[]{:S(2)}, u32[]{:S(2)}) %collective-permute-start.2) | collective-permute-done | bytes 221216 | tf_op jit(solution)/shard_map/ppermute | solution.py:388
  26.2 0.0 copy-done.3
  26.2 0.0 copy-done.4
  26.2 0.7 copy-done.5
  26.9 3.8 %space_fwd.1 = bf16[16,72,128]{2,1,0:T(8,128)(2,1)} custom-call(f32[2,72]{1,0:T(2,128)} %gain_ref.7, bf16[3,288,128]{2,1,0:T(8,128)(2,1)} %get-tuple-element.32.refs_0_, bf16[3,288,128]{2,1,0:T(8,128)(2,1)} %copy-done.3, bf16[3,288,128]{2,1,0:T(8,128)(2,1)} %copy-done.4, bf16[3,288,128]{2,1,0:T(8,128)(2,1)} %copy-done.5), custom_call_target="tpu_custom_call" | custom-call | flops 4000000000 | tf_op jit(solution)/shard_map/space_fwd/pallas_call | solution.py:174
  30.7 0.0 all-to-all-done.1.pair_ref
  30.7 5.3 %all-to-all-start = ((bf16[16,72,128]{2,1,0:T(8,128)(2,1)}), bf16[16,72,128]{2,1,0:T(8,128)(2,1)S(1)}, u32[]{:S(2)}, u32[]{:S(2)}) async-start(bf16[16,72,128]{2,1,0:T(8,128)(2,1)} %space_fwd.1), calls=%async_computation | async-start | bytes 589824 | tf_op jit(solution)/shard_map/all_to_all | solution.py:415
  36.0 4.1 %space_weights.1.weight_ref = bf16[4,512,512]{2,1,0:T(8,128)(2,1)} custom-call(f32[2,72]{1,0:T(2,128)} %gain_ref.7, bf16[3,288,128]{2,1,0:T(8,128)(2,1)} %get-tuple-element.32.refs_0_, bf16[3,288,128]{2,1,0:T(8,128)(2,1)} %copy-done.3, bf16[3,288,128]{2,1,0:T(8,128)(2,1)} %copy-done.4, bf16[3,288,128]{2,1,0:T(8,128)(2,1)} %copy-done.5), custom_call_target="tpu_custom_call" | custom-call | flops 8000000000 | tf_op jit(solution)/shard_map/space_weights/pallas_call | solution.py:197
  40.1 4.7 %all-to-all-done.att_ref = bf16[16,72,128]{2,1,0:T(8,128)(2,1)S(1)} async-done(((bf16[16,72,128]{2,1,0:T(8,128)(2,1)}), bf16[16,72,128]{2,1,0:T(8,128)(2,1)S(1)}, u32[]{:S(2)}, u32[]{:S(2)}) %all-to-all-start) | async-done | bytes 294944 | tf_op jit(solution)/shard_map/all_to_all | solution.py:415
  44.8 0.7 copy-done.2
  45.5 11.6 %middle.1 = (bf16[4,32,1152]{2,1,0:T(8,128)(2,1)}, bf16[16,72,128]{2,1,0:T(8,128)(2,1)}) custom-call(bf16[16,72,128]{2,1,0:T(8,128)(2,1)} %copy-done.2, bf16[4,2,32,1152]{3,2,1,0:T(8,128)(2,1)} %copy-done, f32[2,72]{1,0:T(2,128)} %gain_ref.6, bf16[1152,1152]{1,0:T(8,128)(2,1)} %ow_hbm.1, bf16[3,1152,1152]{2,1,0:T(8,128)(2,1)} %qw_hbm.1), custom_call_target="tpu_custom_call" | custom-call | flops 10000000000 | tf_op jit(solution)/shard_map/middle/pallas_call | solution.py:361
  57.1 14.7 %all_to_all.20.up_ref = bf16[16,72,128]{2,1,0:T(8,128)(2,1)} all-to-all(bf16[16,72,128]{2,1,0:T(8,128)(2,1)} %get-tuple-element.40), channel_id=1, replica_groups=mesh['grp'=2,'seq'=4,'frm'=4] {'seq','frm'}, dimensions={0} | all-to-all | bytes 589824 | tf_op jit(solution)/shard_map/all_to_all | solution.py:420
  71.9 6.3 %space_bwd.1 = (bf16[3,288,128]{2,1,0:T(8,128)(2,1)}, bf16[3,288,128]{2,1,0:T(8,128)(2,1)}, bf16[3,288,128]{2,1,0:T(8,128)(2,1)}, bf16[3,288,128]{2,1,0:T(8,128)(2,1)}) custom-call(f32[2,72]{1,0:T(2,128)} %gain_ref.7, bf16[4,512,512]{2,1,0:T(8,128)(2,1)} %space_weights.1.weight_ref, bf16[16,72,128]{2,1,0:T(8,128)(2,1)} %all_to_all.20.up_ref, ...), custom_call_target="tpu_custom_call" | custom-call | flops 6000000000 | tf_op jit(solution)/shard_map/space_bwd/pallas_call | solution.py:249
  78.2 1.9 %collective-permute-start.3 = (bf16[3,288,128]{2,1,0:T(8,128)(2,1)}, bf16[3,288,128]{2,1,0:T(8,128)(2,1)S(1)}, u32[]{:S(2)}, u32[]{:S(2)}) collective-permute-start(bf16[3,288,128]{2,1,0:T(8,128)(2,1)} %get-tuple-element.41), channel_id=1, source_target_pairs={{0,4},{4,0},{8,12},{12,8},{1,5},{5,1},{9,13},{13,9},{2,6},{6,2},{1... | collective-permute-start | bytes 663560 | tf_op jit(solution)/shard_map/ppermute | solution.py:388
  80.0 1.2 %collective-permute-start.4 = (bf16[3,288,128]{2,1,0:T(8,128)(2,1)}, bf16[3,288,128]{2,1,0:T(8,128)(2,1)S(1)}, u32[]{:S(2)}, u32[]{:S(2)}) collective-permute-start(bf16[3,288,128]{2,1,0:T(8,128)(2,1)} %get-tuple-element.44), channel_id=1, source_target_pairs={{0,8},{4,12},{8,0},{12,4},{1,9},{5,13},{9,1},{13,5},{2,10},{6,14},... | collective-permute-start | bytes 663560 | tf_op jit(solution)/shard_map/ppermute | solution.py:388
  81.2 0.4 collective-permute-start.5
  81.7 6.9 %collective-permute-done.3.refs_1_ = bf16[3,288,128]{2,1,0:T(8,128)(2,1)S(1)} collective-permute-done((bf16[3,288,128]{2,1,0:T(8,128)(2,1)}, bf16[3,288,128]{2,1,0:T(8,128)(2,1)S(1)}, u32[]{:S(2)}, u32[]{:S(2)}) %collective-permute-start.3) | collective-permute-done | bytes 221216 | tf_op jit(solution)/shard_map/ppermute | solution.py:388
  88.6 3.5 %all-to-all-start.3 = ((bf16[4,32,1152]{2,1,0:T(8,128)(2,1)}), bf16[4,32,1152]{2,1,0:T(8,128)(2,1)S(1)}, u32[]{:S(2)}, u32[]{:S(2)}) async-start(bf16[4,32,1152]{2,1,0:T(8,128)(2,1)} %get-tuple-element.42), calls=%async_computation.3 | async-start | bytes 589824 | tf_op jit(solution)/shard_map/all_to_all | solution.py:424
  92.0 4.9 %collective-permute-done.4.refs_2_ = bf16[3,288,128]{2,1,0:T(8,128)(2,1)S(1)} collective-permute-done((bf16[3,288,128]{2,1,0:T(8,128)(2,1)}, bf16[3,288,128]{2,1,0:T(8,128)(2,1)S(1)}, u32[]{:S(2)}, u32[]{:S(2)}) %collective-permute-start.4) | collective-permute-done | bytes 221216 | tf_op jit(solution)/shard_map/ppermute | solution.py:388
  96.9 5.0 %collective-permute-done.5.refs_3_ = bf16[3,288,128]{2,1,0:T(8,128)(2,1)S(1)} collective-permute-done((bf16[3,288,128]{2,1,0:T(8,128)(2,1)}, bf16[3,288,128]{2,1,0:T(8,128)(2,1)S(1)}, u32[]{:S(2)}, u32[]{:S(2)}) %collective-permute-start.5) | collective-permute-done | bytes 221216 | tf_op jit(solution)/shard_map/ppermute | solution.py:388
  101.9 0.0 all-to-all-done.3
  101.9 0.0 copy-done.7
  101.9 0.7 copy-done.8
  102.6 0.1 copy-done.1
  102.7 2.5 %unturn.1 = (bf16[128,1152]{1,0:T(8,128)(2,1)}, bf16[128,1152]{1,0:T(8,128)(2,1)}, bf16[128,1152]{1,0:T(8,128)(2,1)}, bf16[128,1152]{1,0:T(8,128)(2,1)}) custom-call(bf16[128,1152]{1,0:T(8,128)(2,1)} %bitcast.10, bf16[3,288,128]{2,1,0:T(8,128)(2,1)} %get-tuple-element.43.refs_0_, bf16[3,288,128]{2,1,0:T(8,128)(2,1)} %copy-done.6, ...), custom_call_target="tpu_custom_call" | custom-call | flops 3000000000 | tf_op jit(solution)/shard_map/unturn/pallas_call | solution.py:132
  (11 shorter events, 0.0 us)
Async XLA Ops:
  3.4 9.3 %collective-permute-start = (bf16[3,288,128]{2,1,0:T(8,128)(2,1)}, bf16[3,288,128]{2,1,0:T(8,128)(2,1)S(1)}, u32[]{:S(2)}, u32[]{:S(2)}) collective-permute-start(bf16[3,288,128]{2,1,0:T(8,128)(2,1)} %get-tuple-element.28), channel_id=1, source_target_pairs={{0,4},{4,0},{8,12},{12,8},{1,5},{5,1},{9,13},{13,9},{2,6},{6,2},{1... | collective-permute-start | bytes 663560 | tf_op jit(solution)/shard_map/ppermute | solution.py:388
  3.4 18.7 %collective-permute-start.1 = (bf16[3,288,128]{2,1,0:T(8,128)(2,1)}, bf16[3,288,128]{2,1,0:T(8,128)(2,1)S(1)}, u32[]{:S(2)}, u32[]{:S(2)}) collective-permute-start(bf16[3,288,128]{2,1,0:T(8,128)(2,1)} %get-tuple-element.29), channel_id=1, source_target_pairs={{0,8},{4,12},{8,0},{12,4},{1,9},{5,13},{9,1},{13,5},{2,10},{6,14},... | collective-permute-start | bytes 663560 | tf_op jit(solution)/shard_map/ppermute | solution.py:388
  6.4 19.8 %collective-permute-start.2 = (bf16[3,288,128]{2,1,0:T(8,128)(2,1)}, bf16[3,288,128]{2,1,0:T(8,128)(2,1)S(1)}, u32[]{:S(2)}, u32[]{:S(2)}) collective-permute-start(bf16[3,288,128]{2,1,0:T(8,128)(2,1)} %get-tuple-element.30), channel_id=1, source_target_pairs={{0,12},{4,8},{8,4},{12,0},{1,13},{5,9},{9,5},{13,1},{2,14},{6,10},... | collective-permute-start | bytes 663560 | tf_op jit(solution)/shard_map/ppermute | solution.py:388
  6.9 23.8 %all-to-all-start.1 = ((bf16[4,2,32,1152]{3,2,1,0:T(8,128)(2,1)}), bf16[4,2,32,1152]{3,2,1,0:T(8,128)(2,1)S(1)}, u32[]{:S(2)}, u32[]{:S(2)}) async-start(bf16[4,2,32,1152]{3,2,1,0:T(8,128)(2,1)} %get-tuple-element.31), calls=%async_computation.1 | async-start | bytes 1179648 | tf_op jit(solution)/shard_map/all_to_all | solution.py:413
  12.7 13.5 %copy-start.3 = (bf16[3,288,128]{2,1,0:T(8,128)(2,1)}, bf16[3,288,128]{2,1,0:T(8,128)(2,1)S(1)}, u32[]{:S(2)}) copy-start(bf16[3,288,128]{2,1,0:T(8,128)(2,1)S(1)} %collective-permute-done.refs_1_) | copy-start | bytes 663556
  22.1 4.1 %copy-start.4 = (bf16[3,288,128]{2,1,0:T(8,128)(2,1)}, bf16[3,288,128]{2,1,0:T(8,128)(2,1)S(1)}, u32[]{:S(2)}) copy-start(bf16[3,288,128]{2,1,0:T(8,128)(2,1)S(1)} %collective-permute-done.1.refs_2_) | copy-start | bytes 663556
  26.2 0.7 copy-start.5
  30.7 9.4 %copy-start = (bf16[4,2,32,1152]{3,2,1,0:T(8,128)(2,1)}, bf16[4,2,32,1152]{3,2,1,0:T(8,128)(2,1)S(1)}, u32[]{:S(2)}) copy-start(bf16[4,2,32,1152]{3,2,1,0:T(8,128)(2,1)S(1)} %all-to-all-done.1.pair_ref) | copy-start | bytes 1769476
  30.7 14.1 %all-to-all-start = ((bf16[16,72,128]{2,1,0:T(8,128)(2,1)}), bf16[16,72,128]{2,1,0:T(8,128)(2,1)S(1)}, u32[]{:S(2)}, u32[]{:S(2)}) async-start(bf16[16,72,128]{2,1,0:T(8,128)(2,1)} %space_fwd.1), calls=%async_computation | async-start | bytes 589824 | tf_op jit(solution)/shard_map/all_to_all | solution.py:415
  44.8 0.7 copy-start.2
  78.2 10.4 %collective-permute-start.3 = (bf16[3,288,128]{2,1,0:T(8,128)(2,1)}, bf16[3,288,128]{2,1,0:T(8,128)(2,1)S(1)}, u32[]{:S(2)}, u32[]{:S(2)}) collective-permute-start(bf16[3,288,128]{2,1,0:T(8,128)(2,1)} %get-tuple-element.41), channel_id=1, source_target_pairs={{0,4},{4,0},{8,12},{12,8},{1,5},{5,1},{9,13},{13,9},{2,6},{6,2},{1... | collective-permute-start | bytes 663560 | tf_op jit(solution)/shard_map/ppermute | solution.py:388
  80.0 16.9 %collective-permute-start.4 = (bf16[3,288,128]{2,1,0:T(8,128)(2,1)}, bf16[3,288,128]{2,1,0:T(8,128)(2,1)S(1)}, u32[]{:S(2)}, u32[]{:S(2)}) collective-permute-start(bf16[3,288,128]{2,1,0:T(8,128)(2,1)} %get-tuple-element.44), channel_id=1, source_target_pairs={{0,8},{4,12},{8,0},{12,4},{1,9},{5,13},{9,1},{13,5},{2,10},{6,14},... | collective-permute-start | bytes 663560 | tf_op jit(solution)/shard_map/ppermute | solution.py:388
  81.2 20.6 %collective-permute-start.5 = (bf16[3,288,128]{2,1,0:T(8,128)(2,1)}, bf16[3,288,128]{2,1,0:T(8,128)(2,1)S(1)}, u32[]{:S(2)}, u32[]{:S(2)}) collective-permute-start(bf16[3,288,128]{2,1,0:T(8,128)(2,1)} %get-tuple-element.45), channel_id=1, source_target_pairs={{0,12},{4,8},{8,4},{12,0},{1,13},{5,9},{9,5},{13,1},{2,14},{6,10},... | collective-permute-start | bytes 663560 | tf_op jit(solution)/shard_map/ppermute | solution.py:388
  88.6 13.3 %copy-start.6 = (bf16[3,288,128]{2,1,0:T(8,128)(2,1)}, bf16[3,288,128]{2,1,0:T(8,128)(2,1)S(1)}, u32[]{:S(2)}) copy-start(bf16[3,288,128]{2,1,0:T(8,128)(2,1)S(1)} %collective-permute-done.3.refs_1_) | copy-start | bytes 663556
  88.6 13.3 %all-to-all-start.3 = ((bf16[4,32,1152]{2,1,0:T(8,128)(2,1)}), bf16[4,32,1152]{2,1,0:T(8,128)(2,1)S(1)}, u32[]{:S(2)}, u32[]{:S(2)}) async-start(bf16[4,32,1152]{2,1,0:T(8,128)(2,1)} %get-tuple-element.42), calls=%async_computation.3 | async-start | bytes 589824 | tf_op jit(solution)/shard_map/all_to_all | solution.py:424
  96.9 5.0 %copy-start.7 = (bf16[3,288,128]{2,1,0:T(8,128)(2,1)}, bf16[3,288,128]{2,1,0:T(8,128)(2,1)S(1)}, u32[]{:S(2)}) copy-start(bf16[3,288,128]{2,1,0:T(8,128)(2,1)S(1)} %collective-permute-done.4.refs_2_) | copy-start | bytes 663556
  101.9 0.7 copy-start.8
  101.9 0.8 copy-start.1

commit v3 on v2

--- a/solution.py
+++ b/solution.py
@@ -12,9 +12,13 @@
 F32 = jnp.float32
 BF16 = jnp.bfloat16
 LANES = 128
-VMEM_LIMIT = 56 * 1024 * 1024
+VMEM_LIMIT = 40 * 1024 * 1024
 
 PARAMS = pltpu.CompilerParams(vmem_limit_bytes=VMEM_LIMIT)
+
+
+def in_hbm(array):
+    return pltpu.with_memory_space_constraint(array, pltpu.HBM)
 
 
 def cost(micros):
@@ -86,15 +90,21 @@
     return (rows, LANES // parts)
 
 
-def turn_kernel(axis, q_ref, k_ref, v_ref, res_ref, cot_ref, both_ref, *rest):
-    out_refs, held = rest[:-1], rest[-1]
+def turn_kernel(axis, *refs):
+    in_refs, both_ref, out_refs = refs[:5], refs[5], refs[6:-3]
+    landed, held, sems = refs[-3:]
     rows = out_refs[0].shape[1]
     parts, _, own, width = both_ref.shape
     me = lax.axis_index(axis)
-    for n, ref in enumerate((res_ref, cot_ref)):
-        both_ref[:, n] = ref[...].reshape(parts, own, width)
-    for n, ref in enumerate((q_ref, k_ref, v_ref)):
-        held[n] = ref[...].T
+    copies = [pltpu.make_async_copy(ref, landed.at[n], sems.at[n]) for n, ref in enumerate(in_refs)]
+    for copy in copies:
+        copy.start()
+    for n in range(3):
+        copies[n].wait()
+        held[n] = landed[n].T
+    for n in range(2):
+        copies[3 + n].wait()
+        both_ref[:, n] = landed[3 + n].reshape(parts, own, width)
     for s, ref in enumerate(out_refs):
         start = pl.multiple_of((me ^ s) * rows, rows)
         ref[...] = held[:, pl.ds(start, rows), :]
@@ -106,11 +116,16 @@
         functools.partial(turn_kernel, axis),
         out_shape=[jax.ShapeDtypeStruct((parts, 2, tokens // parts, width), BF16)]
         + [jax.ShapeDtypeStruct((3, width // count, tokens), BF16)] * count,
-        scratch_shapes=[pltpu.VMEM((3, width, tokens), BF16)],
+        in_specs=[pl.BlockSpec(memory_space=pltpu.HBM)] * 5,
+        scratch_shapes=[
+            pltpu.VMEM((5, tokens, width), BF16),
+            pltpu.VMEM((3, width, tokens), BF16),
+            pltpu.SemaphoreType.DMA((5,)),
+        ],
         compiler_params=PARAMS,
         cost_estimate=cost(3),
         name="turn",
-    )(*arrays, *frames)
+    )(*(in_hbm(array) for array in (*arrays, *frames)))
     return outs[0], outs[1:]
 
 
@@ -357,14 +372,13 @@
 def middle(count, parts, att, pair, gains, out_weight, qkv_weight):
     width = out_weight.shape[0]
     vmem = pl.BlockSpec(memory_space=pltpu.VMEM)
-    hbm = pl.BlockSpec(memory_space=pl.ANY)
     return pl.pallas_call(
         functools.partial(middle_kernel, count, parts),
         out_shape=[
             jax.ShapeDtypeStruct((pair.shape[0],) + pair.shape[2:], BF16),
             jax.ShapeDtypeStruct(att.shape, BF16),
         ],
-        in_specs=[vmem, vmem, vmem, hbm, hbm],
+        in_specs=[vmem] * 3 + [pl.BlockSpec(memory_space=pltpu.HBM)] * 2,
         out_specs=[vmem, vmem],
         scratch_shapes=[
             pltpu.VMEM(out_weight.shape, BF16),
@@ -379,7 +393,7 @@
         compiler_params=PARAMS,
         cost_estimate=cost(10),
         name="middle",
-    )(att, pair, gains, out_weight, qkv_weight)
+    )(att, pair, gains, in_hbm(out_weight), in_hbm(qkv_weight))
 
 
 def swap(array, axis, count, s):

time: 106 us -> 95.2 us (0.90)
  Pallas kernels: 31.1 us -> 21.8 us
  blocking collectives: 14.7 us -> 13.5 us
    pallas_call x1, Pallas kernels: 4.11 us -> 1.48 us  [space_weights(): pl.pallas_call(space_weights_kernel, out_shape=jax.ShapeDtypeStruct((rows...]
    pallas_call x1, Pallas kernels: 6.29 us -> 3.68 us  [space_bwd(): pl.pallas_call(functools.partial(space_bwd_kernel, axis, parts), out_shap...]
    pallas_call x1, Pallas kernels: 2.53 us -> 1.22 us  [unturn(): pl.pallas_call(functools.partial(unturn_kernel, axis), out_shape=[jax.Sha...]
    pallas_call x1, Pallas kernels: 3.8 us -> 2.52 us  [space_fwd(): pl.pallas_call(functools.partial(space_fwd_kernel, axis, parts), out_shap...]
    all_to_all x1, waiting for transfers between devices: 4.7 us -> 5.97 us  [local(): att = lax.all_to_all(sent, ('seq', 'frm'), 0, 0, tiled=True)]
    all_to_all x1, blocking collectives: 14.7 us -> 13.5 us  [local(): up = lax.all_to_all(up, ('seq', 'frm'), 0, 0, tiled=True)]
    pallas_call x1, Pallas kernels: 11.6 us -> 10.5 us  [middle(): pl.pallas_call(functools.partial(middle_kernel, count, parts), out_shape=...]
    unnamed x18 -> x8, local copies, waits for them, and re-layouts: 2.2 us -> 1.35 us
  transfers between devices with their start and end apart: 9 -> 9, of which waited for: 7 -> 7; matrix products, arithmetic and copies ran while one was open for 0% -> 0% of each run, Pallas kernels for 8% -> 4%
where the time goes in v3:
time: 95.2 us; the launch traced here: 94.8 us
  waiting for transfers between devices  38.2 us (40%)
  Pallas kernels  21.8 us (23%)
  starting transfers between devices  19.3 us (20%)
  blocking collectives  13.5 us (14%)
  local copies, waits for them, and re-layouts  1.35 us (1%)
    ppermute x6, waiting for transfers between devices, swap(): return lax.ppermute(array, axis, [(n, n ^ s) for n in range(count)])  32.2 us
    all_to_all x1, blocking collectives, local(): up = lax.all_to_all(up, ('seq', 'frm'), 0, 0, tiled=True)  13.5 us
    pallas_call x1, Pallas kernels, middle(): pl.pallas_call(functools.partial(middle_kernel, count, parts), out_shape=...  10.5 us
    ppermute x6, starting transfers between devices, swap(): return lax.ppermute(array, axis, [(n, n ^ s) for n in range(count)])  7.1 us
    all_to_all x1, waiting for transfers between devices, local(): att = lax.all_to_all(sent, ('seq', 'frm'), 0, 0, tiled=True)  5.97 us
    all_to_all x1, starting transfers between devices, local(): att = lax.all_to_all(sent, ('seq', 'frm'), 0, 0, tiled=True)  5.28 us
    pallas_call x1, Pallas kernels, space_bwd(): pl.pallas_call(functools.partial(space_bwd_kernel, axis, parts), out_shap...  3.68 us
    all_to_all x1, starting transfers between devices, local(): both = lax.all_to_all(both, 'frm', 0, 0, tiled=True)  3.48 us
  transfers between devices with their start and end apart: 9, of which 7 were waited for; matrix products, arithmetic and copies ran while one was open for 0% of the time, Pallas kernels for 4%

profile of v3, /device:TPU:8, one launch (start us, length us, event | category | flops | bytes accessed | tf_op | source)
XLA Modules:
  0.0 94.8 jit_solution(8637104629337069228)
XLA Ops:
  0.6 0.0 copy-start.1
  0.6 2.4 %turn.1 = (bf16[4,2,32,1152]{3,2,1,0:T(8,128)(2,1)}, bf16[3,288,128]{2,1,0:T(8,128)(2,1)S(1)}, bf16[3,288,128]{2,1,0:T(8,128)(2,1)S(1)}, bf16[3,288,128]{2,1,0:T(8,128)(2,1)S(1)}, bf16[3,288,128]{2,1,0:T(8,128)(2,1)S(1)}) custom-call(bf16[128,1152]{1,0:T(8,128)(2,1)} %bitcast.11, bf16[128,1152]{1,0:T(8,128)(2,1)} %bitcast.12, bf16[128,1152]{1,0:T(8,128)(2,1)} %bitcast.13, ...), custom_call_target="tpu_custom_call" | custom-call | flops 3000000000 | tf_op jit(solution)/shard_map/turn/pallas_call | solution.py:115
  3.0 0.1 collective-permute-start
  3.1 3.0 %collective-permute-start.1 = (bf16[3,288,128]{2,1,0:T(8,128)(2,1)S(1)}, bf16[3,288,128]{2,1,0:T(8,128)(2,1)S(1)}, u32[]{:S(2)}, u32[]{:S(2)}) collective-permute-start(bf16[3,288,128]{2,1,0:T(8,128)(2,1)S(1)} %get-tuple-element.29), channel_id=1, source_target_pairs={{0,8},{4,12},{8,0},{12,4},{1,9},{5,13},{9,1},{13,5},{2,10},{6,14},... | collective-permute-start | bytes 663560 | tf_op jit(solution)/shard_map/ppermute | solution.py:402
  6.1 0.5 collective-permute-start.2
  6.6 3.5 %all-to-all-start.1 = ((bf16[4,2,32,1152]{3,2,1,0:T(8,128)(2,1)}), bf16[4,2,32,1152]{3,2,1,0:T(8,128)(2,1)S(1)}, u32[]{:S(2)}, u32[]{:S(2)}) async-start(bf16[4,2,32,1152]{3,2,1,0:T(8,128)(2,1)} %get-tuple-element.31), calls=%async_computation.1 | async-start | bytes 1179648 | tf_op jit(solution)/shard_map/all_to_all | solution.py:427
  10.0 2.0 %collective-permute-done.refs_1_ = bf16[3,288,128]{2,1,0:T(8,128)(2,1)S(1)} collective-permute-done((bf16[3,288,128]{2,1,0:T(8,128)(2,1)S(1)}, bf16[3,288,128]{2,1,0:T(8,128)(2,1)S(1)}, u32[]{:S(2)}, u32[]{:S(2)}) %collective-permute-start) | collective-permute-done | bytes 221216 | tf_op jit(solution)/shard_map/ppermute | solution.py:402
  12.0 9.4 %collective-permute-done.1.refs_2_ = bf16[3,288,128]{2,1,0:T(8,128)(2,1)S(1)} collective-permute-done((bf16[3,288,128]{2,1,0:T(8,128)(2,1)S(1)}, bf16[3,288,128]{2,1,0:T(8,128)(2,1)S(1)}, u32[]{:S(2)}, u32[]{:S(2)}) %collective-permute-start.1) | collective-permute-done | bytes 221216 | tf_op jit(solution)/shard_map/ppermute | solution.py:402
  21.5 4.2 %collective-permute-done.2.refs_3_ = bf16[3,288,128]{2,1,0:T(8,128)(2,1)S(1)} collective-permute-done((bf16[3,288,128]{2,1,0:T(8,128)(2,1)S(1)}, bf16[3,288,128]{2,1,0:T(8,128)(2,1)S(1)}, u32[]{:S(2)}, u32[]{:S(2)}) %collective-permute-start.2) | collective-permute-done | bytes 221216 | tf_op jit(solution)/shard_map/ppermute | solution.py:402
  25.7 0.0 copy-done.1
  25.7 2.5 %space_fwd.1 = bf16[16,72,128]{2,1,0:T(8,128)(2,1)} custom-call(f32[2,72]{1,0:T(2,128)S(1)} %copy-done.1, bf16[3,288,128]{2,1,0:T(8,128)(2,1)S(1)} %get-tuple-element.32.refs_0_, bf16[3,288,128]{2,1,0:T(8,128)(2,1)S(1)} %collective-permute-done.refs_1_, bf16[3,288,128]{2,1,0:T(8,128)(2,1)S(1)} %collective-permute-done.1.refs_2_, ...), custom_call_target="tpu_custom_call" | custom-call | flops 4000000000 | tf_op jit(solution)/shard_map/space_fwd/pallas_call | solution.py:189
  28.2 0.0 all-to-all-done.1.pair_ref
  28.2 5.3 %all-to-all-start = ((bf16[16,72,128]{2,1,0:T(8,128)(2,1)}), bf16[16,72,128]{2,1,0:T(8,128)(2,1)S(1)}, u32[]{:S(2)}, u32[]{:S(2)}) async-start(bf16[16,72,128]{2,1,0:T(8,128)(2,1)} %space_fwd.1), calls=%async_computation | async-start | bytes 589824 | tf_op jit(solution)/shard_map/all_to_all | solution.py:429
  33.5 0.0 copy-start
  33.5 1.5 %space_weights.1.weight_ref = bf16[4,512,512]{2,1,0:T(8,128)(2,1)S(1)} custom-call(f32[2,72]{1,0:T(2,128)S(1)} %copy-done.1, bf16[3,288,128]{2,1,0:T(8,128)(2,1)S(1)} %get-tuple-element.32.refs_0_, bf16[3,288,128]{2,1,0:T(8,128)(2,1)S(1)} %collective-permute-done.refs_1_, bf16[3,288,128]{2,1,0:T(8,128)(2,1)S(1)} %collective-permute-done.1.refs_2_, ...), custom_call_target="tpu_custom_call" | custom-call | flops 8000000000 | tf_op jit(solution)/shard_map/space_weights/pallas_call | solution.py:212
  35.0 0.0 copy-start.2
  35.0 1.3 %copy-done.2 = bf16[4,512,512]{2,1,0:T(8,128)(2,1)} copy-done((bf16[4,512,512]{2,1,0:T(8,128)(2,1)}, bf16[4,512,512]{2,1,0:T(8,128)(2,1)S(1)}, u32[]{:S(2)}) %copy-start.2) | copy-done | bytes 2097176
  36.3 6.0 %all-to-all-done.att_ref = bf16[16,72,128]{2,1,0:T(8,128)(2,1)S(1)} async-done(((bf16[16,72,128]{2,1,0:T(8,128)(2,1)}), bf16[16,72,128]{2,1,0:T(8,128)(2,1)S(1)}, u32[]{:S(2)}, u32[]{:S(2)}) %all-to-all-start) | async-done | bytes 294944 | tf_op jit(solution)/shard_map/all_to_all | solution.py:429
  42.3 0.0 copy-done
  42.3 10.5 %middle.1 = (bf16[4,32,1152]{2,1,0:T(8,128)(2,1)}, bf16[16,72,128]{2,1,0:T(8,128)(2,1)S(1)}) custom-call(bf16[16,72,128]{2,1,0:T(8,128)(2,1)S(1)} %all-to-all-done.att_ref, bf16[4,2,32,1152]{3,2,1,0:T(8,128)(2,1)S(1)} %all-to-all-done.1.pair_ref, f32[2,72]{1,0:T(2,128)S(1)} %copy-done, bf16[1152,1152]{1,0:T(8,128)(2,1)} %ow_hbm.1, bf16[3,1152,1152]{2,1,0:T(8,128)(2,1)} %qw_hbm.1), custom_call_target="tpu_custom_call" | custom-call | flops 10000000000 | tf_op jit(solution)/shard_map/middle/pallas_call | solution.py:375
  52.9 13.5 %all_to_all.20.up_ref = bf16[16,72,128]{2,1,0:T(8,128)(2,1)S(1)} all-to-all(bf16[16,72,128]{2,1,0:T(8,128)(2,1)S(1)} %get-tuple-element.40), channel_id=1, replica_groups=mesh['grp'=2,'seq'=4,'frm'=4] {'seq','frm'}, dimensions={0} | all-to-all | bytes 589824 | tf_op jit(solution)/shard_map/all_to_all | solution.py:434
  66.3 0.0 copy-done.3
  66.3 3.7 %space_bwd.1 = (bf16[3,288,128]{2,1,0:T(8,128)(2,1)S(1)}, bf16[3,288,128]{2,1,0:T(8,128)(2,1)S(1)}, bf16[3,288,128]{2,1,0:T(8,128)(2,1)S(1)}, bf16[3,288,128]{2,1,0:T(8,128)(2,1)S(1)}) custom-call(f32[2,72]{1,0:T(2,128)S(1)} %copy-done.1, bf16[4,512,512]{2,1,0:T(8,128)(2,1)S(1)} %copy-done.3, bf16[16,72,128]{2,1,0:T(8,128)(2,1)S(1)} %all_to_all.20.up_ref, ...), custom_call_target="tpu_custom_call" | custom-call | flops 6000000000 | tf_op jit(solution)/shard_map/space_bwd/pallas_call | solution.py:264
  70.0 1.9 %collective-permute-start.3 = (bf16[3,288,128]{2,1,0:T(8,128)(2,1)S(1)}, bf16[3,288,128]{2,1,0:T(8,128)(2,1)S(1)}, u32[]{:S(2)}, u32[]{:S(2)}) collective-permute-start(bf16[3,288,128]{2,1,0:T(8,128)(2,1)S(1)} %get-tuple-element.41), channel_id=1, source_target_pairs={{0,4},{4,0},{8,12},{12,8},{1,5},{5,1},{9,13},{13,9},{2,6},{6,2},{1... | collective-permute-start | bytes 663560 | tf_op jit(solution)/shard_map/ppermute | solution.py:402
  71.9 1.2 %collective-permute-start.4 = (bf16[3,288,128]{2,1,0:T(8,128)(2,1)S(1)}, bf16[3,288,128]{2,1,0:T(8,128)(2,1)S(1)}, u32[]{:S(2)}, u32[]{:S(2)}) collective-permute-start(bf16[3,288,128]{2,1,0:T(8,128)(2,1)S(1)} %get-tuple-element.44), channel_id=1, source_target_pairs={{0,8},{4,12},{8,0},{12,4},{1,9},{5,13},{9,1},{13,5},{2,10},{6,14},... | collective-permute-start | bytes 663560 | tf_op jit(solution)/shard_map/ppermute | solution.py:402
  73.2 0.4 collective-permute-start.5
  73.6 6.6 %collective-permute-done.3.refs_1_ = bf16[3,288,128]{2,1,0:T(8,128)(2,1)S(1)} collective-permute-done((bf16[3,288,128]{2,1,0:T(8,128)(2,1)S(1)}, bf16[3,288,128]{2,1,0:T(8,128)(2,1)S(1)}, u32[]{:S(2)}, u32[]{:S(2)}) %collective-permute-start.3) | collective-permute-done | bytes 221216 | tf_op jit(solution)/shard_map/ppermute | solution.py:402
  80.2 3.5 %all-to-all-start.3 = ((bf16[4,32,1152]{2,1,0:T(8,128)(2,1)}), bf16[4,32,1152]{2,1,0:T(8,128)(2,1)S(1)}, u32[]{:S(2)}, u32[]{:S(2)}) async-start(bf16[4,32,1152]{2,1,0:T(8,128)(2,1)} %get-tuple-element.42), calls=%async_computation.3 | async-start | bytes 589824 | tf_op jit(solution)/shard_map/all_to_all | solution.py:438
  83.6 4.9 %collective-permute-done.4.refs_2_ = bf16[3,288,128]{2,1,0:T(8,128)(2,1)S(1)} collective-permute-done((bf16[3,288,128]{2,1,0:T(8,128)(2,1)S(1)}, bf16[3,288,128]{2,1,0:T(8,128)(2,1)S(1)}, u32[]{:S(2)}, u32[]{:S(2)}) %collective-permute-start.4) | collective-permute-done | bytes 221216 | tf_op jit(solution)/shard_map/ppermute | solution.py:402
  88.5 5.0 %collective-permute-done.5.refs_3_ = bf16[3,288,128]{2,1,0:T(8,128)(2,1)S(1)} collective-permute-done((bf16[3,288,128]{2,1,0:T(8,128)(2,1)S(1)}, bf16[3,288,128]{2,1,0:T(8,128)(2,1)S(1)}, u32[]{:S(2)}, u32[]{:S(2)}) %collective-permute-start.5) | collective-permute-done | bytes 221216 | tf_op jit(solution)/shard_map/ppermute | solution.py:402
  93.6 0.0 all-to-all-done.3
  93.6 1.2 %unturn.1 = (bf16[128,1152]{1,0:T(8,128)(2,1)}, bf16[128,1152]{1,0:T(8,128)(2,1)}, bf16[128,1152]{1,0:T(8,128)(2,1)}, bf16[128,1152]{1,0:T(8,128)(2,1)}) custom-call(bf16[128,1152]{1,0:T(8,128)(2,1)S(1)} %bitcast.10, bf16[3,288,128]{2,1,0:T(8,128)(2,1)S(1)} %get-tuple-element.43.refs_0_, bf16[3,288,128]{2,1,0:T(8,128)(2,1)S(1)} %collective-permute-done.3.refs_1_, ...), custom_call_target="tpu_custom_call" | custom-call | flops 3000000000 | tf_op jit(solution)/shard_map/unturn/pallas_call | solution.py:147
  (1 shorter events, 0.0 us)
Async XLA Ops:
  0.6 25.1 %copy-start.1 = (f32[2,72]{1,0:T(2,128)S(1)}, f32[2,72]{1,0:T(2,128)}, u32[]{:S(2)}) copy-start(f32[2,72]{1,0:T(2,128)} %gain_ref.7) | copy-start | bytes 1732
  3.0 9.0 %collective-permute-start = (bf16[3,288,128]{2,1,0:T(8,128)(2,1)S(1)}, bf16[3,288,128]{2,1,0:T(8,128)(2,1)S(1)}, u32[]{:S(2)}, u32[]{:S(2)}) collective-permute-start(bf16[3,288,128]{2,1,0:T(8,128)(2,1)S(1)} %get-tuple-element.28), channel_id=1, source_target_pairs={{0,4},{4,0},{8,12},{12,8},{1,5},{5,1},{9,13},{13,9},{2,6},{6,2},{1... | collective-permute-start | bytes 663560 | tf_op jit(solution)/shard_map/ppermute | solution.py:402
  3.1 18.4 %collective-permute-start.1 = (bf16[3,288,128]{2,1,0:T(8,128)(2,1)S(1)}, bf16[3,288,128]{2,1,0:T(8,128)(2,1)S(1)}, u32[]{:S(2)}, u32[]{:S(2)}) collective-permute-start(bf16[3,288,128]{2,1,0:T(8,128)(2,1)S(1)} %get-tuple-element.29), channel_id=1, source_target_pairs={{0,8},{4,12},{8,0},{12,4},{1,9},{5,13},{9,1},{13,5},{2,10},{6,14},... | collective-permute-start | bytes 663560 | tf_op jit(solution)/shard_map/ppermute | solution.py:402
  6.1 19.6 %collective-permute-start.2 = (bf16[3,288,128]{2,1,0:T(8,128)(2,1)S(1)}, bf16[3,288,128]{2,1,0:T(8,128)(2,1)S(1)}, u32[]{:S(2)}, u32[]{:S(2)}) collective-permute-start(bf16[3,288,128]{2,1,0:T(8,128)(2,1)S(1)} %get-tuple-element.30), channel_id=1, source_target_pairs={{0,12},{4,8},{8,4},{12,0},{1,13},{5,9},{9,5},{13,1},{2,14},{6,10},... | collective-permute-start | bytes 663560 | tf_op jit(solution)/shard_map/ppermute | solution.py:402
  6.6 21.7 %all-to-all-start.1 = ((bf16[4,2,32,1152]{3,2,1,0:T(8,128)(2,1)}), bf16[4,2,32,1152]{3,2,1,0:T(8,128)(2,1)S(1)}, u32[]{:S(2)}, u32[]{:S(2)}) async-start(bf16[4,2,32,1152]{3,2,1,0:T(8,128)(2,1)} %get-tuple-element.31), calls=%async_computation.1 | async-start | bytes 1179648 | tf_op jit(solution)/shard_map/all_to_all | solution.py:427
  28.2 14.1 %all-to-all-start = ((bf16[16,72,128]{2,1,0:T(8,128)(2,1)}), bf16[16,72,128]{2,1,0:T(8,128)(2,1)S(1)}, u32[]{:S(2)}, u32[]{:S(2)}) async-start(bf16[16,72,128]{2,1,0:T(8,128)(2,1)} %space_fwd.1), calls=%async_computation | async-start | bytes 589824 | tf_op jit(solution)/shard_map/all_to_all | solution.py:429
  33.5 8.8 %copy-start = (f32[2,72]{1,0:T(2,128)S(1)}, f32[2,72]{1,0:T(2,128)}, u32[]{:S(2)}) copy-start(f32[2,72]{1,0:T(2,128)} %gain_ref.6) | copy-start | bytes 1732
  35.0 1.3 %copy-start.2 = (bf16[4,512,512]{2,1,0:T(8,128)(2,1)}, bf16[4,512,512]{2,1,0:T(8,128)(2,1)S(1)}, u32[]{:S(2)}) copy-start(bf16[4,512,512]{2,1,0:T(8,128)(2,1)S(1)} %space_weights.1.weight_ref) | copy-start | bytes 6291460
  42.3 24.0 %copy-start.3 = (bf16[4,512,512]{2,1,0:T(8,128)(2,1)S(1)}, bf16[4,512,512]{2,1,0:T(8,128)(2,1)}, u32[]{:S(2)}) copy-start(bf16[4,512,512]{2,1,0:T(8,128)(2,1)} %copy-done.2) | copy-start | bytes 6291460
  70.0 10.2 %collective-permute-start.3 = (bf16[3,288,128]{2,1,0:T(8,128)(2,1)S(1)}, bf16[3,288,128]{2,1,0:T(8,128)(2,1)S(1)}, u32[]{:S(2)}, u32[]{:S(2)}) collective-permute-start(bf16[3,288,128]{2,1,0:T(8,128)(2,1)S(1)} %get-tuple-element.41), channel_id=1, source_target_pairs={{0,4},{4,0},{8,12},{12,8},{1,5},{5,1},{9,13},{13,9},{2,6},{6,2},{1... | collective-permute-start | bytes 663560 | tf_op jit(solution)/shard_map/ppermute | solution.py:402
  71.9 16.6 %collective-permute-start.4 = (bf16[3,288,128]{2,1,0:T(8,128)(2,1)S(1)}, bf16[3,288,128]{2,1,0:T(8,128)(2,1)S(1)}, u32[]{:S(2)}, u32[]{:S(2)}) collective-permute-start(bf16[3,288,128]{2,1,0:T(8,128)(2,1)S(1)} %get-tuple-element.44), channel_id=1, source_target_pairs={{0,8},{4,12},{8,0},{12,4},{1,9},{5,13},{9,1},{13,5},{2,10},{6,14},... | collective-permute-start | bytes 663560 | tf_op jit(solution)/shard_map/ppermute | solution.py:402
  73.2 20.4 %collective-permute-start.5 = (bf16[3,288,128]{2,1,0:T(8,128)(2,1)S(1)}, bf16[3,288,128]{2,1,0:T(8,128)(2,1)S(1)}, u32[]{:S(2)}, u32[]{:S(2)}) collective-permute-start(bf16[3,288,128]{2,1,0:T(8,128)(2,1)S(1)} %get-tuple-element.45), channel_id=1, source_target_pairs={{0,12},{4,8},{8,4},{12,0},{1,13},{5,9},{9,5},{13,1},{2,14},{6,10},... | collective-permute-start | bytes 663560 | tf_op jit(solution)/shard_map/ppermute | solution.py:402
  80.2 13.4 %all-to-all-start.3 = ((bf16[4,32,1152]{2,1,0:T(8,128)(2,1)}), bf16[4,32,1152]{2,1,0:T(8,128)(2,1)S(1)}, u32[]{:S(2)}, u32[]{:S(2)}) async-start(bf16[4,32,1152]{2,1,0:T(8,128)(2,1)} %get-tuple-element.42), calls=%async_computation.3 | async-start | bytes 589824 | tf_op jit(solution)/shard_map/all_to_all | solution.py:438

commit v4 on v3

--- a/solution.py
+++ b/solution.py
@@ -129,11 +129,13 @@
     return outs[0], outs[1:]
 
 
-def unturn_kernel(axis, grad_ref, *refs):
-    in_refs, out_refs, grad_out, held = refs[:-5], refs[-5:-2], refs[-2], refs[-1]
+def unturn_kernel(axis, frame_axis, count, *refs):
+    in_refs, frame_refs = refs[:count], refs[count:-5]
+    out_refs, grad_out, held = refs[-5:-2], refs[-2], refs[-1]
     rows = in_refs[0].shape[1]
-    me = lax.axis_index(axis)
-    grad_out[...] = grad_ref[...]
+    me, mine = lax.axis_index(axis), lax.axis_index(frame_axis)
+    for s, ref in enumerate(frame_refs):
+        grad_out[mine ^ s] = ref[...]
     for s, ref in enumerate(in_refs):
         start = pl.multiple_of((me ^ s) * rows, rows)
         held[:, pl.ds(start, rows), :] = ref[...]
@@ -141,17 +143,18 @@
         ref[...] = held[n].T
 
 
-def unturn(axis, grad, blocks):
+def unturn(axis, frame_axis, blocks, frame_blocks):
     count = len(blocks)
     _, rows, tokens = blocks[0].shape
     return pl.pallas_call(
-        functools.partial(unturn_kernel, axis),
-        out_shape=[jax.ShapeDtypeStruct((tokens, rows * count), BF16)] * 4,
+        functools.partial(unturn_kernel, axis, frame_axis, count),
+        out_shape=[jax.ShapeDtypeStruct((tokens, rows * count), BF16)] * 3
+        + [jax.ShapeDtypeStruct((len(frame_blocks),) + frame_blocks[0].shape, BF16)],
         scratch_shapes=[pltpu.VMEM((3, rows * count, tokens), BF16)],
         compiler_params=PARAMS,
         cost_estimate=cost(3),
         name="unturn",
-    )(grad, *blocks)
+    )(*blocks, *frame_blocks)
 
 
 def gather_part(refs, part):
@@ -197,13 +200,15 @@
 
 
 def space_weights_kernel(gain_ref, *refs):
-    in_refs, weight_ref = refs[:-1], refs[-1]
-    query, key = (gather_part(in_refs, n) for n in range(2))
+    in_refs, weight_ref, att_ref = refs[:-2], refs[-2], refs[-1]
+    query, key, value = (gather_part(in_refs, n) for n in range(3))
     query_gain, key_gain = (column(gain_ref[n : n + 1]) for n in range(2))
     for h in range(weight_ref.shape[0]):
         cut = slice(h * HD, (h + 1) * HD)
         expons, scale = head_expons(query[cut], key[cut], query_gain, key_gain)
-        weight_ref[h] = (expons * scale).astype(BF16)
+        weights = (expons * scale).astype(BF16)
+        weight_ref[h] = weights
+        att_ref[cut, :] = dot(value[cut].astype(BF16), weights, ((1,), (0,)))
 
 
 def space_weights(gains, arrays):
@@ -211,14 +216,17 @@
     _, rows, tokens = arrays[0].shape
     return pl.pallas_call(
         space_weights_kernel,
-        out_shape=jax.ShapeDtypeStruct((rows // HD, count * tokens, count * tokens), BF16),
+        out_shape=[
+            jax.ShapeDtypeStruct((rows // HD, count * tokens, count * tokens), BF16),
+            jax.ShapeDtypeStruct((rows, count * tokens), F32),
+        ],
         compiler_params=PARAMS,
         cost_estimate=cost(8),
         name="space_weights",
     )(gains, *arrays)
 
 
-def space_bwd_kernel(axis, parts, gain_ref, weight_ref, up_ref, *refs):
+def space_bwd_kernel(axis, parts, gain_ref, weight_ref, att_ref, up_ref, *refs):
     count = (len(refs) - 1) // 2
     in_refs, out_refs, held = refs[:count], refs[count:-1], refs[-1]
     rows = in_refs[0].shape[1]
@@ -229,6 +237,8 @@
     query, key, value = (gather_part(in_refs, n) for n in range(3))
     query_gain, key_gain = (column(gain_ref[n : n + 1]) for n in range(2))
     factor = HD ** (-0.5)
+    extra = lax.broadcasted_iota(jnp.int32, (8, query.shape[1]), 0)
+    ones = jnp.where(extra < 2, 1.0, 0.0)
     grads = []
     for h in range(rows // HD):
         cut = slice(h * HD, (h + 1) * HD)
@@ -236,14 +246,18 @@
         key_hat, key_inv = head_norm(key[cut])
         query_nrm = (query_hat * query_gain).astype(BF16)
         key_nrm = (key_hat * key_gain).astype(BF16)
-        up = held[cut, :].astype(BF16)
+        up_wide = held[cut, :]
+        up = up_wide.astype(BF16)
         weights = weight_ref[h]
-        shares = weights.astype(F32)
-        share_grad = dot(value[cut].astype(BF16), up, ((0,), (0,)))
-        centre = jnp.sum(shares * share_grad, axis=0, keepdims=True)
-        score_grad = (shares * (share_grad - centre) * factor).astype(BF16)
-        query_grad = dot(key_nrm, score_grad, ((1,), (0,)))
-        key_grad = dot(query_nrm, score_grad, ((1,), (1,)))
+        centre = jnp.sum(up_wide * att_ref[cut, :], axis=0, keepdims=True)
+        high = rounded(centre)
+        rows_in = jnp.where(extra == 0, -high, jnp.where(extra == 1, high - centre, 0.0))
+        value_rows = jnp.concatenate([value[cut], ones], axis=0).astype(BF16)
+        up_rows = jnp.concatenate([up_wide, rows_in], axis=0).astype(BF16)
+        centred = dot(value_rows, up_rows, ((0,), (0,)))
+        score_grad = (weights.astype(F32) * centred).astype(BF16)
+        query_grad = dot(key_nrm, score_grad, ((1,), (0,))) * factor
+        key_grad = dot(query_nrm, score_grad, ((1,), (1,))) * factor
         value_grad = dot(up, weights, ((1,), (1,)))
         grads.append(
             (
@@ -258,7 +272,7 @@
             out_refs[s][n] = whole[:, s * LANES : (s + 1) * LANES]
 
 
-def space_bwd(axis, parts, gains, weights, up, arrays):
+def space_bwd(axis, parts, gains, weights, attended, up, arrays):
     count = len(arrays)
     _, rows, tokens = arrays[0].shape
     return pl.pallas_call(
@@ -268,7 +282,7 @@
         compiler_params=PARAMS,
         cost_estimate=cost(6),
         name="space_bwd",
-    )(gains, weights, up, *arrays)
+    )(gains, weights, attended, up, *arrays)
 
 
 def time_head(query_in, key_in, value, upward, query_gain, key_gain, parts):
@@ -301,28 +315,14 @@
 
 
 def middle_kernel(
-    count,
-    parts,
-    att_ref,
-    pair_ref,
-    gain_ref,
-    ow_hbm,
-    qw_hbm,
-    gr_ref,
-    up_ref,
-    ow_ref,
-    qw_ref,
-    att_s,
-    low_s,
-    cot_s,
-    qkv_s,
-    grad_s,
-    sems,
+    frame_axis, count, parts, att_ref, pair_ref, gain_ref, ow_hbm, qw_hbm, up_ref, *refs
 ):
+    gr_refs = refs[:parts]
+    ow_ref, qw_ref, att_s, low_s, cot_s, qkv_s, grad_s, back_s, sems = refs[parts:]
     width = ow_ref.shape[0]
     rows = width // count
-    copies = [pltpu.make_async_copy(ow_hbm, ow_ref, sems.at[0])]
-    copies += [pltpu.make_async_copy(qw_hbm.at[n], qw_ref.at[n], sems.at[1 + n]) for n in range(3)]
+    copies = [pltpu.make_async_copy(ow_hbm, ow_ref, sems.at[3])]
+    copies += [pltpu.make_async_copy(qw_hbm.at[n], qw_ref.at[n], sems.at[n]) for n in range(3)]
     for copy in copies:
         copy.start()
     for z in range(count):
@@ -362,24 +362,24 @@
         - low_s[...] * jnp.mean(upward * low_s[...], axis=1, keepdims=True)
     )
     grad = grad.astype(BF16)
-    gr_ref[...] = grad.reshape(gr_ref.shape)
+    back_s[...] = grad.reshape(back_s.shape)
+    mine = lax.axis_index(frame_axis)
+    for s, ref in enumerate(gr_refs):
+        ref[...] = back_s[mine ^ s]
     att_s[...] = dot(ow_ref[...], grad, ((1,), (1,)))
     for z in range(count):
         for f, block in enumerate(pack(att_s[z * rows : (z + 1) * rows, :], parts)):
             up_ref[z * parts + f] = block.astype(BF16)
 
 
-def middle(count, parts, att, pair, gains, out_weight, qkv_weight):
+def middle(frame_axis, count, parts, att, pair, gains, out_weight, qkv_weight):
     width = out_weight.shape[0]
     vmem = pl.BlockSpec(memory_space=pltpu.VMEM)
-    return pl.pallas_call(
-        functools.partial(middle_kernel, count, parts),
-        out_shape=[
-            jax.ShapeDtypeStruct((pair.shape[0],) + pair.shape[2:], BF16),
-            jax.ShapeDtypeStruct(att.shape, BF16),
-        ],
+    outs = pl.pallas_call(
+        functools.partial(middle_kernel, frame_axis, count, parts),
+        out_shape=[jax.ShapeDtypeStruct(att.shape, BF16)]
+        + [jax.ShapeDtypeStruct(pair.shape[2:], BF16)] * parts,
         in_specs=[vmem] * 3 + [pl.BlockSpec(memory_space=pltpu.HBM)] * 2,
-        out_specs=[vmem, vmem],
         scratch_shapes=[
             pltpu.VMEM(out_weight.shape, BF16),
             pltpu.VMEM(qkv_weight.shape, BF16),
@@ -388,12 +388,14 @@
             pltpu.VMEM((width, LANES), F32),
             pltpu.VMEM((3, width, LANES), F32),
             pltpu.VMEM((3, width, LANES), F32),
+            pltpu.VMEM((parts,) + pair.shape[2:], BF16),
             pltpu.SemaphoreType.DMA((4,)),
         ],
         compiler_params=PARAMS,
         cost_estimate=cost(10),
         name="middle",
     )(att, pair, gains, in_hbm(out_weight), in_hbm(qkv_weight))
+    return outs[0], outs[1:]
 
 
 def swap(array, axis, count, s):
@@ -428,18 +430,21 @@
     sent = space_fwd("seq", parts, space_gains, held)
     att = lax.all_to_all(sent, ("seq", "frm"), 0, 0, tiled=True)
     late = lax.optimization_barrier((sent, *held))[1:]
-    weights = space_weights(space_gains, late)
-    att, both, weights = lax.optimization_barrier((att, both, weights))
-    grad, up = middle(count, parts, att, both, time_gains, out_weight, qkv_weight)
+    weights, attended = space_weights(space_gains, late)
+    att, both, weights, attended = lax.optimization_barrier((att, both, weights, attended))
+    up, grad = middle("frm", count, parts, att, both, time_gains, out_weight, qkv_weight)
     up = lax.all_to_all(up, ("seq", "frm"), 0, 0, tiled=True)
-    grads = space_bwd("seq", parts, space_gains, weights, up, held)
+    grads = space_bwd("seq", parts, space_gains, weights, attended, up, held)
     back = [swap(grads[s], "seq", count, s) for s in range(count)]
-    grad, _ = lax.optimization_barrier((grad, back[1]))
-    grad = lax.all_to_all(grad, "frm", 0, 0, tiled=True)
-    grad_query, grad_key, grad_value, grad = unturn(
-        "seq", grad.reshape((tokens, width)), back
-    )
-    return (grad[None], grad_query[None], grad_key[None], grad_value[None])
+    grad = lax.optimization_barrier((*grad, back[1]))[:-1]
+    grad = [swap(grad[s], "frm", parts, s) for s in range(parts)]
+    grad_query, grad_key, grad_value, grad = unturn("seq", "frm", back, grad)
+    return (
+        grad.reshape((1, tokens, width)),
+        grad_query[None],
+        grad_key[None],
+        grad_value[None],
+    )
 
 
 def solution(mesh):

time: 95.2 us -> 93.7 us (0.984)
  starting transfers between devices: 19.3 us -> 17.7 us
  waiting for transfers between devices: 38.2 us -> 39.4 us
  Pallas kernels: 21.8 us -> 20.8 us
    all_to_all x1 -> x0, starting transfers between devices: 3.45 us -> none  [local(): grad = lax.all_to_all(grad, 'frm', 0, 0, tiled=True)]
    ppermute x6 -> x9, starting transfers between devices: 7.1 us -> 8.95 us  [swap(): return lax.ppermute(array, axis, [(n, n ^ s) for n in range(count)])]
    ppermute x6 -> x9, waiting for transfers between devices: 32.2 us -> 33.8 us  [swap(): return lax.ppermute(array, axis, [(n, n ^ s) for n in range(count)])]
  transfers between devices with their start and end apart: 9 -> 11, of which waited for: 7 -> 7; matrix products, arithmetic and copies ran while one was open for 0% -> 0% of each run, Pallas kernels for 4% -> 5%
where the time goes in v4:
time: 93.7 us; the launch traced here: 93.4 us
  waiting for transfers between devices  39.4 us (42%)
  Pallas kernels  20.8 us (22%)
  starting transfers between devices  17.7 us (19%)
  blocking collectives  13.5 us (14%)
  local copies, waits for them, and re-layouts  1.34 us (1%)
    ppermute x9, waiting for transfers between devices, swap(): return lax.ppermute(array, axis, [(n, n ^ s) for n in range(count)])  33.8 us
    all_to_all x1, blocking collectives, local(): up = lax.all_to_all(up, ('seq', 'frm'), 0, 0, tiled=True)  13.5 us
    pallas_call x1, Pallas kernels, middle(): pl.pallas_call(functools.partial(middle_kernel, frame_axis, count, parts)...  9.98 us
    ppermute x9, starting transfers between devices, swap(): return lax.ppermute(array, axis, [(n, n ^ s) for n in range(count)])  8.95 us
    all_to_all x1, waiting for transfers between devices, local(): att = lax.all_to_all(sent, ('seq', 'frm'), 0, 0, tiled=True)  5.58 us
    all_to_all x1, starting transfers between devices, local(): att = lax.all_to_all(sent, ('seq', 'frm'), 0, 0, tiled=True)  5.28 us
    all_to_all x1, starting transfers between devices, local(): both = lax.all_to_all(both, 'frm', 0, 0, tiled=True)  3.48 us
    pallas_call x1, Pallas kernels, space_bwd(): pl.pallas_call(functools.partial(space_bwd_kernel, axis, parts), out_shap...  2.85 us
  transfers between devices with their start and end apart: 11, of which 7 were waited for; matrix products, arithmetic and copies ran while one was open for 0% of the time, Pallas kernels for 5%

profile of v4, /device:TPU:8, one launch (start us, length us, event | category | flops | bytes accessed | tf_op | source)
XLA Modules:
  0.0 93.4 jit_solution(1558304318225209496)
XLA Ops:
  0.6 0.0 copy-start.1
  0.6 2.4 %turn.1 = (bf16[4,2,32,1152]{3,2,1,0:T(8,128)(2,1)}, bf16[3,288,128]{2,1,0:T(8,128)(2,1)S(1)}, bf16[3,288,128]{2,1,0:T(8,128)(2,1)S(1)}, bf16[3,288,128]{2,1,0:T(8,128)(2,1)S(1)}, bf16[3,288,128]{2,1,0:T(8,128)(2,1)S(1)}) custom-call(bf16[128,1152]{1,0:T(8,128)(2,1)} %bitcast.9, bf16[128,1152]{1,0:T(8,128)(2,1)} %bitcast.10, bf16[128,1152]{1,0:T(8,128)(2,1)} %bitcast.11, ...), custom_call_target="tpu_custom_call" | custom-call | flops 3000000000 | tf_op jit(solution)/shard_map/turn/pallas_call | solution.py:115
  3.0 0.1 collective-permute-start
  3.1 3.0 %collective-permute-start.1 = (bf16[3,288,128]{2,1,0:T(8,128)(2,1)S(1)}, bf16[3,288,128]{2,1,0:T(8,128)(2,1)S(1)}, u32[]{:S(2)}, u32[]{:S(2)}) collective-permute-start(bf16[3,288,128]{2,1,0:T(8,128)(2,1)S(1)} %get-tuple-element.38), channel_id=1, source_target_pairs={{0,8},{4,12},{8,0},{12,4},{1,9},{5,13},{9,1},{13,5},{2,10},{6,14},... | collective-permute-start | bytes 663560 | tf_op jit(solution)/shard_map/ppermute | solution.py:404
  6.1 0.5 collective-permute-start.2
  6.6 3.5 %all-to-all-start.1 = ((bf16[4,2,32,1152]{3,2,1,0:T(8,128)(2,1)}), bf16[4,2,32,1152]{3,2,1,0:T(8,128)(2,1)S(1)}, u32[]{:S(2)}, u32[]{:S(2)}) async-start(bf16[4,2,32,1152]{3,2,1,0:T(8,128)(2,1)} %get-tuple-element.40), calls=%async_computation.1 | async-start | bytes 1179648 | tf_op jit(solution)/shard_map/all_to_all | solution.py:429
  10.0 2.0 %collective-permute-done.refs_1_ = bf16[3,288,128]{2,1,0:T(8,128)(2,1)S(1)} collective-permute-done((bf16[3,288,128]{2,1,0:T(8,128)(2,1)S(1)}, bf16[3,288,128]{2,1,0:T(8,128)(2,1)S(1)}, u32[]{:S(2)}, u32[]{:S(2)}) %collective-permute-start) | collective-permute-done | bytes 221216 | tf_op jit(solution)/shard_map/ppermute | solution.py:404
  12.0 9.4 %collective-permute-done.1.refs_2_ = bf16[3,288,128]{2,1,0:T(8,128)(2,1)S(1)} collective-permute-done((bf16[3,288,128]{2,1,0:T(8,128)(2,1)S(1)}, bf16[3,288,128]{2,1,0:T(8,128)(2,1)S(1)}, u32[]{:S(2)}, u32[]{:S(2)}) %collective-permute-start.1) | collective-permute-done | bytes 221216 | tf_op jit(solution)/shard_map/ppermute | solution.py:404
  21.5 4.2 %collective-permute-done.2.refs_3_ = bf16[3,288,128]{2,1,0:T(8,128)(2,1)S(1)} collective-permute-done((bf16[3,288,128]{2,1,0:T(8,128)(2,1)S(1)}, bf16[3,288,128]{2,1,0:T(8,128)(2,1)S(1)}, u32[]{:S(2)}, u32[]{:S(2)}) %collective-permute-start.2) | collective-permute-done | bytes 221216 | tf_op jit(solution)/shard_map/ppermute | solution.py:404
  25.7 2.5 %space_fwd.1 = bf16[16,72,128]{2,1,0:T(8,128)(2,1)} custom-call(f32[2,72]{1,0:T(2,128)S(1)} %copy-done.1, bf16[3,288,128]{2,1,0:T(8,128)(2,1)S(1)} %get-tuple-element.41.refs_0_, bf16[3,288,128]{2,1,0:T(8,128)(2,1)S(1)} %collective-permute-done.refs_1_, bf16[3,288,128]{2,1,0:T(8,128)(2,1)S(1)} %collective-permute-done.1.refs_2_, ...), custom_call_target="tpu_custom_call" | custom-call | flops 4000000000 | tf_op jit(solution)/shard_map/space_fwd/pallas_call | solution.py:192
  28.2 0.0 all-to-all-done.1.pair_ref
  28.2 5.3 %all-to-all-start = ((bf16[16,72,128]{2,1,0:T(8,128)(2,1)}), bf16[16,72,128]{2,1,0:T(8,128)(2,1)S(1)}, u32[]{:S(2)}, u32[]{:S(2)}) async-start(bf16[16,72,128]{2,1,0:T(8,128)(2,1)} %space_fwd.1), calls=%async_computation | async-start | bytes 589824 | tf_op jit(solution)/shard_map/all_to_all | solution.py:431
  33.5 1.9 %space_weights.1 = (bf16[4,512,512]{2,1,0:T(8,128)(2,1)S(1)}, f32[288,512]{1,0:T(8,128)S(1)}) custom-call(f32[2,72]{1,0:T(2,128)S(1)} %copy-done.1, bf16[3,288,128]{2,1,0:T(8,128)(2,1)S(1)} %get-tuple-element.41.refs_0_, bf16[3,288,128]{2,1,0:T(8,128)(2,1)S(1)} %collective-permute-done.refs_1_, bf16[3,288,128]{2,1,0:T(8,128)(2,1)S(1)} %collective-permute-done.1.refs_2_, ...), custom_call_target="tpu_custom_call" | custom-call | flops 8000000000 | tf_op jit(solution)/shard_map/space_weights/pallas_call | solution.py:217
  35.4 1.3 %copy-done.2 = bf16[4,512,512]{2,1,0:T(8,128)(2,1)} copy-done((bf16[4,512,512]{2,1,0:T(8,128)(2,1)}, bf16[4,512,512]{2,1,0:T(8,128)(2,1)S(1)}, u32[]{:S(2)}) %copy-start.2) | copy-done | bytes 2097176
  36.7 5.6 %all-to-all-done.att_ref = bf16[16,72,128]{2,1,0:T(8,128)(2,1)S(1)} async-done(((bf16[16,72,128]{2,1,0:T(8,128)(2,1)}), bf16[16,72,128]{2,1,0:T(8,128)(2,1)S(1)}, u32[]{:S(2)}, u32[]{:S(2)}) %all-to-all-start) | async-done | bytes 294944 | tf_op jit(solution)/shard_map/all_to_all | solution.py:431
  42.3 10.0 %middle.1 = (bf16[16,72,128]{2,1,0:T(8,128)(2,1)S(1)}, bf16[32,1152]{1,0:T(8,128)(2,1)S(1)}, bf16[32,1152]{1,0:T(8,128)(2,1)S(1)}, bf16[32,1152]{1,0:T(8,128)(2,1)S(1)}, bf16[32,1152]{1,0:T(8,128)(2,1)S(1)}) custom-call(bf16[16,72,128]{2,1,0:T(8,128)(2,1)S(1)} %all-to-all-done.att_ref, bf16[4,2,32,1152]{3,2,1,0:T(8,128)(2,1)S(1)} %all-to-all-done.1.pair_ref, ...), custom_call_target="tpu_custom_call" | custom-call | flops 10000000000 | tf_op jit(solution)/shard_map/middle/pallas_call | solution.py:378
  52.3 13.5 %all_to_all.15.up_ref = bf16[16,72,128]{2,1,0:T(8,128)(2,1)S(1)} all-to-all(bf16[16,72,128]{2,1,0:T(8,128)(2,1)S(1)} %get-tuple-element.51), channel_id=1, replica_groups=mesh['grp'=2,'seq'=4,'frm'=4] {'seq','frm'}, dimensions={0} | all-to-all | bytes 589824 | tf_op jit(solution)/shard_map/all_to_all | solution.py:436
  65.8 0.0 copy-done.3
  65.8 2.9 %space_bwd.1 = (bf16[3,288,128]{2,1,0:T(8,128)(2,1)S(1)}, bf16[3,288,128]{2,1,0:T(8,128)(2,1)S(1)}, bf16[3,288,128]{2,1,0:T(8,128)(2,1)S(1)}, bf16[3,288,128]{2,1,0:T(8,128)(2,1)S(1)}) custom-call(f32[2,72]{1,0:T(2,128)S(1)} %copy-done.1, bf16[4,512,512]{2,1,0:T(8,128)(2,1)S(1)} %copy-done.3, f32[288,512]{1,0:T(8,128)S(1)} %get-tuple-element.48.att_ref, ...), custom_call_target="tpu_custom_call" | custom-call | flops 6000000000 | tf_op jit(solution)/shard_map/space_bwd/pallas_call | solution.py:278
  68.6 1.9 %collective-permute-start.3 = (bf16[3,288,128]{2,1,0:T(8,128)(2,1)S(1)}, bf16[3,288,128]{2,1,0:T(8,128)(2,1)S(1)}, u32[]{:S(2)}, u32[]{:S(2)}) collective-permute-start(bf16[3,288,128]{2,1,0:T(8,128)(2,1)S(1)} %get-tuple-element.53), channel_id=1, source_target_pairs={{0,4},{4,0},{8,12},{12,8},{1,5},{5,1},{9,13},{13,9},{2,6},{6,2},{1... | collective-permute-start | bytes 663560 | tf_op jit(solution)/shard_map/ppermute | solution.py:404
  70.6 1.2 %collective-permute-start.4 = (bf16[3,288,128]{2,1,0:T(8,128)(2,1)S(1)}, bf16[3,288,128]{2,1,0:T(8,128)(2,1)S(1)}, u32[]{:S(2)}, u32[]{:S(2)}) collective-permute-start(bf16[3,288,128]{2,1,0:T(8,128)(2,1)S(1)} %get-tuple-element.54), channel_id=1, source_target_pairs={{0,8},{4,12},{8,0},{12,4},{1,9},{5,13},{9,1},{13,5},{2,10},{6,14},... | collective-permute-start | bytes 663560 | tf_op jit(solution)/shard_map/ppermute | solution.py:404
  71.8 0.4 collective-permute-start.5
  72.2 6.6 %collective-permute-done.3.refs_1_ = bf16[3,288,128]{2,1,0:T(8,128)(2,1)S(1)} collective-permute-done((bf16[3,288,128]{2,1,0:T(8,128)(2,1)S(1)}, bf16[3,288,128]{2,1,0:T(8,128)(2,1)S(1)}, u32[]{:S(2)}, u32[]{:S(2)}) %collective-permute-start.3) | collective-permute-done | bytes 221216 | tf_op jit(solution)/shard_map/ppermute | solution.py:404
  78.8 0.0 collective-permute-start.6
  78.8 0.7 collective-permute-start.7
  79.5 1.1 %collective-permute-start.8 = (bf16[32,1152]{1,0:T(8,128)(2,1)S(1)}, bf16[32,1152]{1,0:T(8,128)(2,1)S(1)}, u32[]{:S(2)}, u32[]{:S(2)}) collective-permute-start(bf16[32,1152]{1,0:T(8,128)(2,1)S(1)} %get-tuple-element.63), channel_id=1, source_target_pairs={{0,3},{1,2},{2,1},{3,0},{4,7},{5,6},{6,5},{7,4},{8,11},{9,10},{10,... | collective-permute-start | bytes 221192 | tf_op jit(solution)/shard_map/ppermute | solution.py:404
  80.6 6.5 %collective-permute-done.4.refs_2_ = bf16[3,288,128]{2,1,0:T(8,128)(2,1)S(1)} collective-permute-done((bf16[3,288,128]{2,1,0:T(8,128)(2,1)S(1)}, bf16[3,288,128]{2,1,0:T(8,128)(2,1)S(1)}, u32[]{:S(2)}, u32[]{:S(2)}) %collective-permute-start.4) | collective-permute-done | bytes 221216 | tf_op jit(solution)/shard_map/ppermute | solution.py:404
  87.2 5.0 %collective-permute-done.5.refs_3_ = bf16[3,288,128]{2,1,0:T(8,128)(2,1)S(1)} collective-permute-done((bf16[3,288,128]{2,1,0:T(8,128)(2,1)S(1)}, bf16[3,288,128]{2,1,0:T(8,128)(2,1)S(1)}, u32[]{:S(2)}, u32[]{:S(2)}) %collective-permute-start.5) | collective-permute-done | bytes 221216 | tf_op jit(solution)/shard_map/ppermute | solution.py:404
  92.2 0.0 collective-permute-done.6.refs_5_
  92.2 0.0 collective-permute-done.7.refs_6_
  92.2 0.0 collective-permute-done.8.refs_7_
  92.2 1.2 %unturn.1 = (bf16[128,1152]{1,0:T(8,128)(2,1)}, bf16[128,1152]{1,0:T(8,128)(2,1)}, bf16[128,1152]{1,0:T(8,128)(2,1)}, bf16[4,32,1152]{2,1,0:T(8,128)(2,1)}) custom-call(bf16[3,288,128]{2,1,0:T(8,128)(2,1)S(1)} %get-tuple-element.52.refs_0_, bf16[3,288,128]{2,1,0:T(8,128)(2,1)S(1)} %collective-permute-done.3.refs_1_, ...), custom_call_target="tpu_custom_call" | custom-call | flops 3000000000 | tf_op jit(solution)/shard_map/unturn/pallas_call | solution.py:149
  (5 shorter events, 0.0 us)
Async XLA Ops:
  0.6 25.1 %copy-start.1 = (f32[2,72]{1,0:T(2,128)S(1)}, f32[2,72]{1,0:T(2,128)}, u32[]{:S(2)}) copy-start(f32[2,72]{1,0:T(2,128)} %gain_ref.7) | copy-start | bytes 1732
  3.0 9.0 %collective-permute-start = (bf16[3,288,128]{2,1,0:T(8,128)(2,1)S(1)}, bf16[3,288,128]{2,1,0:T(8,128)(2,1)S(1)}, u32[]{:S(2)}, u32[]{:S(2)}) collective-permute-start(bf16[3,288,128]{2,1,0:T(8,128)(2,1)S(1)} %get-tuple-element.37), channel_id=1, source_target_pairs={{0,4},{4,0},{8,12},{12,8},{1,5},{5,1},{9,13},{13,9},{2,6},{6,2},{1... | collective-permute-start | bytes 663560 | tf_op jit(solution)/shard_map/ppermute | solution.py:404
  3.1 18.4 %collective-permute-start.1 = (bf16[3,288,128]{2,1,0:T(8,128)(2,1)S(1)}, bf16[3,288,128]{2,1,0:T(8,128)(2,1)S(1)}, u32[]{:S(2)}, u32[]{:S(2)}) collective-permute-start(bf16[3,288,128]{2,1,0:T(8,128)(2,1)S(1)} %get-tuple-element.38), channel_id=1, source_target_pairs={{0,8},{4,12},{8,0},{12,4},{1,9},{5,13},{9,1},{13,5},{2,10},{6,14},... | collective-permute-start | bytes 663560 | tf_op jit(solution)/shard_map/ppermute | solution.py:404
  6.1 19.6 %collective-permute-start.2 = (bf16[3,288,128]{2,1,0:T(8,128)(2,1)S(1)}, bf16[3,288,128]{2,1,0:T(8,128)(2,1)S(1)}, u32[]{:S(2)}, u32[]{:S(2)}) collective-permute-start(bf16[3,288,128]{2,1,0:T(8,128)(2,1)S(1)} %get-tuple-element.39), channel_id=1, source_target_pairs={{0,12},{4,8},{8,4},{12,0},{1,13},{5,9},{9,5},{13,1},{2,14},{6,10},... | collective-permute-start | bytes 663560 | tf_op jit(solution)/shard_map/ppermute | solution.py:404
  6.6 21.7 %all-to-all-start.1 = ((bf16[4,2,32,1152]{3,2,1,0:T(8,128)(2,1)}), bf16[4,2,32,1152]{3,2,1,0:T(8,128)(2,1)S(1)}, u32[]{:S(2)}, u32[]{:S(2)}) async-start(bf16[4,2,32,1152]{3,2,1,0:T(8,128)(2,1)} %get-tuple-element.40), calls=%async_computation.1 | async-start | bytes 1179648 | tf_op jit(solution)/shard_map/all_to_all | solution.py:429
  28.2 14.1 %all-to-all-start = ((bf16[16,72,128]{2,1,0:T(8,128)(2,1)}), bf16[16,72,128]{2,1,0:T(8,128)(2,1)S(1)}, u32[]{:S(2)}, u32[]{:S(2)}) async-start(bf16[16,72,128]{2,1,0:T(8,128)(2,1)} %space_fwd.1), calls=%async_computation | async-start | bytes 589824 | tf_op jit(solution)/shard_map/all_to_all | solution.py:431
  33.5 8.8 %copy-start = (f32[2,72]{1,0:T(2,128)S(1)}, f32[2,72]{1,0:T(2,128)}, u32[]{:S(2)}) copy-start(f32[2,72]{1,0:T(2,128)} %gain_ref.6) | copy-start | bytes 1732
  35.4 1.3 %copy-start.2 = (bf16[4,512,512]{2,1,0:T(8,128)(2,1)}, bf16[4,512,512]{2,1,0:T(8,128)(2,1)S(1)}, u32[]{:S(2)}) copy-start(bf16[4,512,512]{2,1,0:T(8,128)(2,1)S(1)} %get-tuple-element.47.weight_ref) | copy-start | bytes 6291460
  42.3 23.5 %copy-start.3 = (bf16[4,512,512]{2,1,0:T(8,128)(2,1)S(1)}, bf16[4,512,512]{2,1,0:T(8,128)(2,1)}, u32[]{:S(2)}) copy-start(bf16[4,512,512]{2,1,0:T(8,128)(2,1)} %copy-done.2) | copy-start | bytes 6291460
  68.6 10.1 %collective-permute-start.3 = (bf16[3,288,128]{2,1,0:T(8,128)(2,1)S(1)}, bf16[3,288,128]{2,1,0:T(8,128)(2,1)S(1)}, u32[]{:S(2)}, u32[]{:S(2)}) collective-permute-start(bf16[3,288,128]{2,1,0:T(8,128)(2,1)S(1)} %get-tuple-element.53), channel_id=1, source_target_pairs={{0,4},{4,0},{8,12},{12,8},{1,5},{5,1},{9,13},{13,9},{2,6},{6,2},{1... | collective-permute-start | bytes 663560 | tf_op jit(solution)/shard_map/ppermute | solution.py:404
  70.6 16.6 %collective-permute-start.4 = (bf16[3,288,128]{2,1,0:T(8,128)(2,1)S(1)}, bf16[3,288,128]{2,1,0:T(8,128)(2,1)S(1)}, u32[]{:S(2)}, u32[]{:S(2)}) collective-permute-start(bf16[3,288,128]{2,1,0:T(8,128)(2,1)S(1)} %get-tuple-element.54), channel_id=1, source_target_pairs={{0,8},{4,12},{8,0},{12,4},{1,9},{5,13},{9,1},{13,5},{2,10},{6,14},... | collective-permute-start | bytes 663560 | tf_op jit(solution)/shard_map/ppermute | solution.py:404
  71.8 20.4 %collective-permute-start.5 = (bf16[3,288,128]{2,1,0:T(8,128)(2,1)S(1)}, bf16[3,288,128]{2,1,0:T(8,128)(2,1)S(1)}, u32[]{:S(2)}, u32[]{:S(2)}) collective-permute-start(bf16[3,288,128]{2,1,0:T(8,128)(2,1)S(1)} %get-tuple-element.55), channel_id=1, source_target_pairs={{0,12},{4,8},{8,4},{12,0},{1,13},{5,9},{9,5},{13,1},{2,14},{6,10},... | collective-permute-start | bytes 663560 | tf_op jit(solution)/shard_map/ppermute | solution.py:404
  78.8 13.4 %collective-permute-start.6 = (bf16[32,1152]{1,0:T(8,128)(2,1)S(1)}, bf16[32,1152]{1,0:T(8,128)(2,1)S(1)}, u32[]{:S(2)}, u32[]{:S(2)}) collective-permute-start(bf16[32,1152]{1,0:T(8,128)(2,1)S(1)} %get-tuple-element.61), channel_id=1, source_target_pairs={{0,1},{1,0},{2,3},{3,2},{4,5},{5,4},{6,7},{7,6},{8,9},{9,8},{10,11... | collective-permute-start | bytes 221192 | tf_op jit(solution)/shard_map/ppermute | solution.py:404
  78.8 13.4 %collective-permute-start.7 = (bf16[32,1152]{1,0:T(8,128)(2,1)S(1)}, bf16[32,1152]{1,0:T(8,128)(2,1)S(1)}, u32[]{:S(2)}, u32[]{:S(2)}) collective-permute-start(bf16[32,1152]{1,0:T(8,128)(2,1)S(1)} %get-tuple-element.62), channel_id=1, source_target_pairs={{0,2},{1,3},{2,0},{3,1},{4,6},{5,7},{6,4},{7,5},{8,10},{9,11},{10,... | collective-permute-start | bytes 221192 | tf_op jit(solution)/shard_map/ppermute | solution.py:404
  79.5 12.7 %collective-permute-start.8 = (bf16[32,1152]{1,0:T(8,128)(2,1)S(1)}, bf16[32,1152]{1,0:T(8,128)(2,1)S(1)}, u32[]{:S(2)}, u32[]{:S(2)}) collective-permute-start(bf16[32,1152]{1,0:T(8,128)(2,1)S(1)} %get-tuple-element.63), channel_id=1, source_target_pairs={{0,3},{1,2},{2,1},{3,0},{4,7},{5,6},{6,5},{7,4},{8,11},{9,10},{10,... | collective-permute-start | bytes 221192 | tf_op jit(solution)/shard_map/ppermute | solution.py:404

commit v5 on v4

--- a/solution.py
+++ b/solution.py
@@ -91,42 +91,64 @@
 
 
 def turn_kernel(axis, *refs):
-    in_refs, both_ref, out_refs = refs[:5], refs[5], refs[6:-3]
+    in_refs, out_refs = refs[:3], refs[3:-3]
     landed, held, sems = refs[-3:]
     rows = out_refs[0].shape[1]
-    parts, _, own, width = both_ref.shape
     me = lax.axis_index(axis)
     copies = [pltpu.make_async_copy(ref, landed.at[n], sems.at[n]) for n, ref in enumerate(in_refs)]
     for copy in copies:
         copy.start()
-    for n in range(3):
-        copies[n].wait()
+    for n, copy in enumerate(copies):
+        copy.wait()
         held[n] = landed[n].T
-    for n in range(2):
-        copies[3 + n].wait()
-        both_ref[:, n] = landed[3 + n].reshape(parts, own, width)
     for s, ref in enumerate(out_refs):
         start = pl.multiple_of((me ^ s) * rows, rows)
         ref[...] = held[:, pl.ds(start, rows), :]
 
 
-def turn(axis, count, parts, arrays, frames):
+def turn(axis, count, arrays):
     tokens, width = arrays[0].shape
-    outs = pl.pallas_call(
+    return pl.pallas_call(
         functools.partial(turn_kernel, axis),
-        out_shape=[jax.ShapeDtypeStruct((parts, 2, tokens // parts, width), BF16)]
-        + [jax.ShapeDtypeStruct((3, width // count, tokens), BF16)] * count,
-        in_specs=[pl.BlockSpec(memory_space=pltpu.HBM)] * 5,
+        out_shape=[jax.ShapeDtypeStruct((3, width // count, tokens), BF16)] * count,
+        in_specs=[pl.BlockSpec(memory_space=pltpu.HBM)] * 3,
         scratch_shapes=[
-            pltpu.VMEM((5, tokens, width), BF16),
+            pltpu.VMEM((3, tokens, width), BF16),
             pltpu.VMEM((3, width, tokens), BF16),
-            pltpu.SemaphoreType.DMA((5,)),
+            pltpu.SemaphoreType.DMA((3,)),
         ],
         compiler_params=PARAMS,
         cost_estimate=cost(3),
         name="turn",
-    )(*(in_hbm(array) for array in (*arrays, *frames)))
-    return outs[0], outs[1:]
+    )(*(in_hbm(array) for array in arrays))
+
+
+def frames_kernel(res_hbm, cot_hbm, both_ref, landed, sems):
+    parts, _, own, width = both_ref.shape
+    copies = [
+        pltpu.make_async_copy(ref, landed.at[n], sems.at[n]) for n, ref in enumerate((res_hbm, cot_hbm))
+    ]
+    for copy in copies:
+        copy.start()
+    for n, copy in enumerate(copies):
+        copy.wait()
+        both_ref[:, n] = landed[n].reshape(parts, own, width)
+
+
+def frames(parts, residual, cotangent):
+    tokens, width = residual.shape
+    return pl.pallas_call(
+        frames_kernel,
+        out_shape=jax.ShapeDtypeStruct((parts, 2, tokens // parts, width), BF16),
+        in_specs=[pl.BlockSpec(memory_space=pltpu.HBM)] * 2,
+        scratch_shapes=[
+            pltpu.VMEM((2, tokens, width), BF16),
+            pltpu.SemaphoreType.DMA((2,)),
+        ],
+        compiler_params=PARAMS,
+        cost_estimate=cost(2),
+        name="frames",
+    )(in_hbm(residual), in_hbm(cotangent))
 
 
 def unturn_kernel(axis, frame_axis, count, *refs):
@@ -418,13 +440,9 @@
     cotangent,
 ):
     tokens, width = residual.shape[1:]
-    both, own = turn(
-        "seq",
-        count,
-        parts,
-        (spatial_query[0], spatial_key[0], spatial_value[0]),
-        (residual[0], cotangent[0]),
-    )
+    own = turn("seq", count, (spatial_query[0], spatial_key[0], spatial_value[0]))
+    residual, cotangent, _ = lax.optimization_barrier((residual, cotangent, own[0]))
+    both = frames(parts, residual[0], cotangent[0])
     held = [swap(own[s], "seq", count, s) for s in range(count)]
     both = lax.all_to_all(both, "frm", 0, 0, tiled=True)
     sent = space_fwd("seq", parts, space_gains, held)

time: 93.7 us -> 92.9 us (level)
  waiting for transfers between devices: 39.4 us -> 37.4 us
  Pallas kernels: 20.8 us -> 21.8 us
    ppermute x9, waiting for transfers between devices: 33.8 us -> 31.8 us  [swap(): return lax.ppermute(array, axis, [(n, n ^ s) for n in range(count)])]
    pallas_call x0 -> x1, Pallas kernels: none -> 1.92 us  [frames(): pl.pallas_call(frames_kernel, out_shape=jax.ShapeDtypeStruct((parts, 2, t...]
  transfers between devices with their start and end apart: 11 -> 11, of which waited for: 7 -> 7; matrix products, arithmetic and copies ran while one was open for 0% -> 0% of each run, Pallas kernels for 5% -> 7%
where the time goes in v5:
time: 92.9 us; the launch traced here: 92.5 us
  waiting for transfers between devices  37.4 us (40%)
  Pallas kernels  21.8 us (23%)
  starting transfers between devices  17.7 us (19%)
  blocking collectives  13.5 us (15%)
  local copies, waits for them, and re-layouts  1.34 us (1%)
    ppermute x9, waiting for transfers between devices, swap(): return lax.ppermute(array, axis, [(n, n ^ s) for n in range(count)])  31.8 us
    all_to_all x1, blocking collectives, local(): up = lax.all_to_all(up, ('seq', 'frm'), 0, 0, tiled=True)  13.5 us
    pallas_call x1, Pallas kernels, middle(): pl.pallas_call(functools.partial(middle_kernel, frame_axis, count, parts)...  9.98 us
    ppermute x9, starting transfers between devices, swap(): return lax.ppermute(array, axis, [(n, n ^ s) for n in range(count)])  8.95 us
    all_to_all x1, waiting for transfers between devices, local(): att = lax.all_to_all(sent, ('seq', 'frm'), 0, 0, tiled=True)  5.59 us
    all_to_all x1, starting transfers between devices, local(): att = lax.all_to_all(sent, ('seq', 'frm'), 0, 0, tiled=True)  5.28 us
    all_to_all x1, starting transfers between devices, local(): both = lax.all_to_all(both, 'frm', 0, 0, tiled=True)  3.49 us
    pallas_call x1, Pallas kernels, space_bwd(): pl.pallas_call(functools.partial(space_bwd_kernel, axis, parts), out_shap...  2.85 us
  transfers between devices with their start and end apart: 11, of which 7 were waited for; matrix products, arithmetic and copies ran while one was open for 0% of the time, Pallas kernels for 7%

profile of v5, /device:TPU:8, one launch (start us, length us, event | category | flops | bytes accessed | tf_op | source)
XLA Modules:
  0.0 92.5 jit_solution(4532072886001911402)
XLA Ops:
  0.6 1.5 %turn.1 = (bf16[3,288,128]{2,1,0:T(8,128)(2,1)S(1)}, bf16[3,288,128]{2,1,0:T(8,128)(2,1)S(1)}, bf16[3,288,128]{2,1,0:T(8,128)(2,1)S(1)}, bf16[3,288,128]{2,1,0:T(8,128)(2,1)S(1)}) custom-call(bf16[128,1152]{1,0:T(8,128)(2,1)} %bitcast.9, bf16[128,1152]{1,0:T(8,128)(2,1)} %bitcast.10, bf16[128,1152]{1,0:T(8,128)(2,1)} %bitcast.11), custom_call_target="tpu_custom_call" | custom-call | flops 3000000000 | tf_op jit(solution)/shard_map/turn/pallas_call | solution.py:111
  2.1 0.1 collective-permute-start
  2.2 3.0 %collective-permute-start.1 = (bf16[3,288,128]{2,1,0:T(8,128)(2,1)S(1)}, bf16[3,288,128]{2,1,0:T(8,128)(2,1)S(1)}, u32[]{:S(2)}, u32[]{:S(2)}) collective-permute-start(bf16[3,288,128]{2,1,0:T(8,128)(2,1)S(1)} %get-tuple-element.39), channel_id=1, source_target_pairs={{0,8},{4,12},{8,0},{12,4},{1,9},{5,13},{9,1},{13,5},{2,10},{6,14},... | collective-permute-start | bytes 663560 | tf_op jit(solution)/shard_map/ppermute | solution.py:426
  5.2 0.5 collective-permute-start.2
  5.7 1.9 %frames.1 = bf16[4,2,32,1152]{3,2,1,0:T(8,128)(2,1)} custom-call(bf16[128,1152]{1,0:T(8,128)(2,1)} %bitcast.12, bf16[128,1152]{1,0:T(8,128)(2,1)} %bitcast.13), custom_call_target="tpu_custom_call" | custom-call | flops 2000000000 | tf_op jit(solution)/shard_map/frames/pallas_call | solution.py:140
  7.6 3.5 %all-to-all-start.1 = ((bf16[4,2,32,1152]{3,2,1,0:T(8,128)(2,1)}), bf16[4,2,32,1152]{3,2,1,0:T(8,128)(2,1)S(1)}, u32[]{:S(2)}, u32[]{:S(2)}) async-start(bf16[4,2,32,1152]{3,2,1,0:T(8,128)(2,1)} %frames.1), calls=%async_computation.1 | async-start | bytes 1179648 | tf_op jit(solution)/shard_map/all_to_all | solution.py:447
  11.1 0.1 collective-permute-done.refs_1_
  11.2 9.4 %collective-permute-done.1.refs_2_ = bf16[3,288,128]{2,1,0:T(8,128)(2,1)S(1)} collective-permute-done((bf16[3,288,128]{2,1,0:T(8,128)(2,1)S(1)}, bf16[3,288,128]{2,1,0:T(8,128)(2,1)S(1)}, u32[]{:S(2)}, u32[]{:S(2)}) %collective-permute-start.1) | collective-permute-done | bytes 221216 | tf_op jit(solution)/shard_map/ppermute | solution.py:426
  20.6 4.2 %collective-permute-done.2.refs_3_ = bf16[3,288,128]{2,1,0:T(8,128)(2,1)S(1)} collective-permute-done((bf16[3,288,128]{2,1,0:T(8,128)(2,1)S(1)}, bf16[3,288,128]{2,1,0:T(8,128)(2,1)S(1)}, u32[]{:S(2)}, u32[]{:S(2)}) %collective-permute-start.2) | collective-permute-done | bytes 221216 | tf_op jit(solution)/shard_map/ppermute | solution.py:426
  24.8 0.0 copy-done.1
  24.8 2.5 %space_fwd.1 = bf16[16,72,128]{2,1,0:T(8,128)(2,1)} custom-call(f32[2,72]{1,0:T(2,128)S(1)} %copy-done.1, bf16[3,288,128]{2,1,0:T(8,128)(2,1)S(1)} %get-tuple-element.43.refs_0_, bf16[3,288,128]{2,1,0:T(8,128)(2,1)S(1)} %collective-permute-done.refs_1_, bf16[3,288,128]{2,1,0:T(8,128)(2,1)S(1)} %collective-permute-done.1.refs_2_, ...), custom_call_target="tpu_custom_call" | custom-call | flops 4000000000 | tf_op jit(solution)/shard_map/space_fwd/pallas_call | solution.py:214
  27.3 0.0 all-to-all-done.1.pair_ref
  27.3 5.3 %all-to-all-start = ((bf16[16,72,128]{2,1,0:T(8,128)(2,1)}), bf16[16,72,128]{2,1,0:T(8,128)(2,1)S(1)}, u32[]{:S(2)}, u32[]{:S(2)}) async-start(bf16[16,72,128]{2,1,0:T(8,128)(2,1)} %space_fwd.1), calls=%async_computation | async-start | bytes 589824 | tf_op jit(solution)/shard_map/all_to_all | solution.py:449
  32.6 1.9 %space_weights.1 = (bf16[4,512,512]{2,1,0:T(8,128)(2,1)S(1)}, f32[288,512]{1,0:T(8,128)S(1)}) custom-call(f32[2,72]{1,0:T(2,128)S(1)} %copy-done.1, bf16[3,288,128]{2,1,0:T(8,128)(2,1)S(1)} %get-tuple-element.43.refs_0_, bf16[3,288,128]{2,1,0:T(8,128)(2,1)S(1)} %collective-permute-done.refs_1_, bf16[3,288,128]{2,1,0:T(8,128)(2,1)S(1)} %collective-permute-done.1.refs_2_, ...), custom_call_target="tpu_custom_call" | custom-call | flops 8000000000 | tf_op jit(solution)/shard_map/space_weights/pallas_call | solution.py:239
  34.5 1.3 %copy-done.2 = bf16[4,512,512]{2,1,0:T(8,128)(2,1)} copy-done((bf16[4,512,512]{2,1,0:T(8,128)(2,1)}, bf16[4,512,512]{2,1,0:T(8,128)(2,1)S(1)}, u32[]{:S(2)}) %copy-start.2) | copy-done | bytes 2097176
  35.8 5.6 %all-to-all-done.att_ref = bf16[16,72,128]{2,1,0:T(8,128)(2,1)S(1)} async-done(((bf16[16,72,128]{2,1,0:T(8,128)(2,1)}), bf16[16,72,128]{2,1,0:T(8,128)(2,1)S(1)}, u32[]{:S(2)}, u32[]{:S(2)}) %all-to-all-start) | async-done | bytes 294944 | tf_op jit(solution)/shard_map/all_to_all | solution.py:449
  41.4 10.0 %middle.1 = (bf16[16,72,128]{2,1,0:T(8,128)(2,1)S(1)}, bf16[32,1152]{1,0:T(8,128)(2,1)S(1)}, bf16[32,1152]{1,0:T(8,128)(2,1)S(1)}, bf16[32,1152]{1,0:T(8,128)(2,1)S(1)}, bf16[32,1152]{1,0:T(8,128)(2,1)S(1)}) custom-call(bf16[16,72,128]{2,1,0:T(8,128)(2,1)S(1)} %all-to-all-done.att_ref, bf16[4,2,32,1152]{3,2,1,0:T(8,128)(2,1)S(1)} %all-to-all-done.1.pair_ref, ...), custom_call_target="tpu_custom_call" | custom-call | flops 10000000000 | tf_op jit(solution)/shard_map/middle/pallas_call | solution.py:400
  51.4 13.5 %all_to_all.15.up_ref = bf16[16,72,128]{2,1,0:T(8,128)(2,1)S(1)} all-to-all(bf16[16,72,128]{2,1,0:T(8,128)(2,1)S(1)} %get-tuple-element.53), channel_id=1, replica_groups=mesh['grp'=2,'seq'=4,'frm'=4] {'seq','frm'}, dimensions={0} | all-to-all | bytes 589824 | tf_op jit(solution)/shard_map/all_to_all | solution.py:454
  64.9 2.9 %space_bwd.1 = (bf16[3,288,128]{2,1,0:T(8,128)(2,1)S(1)}, bf16[3,288,128]{2,1,0:T(8,128)(2,1)S(1)}, bf16[3,288,128]{2,1,0:T(8,128)(2,1)S(1)}, bf16[3,288,128]{2,1,0:T(8,128)(2,1)S(1)}) custom-call(f32[2,72]{1,0:T(2,128)S(1)} %copy-done.1, bf16[4,512,512]{2,1,0:T(8,128)(2,1)S(1)} %copy-done.3, f32[288,512]{1,0:T(8,128)S(1)} %get-tuple-element.50.att_ref, ...), custom_call_target="tpu_custom_call" | custom-call | flops 6000000000 | tf_op jit(solution)/shard_map/space_bwd/pallas_call | solution.py:300
  67.7 1.9 %collective-permute-start.3 = (bf16[3,288,128]{2,1,0:T(8,128)(2,1)S(1)}, bf16[3,288,128]{2,1,0:T(8,128)(2,1)S(1)}, u32[]{:S(2)}, u32[]{:S(2)}) collective-permute-start(bf16[3,288,128]{2,1,0:T(8,128)(2,1)S(1)} %get-tuple-element.55), channel_id=1, source_target_pairs={{0,4},{4,0},{8,12},{12,8},{1,5},{5,1},{9,13},{13,9},{2,6},{6,2},{1... | collective-permute-start | bytes 663560 | tf_op jit(solution)/shard_map/ppermute | solution.py:426
  69.7 1.2 %collective-permute-start.4 = (bf16[3,288,128]{2,1,0:T(8,128)(2,1)S(1)}, bf16[3,288,128]{2,1,0:T(8,128)(2,1)S(1)}, u32[]{:S(2)}, u32[]{:S(2)}) collective-permute-start(bf16[3,288,128]{2,1,0:T(8,128)(2,1)S(1)} %get-tuple-element.56), channel_id=1, source_target_pairs={{0,8},{4,12},{8,0},{12,4},{1,9},{5,13},{9,1},{13,5},{2,10},{6,14},... | collective-permute-start | bytes 663560 | tf_op jit(solution)/shard_map/ppermute | solution.py:426
  70.9 0.4 collective-permute-start.5
  71.3 6.6 %collective-permute-done.3.refs_1_ = bf16[3,288,128]{2,1,0:T(8,128)(2,1)S(1)} collective-permute-done((bf16[3,288,128]{2,1,0:T(8,128)(2,1)S(1)}, bf16[3,288,128]{2,1,0:T(8,128)(2,1)S(1)}, u32[]{:S(2)}, u32[]{:S(2)}) %collective-permute-start.3) | collective-permute-done | bytes 221216 | tf_op jit(solution)/shard_map/ppermute | solution.py:426
  77.9 0.0 collective-permute-start.6
  77.9 0.7 collective-permute-start.7
  78.6 1.1 %collective-permute-start.8 = (bf16[32,1152]{1,0:T(8,128)(2,1)S(1)}, bf16[32,1152]{1,0:T(8,128)(2,1)S(1)}, u32[]{:S(2)}, u32[]{:S(2)}) collective-permute-start(bf16[32,1152]{1,0:T(8,128)(2,1)S(1)} %get-tuple-element.65), channel_id=1, source_target_pairs={{0,3},{1,2},{2,1},{3,0},{4,7},{5,6},{6,5},{7,4},{8,11},{9,10},{10,... | collective-permute-start | bytes 221192 | tf_op jit(solution)/shard_map/ppermute | solution.py:426
  79.7 6.5 %collective-permute-done.4.refs_2_ = bf16[3,288,128]{2,1,0:T(8,128)(2,1)S(1)} collective-permute-done((bf16[3,288,128]{2,1,0:T(8,128)(2,1)S(1)}, bf16[3,288,128]{2,1,0:T(8,128)(2,1)S(1)}, u32[]{:S(2)}, u32[]{:S(2)}) %collective-permute-start.4) | collective-permute-done | bytes 221216 | tf_op jit(solution)/shard_map/ppermute | solution.py:426
  86.3 5.0 %collective-permute-done.5.refs_3_ = bf16[3,288,128]{2,1,0:T(8,128)(2,1)S(1)} collective-permute-done((bf16[3,288,128]{2,1,0:T(8,128)(2,1)S(1)}, bf16[3,288,128]{2,1,0:T(8,128)(2,1)S(1)}, u32[]{:S(2)}, u32[]{:S(2)}) %collective-permute-start.5) | collective-permute-done | bytes 221216 | tf_op jit(solution)/shard_map/ppermute | solution.py:426
  91.3 0.0 collective-permute-done.6.refs_5_
  91.3 0.0 collective-permute-done.7.refs_6_
  91.3 0.0 collective-permute-done.8.refs_7_
  91.3 1.2 %unturn.1 = (bf16[128,1152]{1,0:T(8,128)(2,1)}, bf16[128,1152]{1,0:T(8,128)(2,1)}, bf16[128,1152]{1,0:T(8,128)(2,1)}, bf16[4,32,1152]{2,1,0:T(8,128)(2,1)}) custom-call(bf16[3,288,128]{2,1,0:T(8,128)(2,1)S(1)} %get-tuple-element.54.refs_0_, bf16[3,288,128]{2,1,0:T(8,128)(2,1)S(1)} %collective-permute-done.3.refs_1_, ...), custom_call_target="tpu_custom_call" | custom-call | flops 3000000000 | tf_op jit(solution)/shard_map/unturn/pallas_call | solution.py:171
  (6 shorter events, 0.0 us)
Async XLA Ops:
  2.1 9.0 %collective-permute-start = (bf16[3,288,128]{2,1,0:T(8,128)(2,1)S(1)}, bf16[3,288,128]{2,1,0:T(8,128)(2,1)S(1)}, u32[]{:S(2)}, u32[]{:S(2)}) collective-permute-start(bf16[3,288,128]{2,1,0:T(8,128)(2,1)S(1)} %get-tuple-element.38), channel_id=1, source_target_pairs={{0,4},{4,0},{8,12},{12,8},{1,5},{5,1},{9,13},{13,9},{2,6},{6,2},{1... | collective-permute-start | bytes 663560 | tf_op jit(solution)/shard_map/ppermute | solution.py:426
  2.2 18.4 %collective-permute-start.1 = (bf16[3,288,128]{2,1,0:T(8,128)(2,1)S(1)}, bf16[3,288,128]{2,1,0:T(8,128)(2,1)S(1)}, u32[]{:S(2)}, u32[]{:S(2)}) collective-permute-start(bf16[3,288,128]{2,1,0:T(8,128)(2,1)S(1)} %get-tuple-element.39), channel_id=1, source_target_pairs={{0,8},{4,12},{8,0},{12,4},{1,9},{5,13},{9,1},{13,5},{2,10},{6,14},... | collective-permute-start | bytes 663560 | tf_op jit(solution)/shard_map/ppermute | solution.py:426
  5.2 19.6 %collective-permute-start.2 = (bf16[3,288,128]{2,1,0:T(8,128)(2,1)S(1)}, bf16[3,288,128]{2,1,0:T(8,128)(2,1)S(1)}, u32[]{:S(2)}, u32[]{:S(2)}) collective-permute-start(bf16[3,288,128]{2,1,0:T(8,128)(2,1)S(1)} %get-tuple-element.40), channel_id=1, source_target_pairs={{0,12},{4,8},{8,4},{12,0},{1,13},{5,9},{9,5},{13,1},{2,14},{6,10},... | collective-permute-start | bytes 663560 | tf_op jit(solution)/shard_map/ppermute | solution.py:426
  5.7 19.1 %copy-start.1 = (f32[2,72]{1,0:T(2,128)S(1)}, f32[2,72]{1,0:T(2,128)}, u32[]{:S(2)}) copy-start(f32[2,72]{1,0:T(2,128)} %gain_ref.7) | copy-start | bytes 1732
  7.6 19.7 %all-to-all-start.1 = ((bf16[4,2,32,1152]{3,2,1,0:T(8,128)(2,1)}), bf16[4,2,32,1152]{3,2,1,0:T(8,128)(2,1)S(1)}, u32[]{:S(2)}, u32[]{:S(2)}) async-start(bf16[4,2,32,1152]{3,2,1,0:T(8,128)(2,1)} %frames.1), calls=%async_computation.1 | async-start | bytes 1179648 | tf_op jit(solution)/shard_map/all_to_all | solution.py:447
  27.3 14.1 %all-to-all-start = ((bf16[16,72,128]{2,1,0:T(8,128)(2,1)}), bf16[16,72,128]{2,1,0:T(8,128)(2,1)S(1)}, u32[]{:S(2)}, u32[]{:S(2)}) async-start(bf16[16,72,128]{2,1,0:T(8,128)(2,1)} %space_fwd.1), calls=%async_computation | async-start | bytes 589824 | tf_op jit(solution)/shard_map/all_to_all | solution.py:449
  32.6 8.8 %copy-start = (f32[2,72]{1,0:T(2,128)S(1)}, f32[2,72]{1,0:T(2,128)}, u32[]{:S(2)}) copy-start(f32[2,72]{1,0:T(2,128)} %gain_ref.6) | copy-start | bytes 1732
  34.5 1.3 %copy-start.2 = (bf16[4,512,512]{2,1,0:T(8,128)(2,1)}, bf16[4,512,512]{2,1,0:T(8,128)(2,1)S(1)}, u32[]{:S(2)}) copy-start(bf16[4,512,512]{2,1,0:T(8,128)(2,1)S(1)} %get-tuple-element.49.weight_ref) | copy-start | bytes 6291460
  41.4 23.5 %copy-start.3 = (bf16[4,512,512]{2,1,0:T(8,128)(2,1)S(1)}, bf16[4,512,512]{2,1,0:T(8,128)(2,1)}, u32[]{:S(2)}) copy-start(bf16[4,512,512]{2,1,0:T(8,128)(2,1)} %copy-done.2) | copy-start | bytes 6291460
  67.7 10.1 %collective-permute-start.3 = (bf16[3,288,128]{2,1,0:T(8,128)(2,1)S(1)}, bf16[3,288,128]{2,1,0:T(8,128)(2,1)S(1)}, u32[]{:S(2)}, u32[]{:S(2)}) collective-permute-start(bf16[3,288,128]{2,1,0:T(8,128)(2,1)S(1)} %get-tuple-element.55), channel_id=1, source_target_pairs={{0,4},{4,0},{8,12},{12,8},{1,5},{5,1},{9,13},{13,9},{2,6},{6,2},{1... | collective-permute-start | bytes 663560 | tf_op jit(solution)/shard_map/ppermute | solution.py:426
  69.7 16.6 %collective-permute-start.4 = (bf16[3,288,128]{2,1,0:T(8,128)(2,1)S(1)}, bf16[3,288,128]{2,1,0:T(8,128)(2,1)S(1)}, u32[]{:S(2)}, u32[]{:S(2)}) collective-permute-start(bf16[3,288,128]{2,1,0:T(8,128)(2,1)S(1)} %get-tuple-element.56), channel_id=1, source_target_pairs={{0,8},{4,12},{8,0},{12,4},{1,9},{5,13},{9,1},{13,5},{2,10},{6,14},... | collective-permute-start | bytes 663560 | tf_op jit(solution)/shard_map/ppermute | solution.py:426
  70.9 20.4 %collective-permute-start.5 = (bf16[3,288,128]{2,1,0:T(8,128)(2,1)S(1)}, bf16[3,288,128]{2,1,0:T(8,128)(2,1)S(1)}, u32[]{:S(2)}, u32[]{:S(2)}) collective-permute-start(bf16[3,288,128]{2,1,0:T(8,128)(2,1)S(1)} %get-tuple-element.57), channel_id=1, source_target_pairs={{0,12},{4,8},{8,4},{12,0},{1,13},{5,9},{9,5},{13,1},{2,14},{6,10},... | collective-permute-start | bytes 663560 | tf_op jit(solution)/shard_map/ppermute | solution.py:426
  77.9 13.4 %collective-permute-start.6 = (bf16[32,1152]{1,0:T(8,128)(2,1)S(1)}, bf16[32,1152]{1,0:T(8,128)(2,1)S(1)}, u32[]{:S(2)}, u32[]{:S(2)}) collective-permute-start(bf16[32,1152]{1,0:T(8,128)(2,1)S(1)} %get-tuple-element.63), channel_id=1, source_target_pairs={{0,1},{1,0},{2,3},{3,2},{4,5},{5,4},{6,7},{7,6},{8,9},{9,8},{10,11... | collective-permute-start | bytes 221192 | tf_op jit(solution)/shard_map/ppermute | solution.py:426
  77.9 13.4 %collective-permute-start.7 = (bf16[32,1152]{1,0:T(8,128)(2,1)S(1)}, bf16[32,1152]{1,0:T(8,128)(2,1)S(1)}, u32[]{:S(2)}, u32[]{:S(2)}) collective-permute-start(bf16[32,1152]{1,0:T(8,128)(2,1)S(1)} %get-tuple-element.64), channel_id=1, source_target_pairs={{0,2},{1,3},{2,0},{3,1},{4,6},{5,7},{6,4},{7,5},{8,10},{9,11},{10,... | collective-permute-start | bytes 221192 | tf_op jit(solution)/shard_map/ppermute | solution.py:426
  78.6 12.7 %collective-permute-start.8 = (bf16[32,1152]{1,0:T(8,128)(2,1)S(1)}, bf16[32,1152]{1,0:T(8,128)(2,1)S(1)}, u32[]{:S(2)}, u32[]{:S(2)}) collective-permute-start(bf16[32,1152]{1,0:T(8,128)(2,1)S(1)} %get-tuple-element.65), channel_id=1, source_target_pairs={{0,3},{1,2},{2,1},{3,0},{4,7},{5,6},{6,5},{7,4},{8,11},{9,10},{10,... | collective-permute-start | bytes 221192 | tf_op jit(solution)/shard_map/ppermute | solution.py:426

commit v6 on v5

--- a/solution.py
+++ b/solution.py
@@ -186,8 +186,7 @@
 def head_expons(query, key, query_gain, key_gain):
     query_nrm = (head_norm(query)[0] * query_gain).astype(BF16)
     key_nrm = (head_norm(key)[0] * key_gain).astype(BF16)
-    expons = jnp.exp(dot(key_nrm, query_nrm, ((0,), (0,))) * (HD ** (-0.5)))
-    return expons, 1.0 / jnp.sum(expons, axis=0, keepdims=True)
+    return jnp.exp(dot(key_nrm, query_nrm, ((0,), (0,))) * (HD ** (-0.5)))
 
 
 def space_fwd_kernel(axis, parts, gain_ref, *refs):
@@ -197,11 +196,13 @@
     me = lax.axis_index(axis)
     query, key, value = (gather_part(in_refs, n) for n in range(3))
     query_gain, key_gain = (column(gain_ref[n : n + 1]) for n in range(2))
+    ones = jnp.ones((8, query.shape[1]), F32)
     for h in range(rows // HD):
         cut = slice(h * HD, (h + 1) * HD)
-        expons, scale = head_expons(query[cut], key[cut], query_gain, key_gain)
-        attended = dot(value[cut].astype(BF16), expons.astype(BF16), ((1,), (0,)))
-        held[cut, :] = attended * scale
+        expons = head_expons(query[cut], key[cut], query_gain, key_gain)
+        rows_in = jnp.concatenate([value[cut], ones], axis=0).astype(BF16)
+        attended = dot(rows_in, expons.astype(BF16), ((1,), (0,)))
+        held[cut, :] = attended[:HD] * (1.0 / attended[HD : HD + 1])
     for s in range(count):
         blocks = pack(held[:, s * LANES : (s + 1) * LANES], parts)
         for f, block in enumerate(blocks):
@@ -227,8 +228,8 @@
     query_gain, key_gain = (column(gain_ref[n : n + 1]) for n in range(2))
     for h in range(weight_ref.shape[0]):
         cut = slice(h * HD, (h + 1) * HD)
-        expons, scale = head_expons(query[cut], key[cut], query_gain, key_gain)
-        weights = (expons * scale).astype(BF16)
+        expons = head_expons(query[cut], key[cut], query_gain, key_gain)
+        weights = (expons * (1.0 / jnp.sum(expons, axis=0, keepdims=True))).astype(BF16)
         weight_ref[h] = weights
         att_ref[cut, :] = dot(value[cut].astype(BF16), weights, ((1,), (0,)))
 

time: 92.9 us -> 92.8 us (level)
  no operation moved by 1% of the time
where the time goes in v6:
time: 92.8 us; the launch traced here: 92.5 us
  waiting for transfers between devices  37.4 us (40%)
  Pallas kernels  21.8 us (23%)
  starting transfers between devices  17.7 us (19%)
  blocking collectives  13.5 us (15%)
  local copies, waits for them, and re-layouts  1.34 us (1%)
    ppermute x9, waiting for transfers between devices, swap(): return lax.ppermute(array, axis, [(n, n ^ s) for n in range(count)])  31.8 us
    all_to_all x1, blocking collectives, local(): up = lax.all_to_all(up, ('seq', 'frm'), 0, 0, tiled=True)  13.5 us
    pallas_call x1, Pallas kernels, middle(): pl.pallas_call(functools.partial(middle_kernel, frame_axis, count, parts)...  9.98 us
    ppermute x9, starting transfers between devices, swap(): return lax.ppermute(array, axis, [(n, n ^ s) for n in range(count)])  8.95 us
    all_to_all x1, waiting for transfers between devices, local(): att = lax.all_to_all(sent, ('seq', 'frm'), 0, 0, tiled=True)  5.59 us
    all_to_all x1, starting transfers between devices, local(): att = lax.all_to_all(sent, ('seq', 'frm'), 0, 0, tiled=True)  5.29 us
    all_to_all x1, starting transfers between devices, local(): both = lax.all_to_all(both, 'frm', 0, 0, tiled=True)  3.49 us
    pallas_call x1, Pallas kernels, space_bwd(): pl.pallas_call(functools.partial(space_bwd_kernel, axis, parts), out_shap...  2.85 us
  transfers between devices with their start and end apart: 11, of which 7 were waited for; matrix products, arithmetic and copies ran while one was open for 0% of the time, Pallas kernels for 7%

profile of v6, /device:TPU:8, one launch (start us, length us, event | category | flops | bytes accessed | tf_op | source)
XLA Modules:
  0.0 92.5 jit_solution(17384708075462223905)
XLA Ops:
  0.6 1.5 %turn.1 = (bf16[3,288,128]{2,1,0:T(8,128)(2,1)S(1)}, bf16[3,288,128]{2,1,0:T(8,128)(2,1)S(1)}, bf16[3,288,128]{2,1,0:T(8,128)(2,1)S(1)}, bf16[3,288,128]{2,1,0:T(8,128)(2,1)S(1)}) custom-call(bf16[128,1152]{1,0:T(8,128)(2,1)} %bitcast.9, bf16[128,1152]{1,0:T(8,128)(2,1)} %bitcast.10, bf16[128,1152]{1,0:T(8,128)(2,1)} %bitcast.11), custom_call_target="tpu_custom_call" | custom-call | flops 3000000000 | tf_op jit(solution)/shard_map/turn/pallas_call | solution.py:111
  2.1 0.1 collective-permute-start
  2.2 3.0 %collective-permute-start.1 = (bf16[3,288,128]{2,1,0:T(8,128)(2,1)S(1)}, bf16[3,288,128]{2,1,0:T(8,128)(2,1)S(1)}, u32[]{:S(2)}, u32[]{:S(2)}) collective-permute-start(bf16[3,288,128]{2,1,0:T(8,128)(2,1)S(1)} %get-tuple-element.39), channel_id=1, source_target_pairs={{0,8},{4,12},{8,0},{12,4},{1,9},{5,13},{9,1},{13,5},{2,10},{6,14},... | collective-permute-start | bytes 663560 | tf_op jit(solution)/shard_map/ppermute | solution.py:427
  5.2 0.5 collective-permute-start.2
  5.7 1.9 %frames.1 = bf16[4,2,32,1152]{3,2,1,0:T(8,128)(2,1)} custom-call(bf16[128,1152]{1,0:T(8,128)(2,1)} %bitcast.12, bf16[128,1152]{1,0:T(8,128)(2,1)} %bitcast.13), custom_call_target="tpu_custom_call" | custom-call | flops 2000000000 | tf_op jit(solution)/shard_map/frames/pallas_call | solution.py:140
  7.6 3.5 %all-to-all-start.1 = ((bf16[4,2,32,1152]{3,2,1,0:T(8,128)(2,1)}), bf16[4,2,32,1152]{3,2,1,0:T(8,128)(2,1)S(1)}, u32[]{:S(2)}, u32[]{:S(2)}) async-start(bf16[4,2,32,1152]{3,2,1,0:T(8,128)(2,1)} %frames.1), calls=%async_computation.1 | async-start | bytes 1179648 | tf_op jit(solution)/shard_map/all_to_all | solution.py:448
  11.1 0.1 collective-permute-done.refs_1_
  11.2 9.4 %collective-permute-done.1.refs_2_ = bf16[3,288,128]{2,1,0:T(8,128)(2,1)S(1)} collective-permute-done((bf16[3,288,128]{2,1,0:T(8,128)(2,1)S(1)}, bf16[3,288,128]{2,1,0:T(8,128)(2,1)S(1)}, u32[]{:S(2)}, u32[]{:S(2)}) %collective-permute-start.1) | collective-permute-done | bytes 221216 | tf_op jit(solution)/shard_map/ppermute | solution.py:427
  20.6 4.2 %collective-permute-done.2.refs_3_ = bf16[3,288,128]{2,1,0:T(8,128)(2,1)S(1)} collective-permute-done((bf16[3,288,128]{2,1,0:T(8,128)(2,1)S(1)}, bf16[3,288,128]{2,1,0:T(8,128)(2,1)S(1)}, u32[]{:S(2)}, u32[]{:S(2)}) %collective-permute-start.2) | collective-permute-done | bytes 221216 | tf_op jit(solution)/shard_map/ppermute | solution.py:427
  24.8 2.4 %space_fwd.1 = bf16[16,72,128]{2,1,0:T(8,128)(2,1)} custom-call(f32[2,72]{1,0:T(2,128)S(1)} %copy-done.1, bf16[3,288,128]{2,1,0:T(8,128)(2,1)S(1)} %get-tuple-element.43.refs_0_, bf16[3,288,128]{2,1,0:T(8,128)(2,1)S(1)} %collective-permute-done.refs_1_, bf16[3,288,128]{2,1,0:T(8,128)(2,1)S(1)} %collective-permute-done.1.refs_2_, ...), custom_call_target="tpu_custom_call" | custom-call | flops 4000000000 | tf_op jit(solution)/shard_map/space_fwd/pallas_call | solution.py:215
  27.2 0.0 all-to-all-done.1.pair_ref
  27.2 5.3 %all-to-all-start = ((bf16[16,72,128]{2,1,0:T(8,128)(2,1)}), bf16[16,72,128]{2,1,0:T(8,128)(2,1)S(1)}, u32[]{:S(2)}, u32[]{:S(2)}) async-start(bf16[16,72,128]{2,1,0:T(8,128)(2,1)} %space_fwd.1), calls=%async_computation | async-start | bytes 589824 | tf_op jit(solution)/shard_map/all_to_all | solution.py:450
  32.5 1.9 %space_weights.1 = (bf16[4,512,512]{2,1,0:T(8,128)(2,1)S(1)}, f32[288,512]{1,0:T(8,128)S(1)}) custom-call(f32[2,72]{1,0:T(2,128)S(1)} %copy-done.1, bf16[3,288,128]{2,1,0:T(8,128)(2,1)S(1)} %get-tuple-element.43.refs_0_, bf16[3,288,128]{2,1,0:T(8,128)(2,1)S(1)} %collective-permute-done.refs_1_, bf16[3,288,128]{2,1,0:T(8,128)(2,1)S(1)} %collective-permute-done.1.refs_2_, ...), custom_call_target="tpu_custom_call" | custom-call | flops 8000000000 | tf_op jit(solution)/shard_map/space_weights/pallas_call | solution.py:240
  34.4 1.3 %copy-done.2 = bf16[4,512,512]{2,1,0:T(8,128)(2,1)} copy-done((bf16[4,512,512]{2,1,0:T(8,128)(2,1)}, bf16[4,512,512]{2,1,0:T(8,128)(2,1)S(1)}, u32[]{:S(2)}) %copy-start.2) | copy-done | bytes 2097176
  35.7 5.6 %all-to-all-done.att_ref = bf16[16,72,128]{2,1,0:T(8,128)(2,1)S(1)} async-done(((bf16[16,72,128]{2,1,0:T(8,128)(2,1)}), bf16[16,72,128]{2,1,0:T(8,128)(2,1)S(1)}, u32[]{:S(2)}, u32[]{:S(2)}) %all-to-all-start) | async-done | bytes 294944 | tf_op jit(solution)/shard_map/all_to_all | solution.py:450
  41.3 10.0 %middle.1 = (bf16[16,72,128]{2,1,0:T(8,128)(2,1)S(1)}, bf16[32,1152]{1,0:T(8,128)(2,1)S(1)}, bf16[32,1152]{1,0:T(8,128)(2,1)S(1)}, bf16[32,1152]{1,0:T(8,128)(2,1)S(1)}, bf16[32,1152]{1,0:T(8,128)(2,1)S(1)}) custom-call(bf16[16,72,128]{2,1,0:T(8,128)(2,1)S(1)} %all-to-all-done.att_ref, bf16[4,2,32,1152]{3,2,1,0:T(8,128)(2,1)S(1)} %all-to-all-done.1.pair_ref, ...), custom_call_target="tpu_custom_call" | custom-call | flops 10000000000 | tf_op jit(solution)/shard_map/middle/pallas_call | solution.py:401
  51.3 13.5 %all_to_all.15.up_ref = bf16[16,72,128]{2,1,0:T(8,128)(2,1)S(1)} all-to-all(bf16[16,72,128]{2,1,0:T(8,128)(2,1)S(1)} %get-tuple-element.53), channel_id=1, replica_groups=mesh['grp'=2,'seq'=4,'frm'=4] {'seq','frm'}, dimensions={0} | all-to-all | bytes 589824 | tf_op jit(solution)/shard_map/all_to_all | solution.py:455
  64.8 0.0 copy-done.3
  64.8 2.9 %space_bwd.1 = (bf16[3,288,128]{2,1,0:T(8,128)(2,1)S(1)}, bf16[3,288,128]{2,1,0:T(8,128)(2,1)S(1)}, bf16[3,288,128]{2,1,0:T(8,128)(2,1)S(1)}, bf16[3,288,128]{2,1,0:T(8,128)(2,1)S(1)}) custom-call(f32[2,72]{1,0:T(2,128)S(1)} %copy-done.1, bf16[4,512,512]{2,1,0:T(8,128)(2,1)S(1)} %copy-done.3, f32[288,512]{1,0:T(8,128)S(1)} %get-tuple-element.50.att_ref, ...), custom_call_target="tpu_custom_call" | custom-call | flops 6000000000 | tf_op jit(solution)/shard_map/space_bwd/pallas_call | solution.py:301
  67.7 1.9 %collective-permute-start.3 = (bf16[3,288,128]{2,1,0:T(8,128)(2,1)S(1)}, bf16[3,288,128]{2,1,0:T(8,128)(2,1)S(1)}, u32[]{:S(2)}, u32[]{:S(2)}) collective-permute-start(bf16[3,288,128]{2,1,0:T(8,128)(2,1)S(1)} %get-tuple-element.55), channel_id=1, source_target_pairs={{0,4},{4,0},{8,12},{12,8},{1,5},{5,1},{9,13},{13,9},{2,6},{6,2},{1... | collective-permute-start | bytes 663560 | tf_op jit(solution)/shard_map/ppermute | solution.py:427
  69.6 1.2 %collective-permute-start.4 = (bf16[3,288,128]{2,1,0:T(8,128)(2,1)S(1)}, bf16[3,288,128]{2,1,0:T(8,128)(2,1)S(1)}, u32[]{:S(2)}, u32[]{:S(2)}) collective-permute-start(bf16[3,288,128]{2,1,0:T(8,128)(2,1)S(1)} %get-tuple-element.56), channel_id=1, source_target_pairs={{0,8},{4,12},{8,0},{12,4},{1,9},{5,13},{9,1},{13,5},{2,10},{6,14},... | collective-permute-start | bytes 663560 | tf_op jit(solution)/shard_map/ppermute | solution.py:427
  70.8 0.4 collective-permute-start.5
  71.2 6.6 %collective-permute-done.3.refs_1_ = bf16[3,288,128]{2,1,0:T(8,128)(2,1)S(1)} collective-permute-done((bf16[3,288,128]{2,1,0:T(8,128)(2,1)S(1)}, bf16[3,288,128]{2,1,0:T(8,128)(2,1)S(1)}, u32[]{:S(2)}, u32[]{:S(2)}) %collective-permute-start.3) | collective-permute-done | bytes 221216 | tf_op jit(solution)/shard_map/ppermute | solution.py:427
  77.8 0.0 collective-permute-start.6
  77.8 0.7 collective-permute-start.7
  78.5 1.1 %collective-permute-start.8 = (bf16[32,1152]{1,0:T(8,128)(2,1)S(1)}, bf16[32,1152]{1,0:T(8,128)(2,1)S(1)}, u32[]{:S(2)}, u32[]{:S(2)}) collective-permute-start(bf16[32,1152]{1,0:T(8,128)(2,1)S(1)} %get-tuple-element.65), channel_id=1, source_target_pairs={{0,3},{1,2},{2,1},{3,0},{4,7},{5,6},{6,5},{7,4},{8,11},{9,10},{10,... | collective-permute-start | bytes 221192 | tf_op jit(solution)/shard_map/ppermute | solution.py:427
  79.7 6.5 %collective-permute-done.4.refs_2_ = bf16[3,288,128]{2,1,0:T(8,128)(2,1)S(1)} collective-permute-done((bf16[3,288,128]{2,1,0:T(8,128)(2,1)S(1)}, bf16[3,288,128]{2,1,0:T(8,128)(2,1)S(1)}, u32[]{:S(2)}, u32[]{:S(2)}) %collective-permute-start.4) | collective-permute-done | bytes 221216 | tf_op jit(solution)/shard_map/ppermute | solution.py:427
  86.2 5.0 %collective-permute-done.5.refs_3_ = bf16[3,288,128]{2,1,0:T(8,128)(2,1)S(1)} collective-permute-done((bf16[3,288,128]{2,1,0:T(8,128)(2,1)S(1)}, bf16[3,288,128]{2,1,0:T(8,128)(2,1)S(1)}, u32[]{:S(2)}, u32[]{:S(2)}) %collective-permute-start.5) | collective-permute-done | bytes 221216 | tf_op jit(solution)/shard_map/ppermute | solution.py:427
  91.2 0.0 collective-permute-done.6.refs_5_
  91.2 0.0 collective-permute-done.7.refs_6_
  91.2 0.0 collective-permute-done.8.refs_7_
  91.2 1.2 %unturn.1 = (bf16[128,1152]{1,0:T(8,128)(2,1)}, bf16[128,1152]{1,0:T(8,128)(2,1)}, bf16[128,1152]{1,0:T(8,128)(2,1)}, bf16[4,32,1152]{2,1,0:T(8,128)(2,1)}) custom-call(bf16[3,288,128]{2,1,0:T(8,128)(2,1)S(1)} %get-tuple-element.54.refs_0_, bf16[3,288,128]{2,1,0:T(8,128)(2,1)S(1)} %collective-permute-done.3.refs_1_, ...), custom_call_target="tpu_custom_call" | custom-call | flops 3000000000 | tf_op jit(solution)/shard_map/unturn/pallas_call | solution.py:171
  (6 shorter events, 0.0 us)
Async XLA Ops:
  2.1 9.0 %collective-permute-start = (bf16[3,288,128]{2,1,0:T(8,128)(2,1)S(1)}, bf16[3,288,128]{2,1,0:T(8,128)(2,1)S(1)}, u32[]{:S(2)}, u32[]{:S(2)}) collective-permute-start(bf16[3,288,128]{2,1,0:T(8,128)(2,1)S(1)} %get-tuple-element.38), channel_id=1, source_target_pairs={{0,4},{4,0},{8,12},{12,8},{1,5},{5,1},{9,13},{13,9},{2,6},{6,2},{1... | collective-permute-start | bytes 663560 | tf_op jit(solution)/shard_map/ppermute | solution.py:427
  2.2 18.4 %collective-permute-start.1 = (bf16[3,288,128]{2,1,0:T(8,128)(2,1)S(1)}, bf16[3,288,128]{2,1,0:T(8,128)(2,1)S(1)}, u32[]{:S(2)}, u32[]{:S(2)}) collective-permute-start(bf16[3,288,128]{2,1,0:T(8,128)(2,1)S(1)} %get-tuple-element.39), channel_id=1, source_target_pairs={{0,8},{4,12},{8,0},{12,4},{1,9},{5,13},{9,1},{13,5},{2,10},{6,14},... | collective-permute-start | bytes 663560 | tf_op jit(solution)/shard_map/ppermute | solution.py:427
  5.2 19.6 %collective-permute-start.2 = (bf16[3,288,128]{2,1,0:T(8,128)(2,1)S(1)}, bf16[3,288,128]{2,1,0:T(8,128)(2,1)S(1)}, u32[]{:S(2)}, u32[]{:S(2)}) collective-permute-start(bf16[3,288,128]{2,1,0:T(8,128)(2,1)S(1)} %get-tuple-element.40), channel_id=1, source_target_pairs={{0,12},{4,8},{8,4},{12,0},{1,13},{5,9},{9,5},{13,1},{2,14},{6,10},... | collective-permute-start | bytes 663560 | tf_op jit(solution)/shard_map/ppermute | solution.py:427
  5.7 19.1 %copy-start.1 = (f32[2,72]{1,0:T(2,128)S(1)}, f32[2,72]{1,0:T(2,128)}, u32[]{:S(2)}) copy-start(f32[2,72]{1,0:T(2,128)} %gain_ref.7) | copy-start | bytes 1732
  7.6 19.6 %all-to-all-start.1 = ((bf16[4,2,32,1152]{3,2,1,0:T(8,128)(2,1)}), bf16[4,2,32,1152]{3,2,1,0:T(8,128)(2,1)S(1)}, u32[]{:S(2)}, u32[]{:S(2)}) async-start(bf16[4,2,32,1152]{3,2,1,0:T(8,128)(2,1)} %frames.1), calls=%async_computation.1 | async-start | bytes 1179648 | tf_op jit(solution)/shard_map/all_to_all | solution.py:448
  27.2 14.1 %all-to-all-start = ((bf16[16,72,128]{2,1,0:T(8,128)(2,1)}), bf16[16,72,128]{2,1,0:T(8,128)(2,1)S(1)}, u32[]{:S(2)}, u32[]{:S(2)}) async-start(bf16[16,72,128]{2,1,0:T(8,128)(2,1)} %space_fwd.1), calls=%async_computation | async-start | bytes 589824 | tf_op jit(solution)/shard_map/all_to_all | solution.py:450
  32.5 8.8 %copy-start = (f32[2,72]{1,0:T(2,128)S(1)}, f32[2,72]{1,0:T(2,128)}, u32[]{:S(2)}) copy-start(f32[2,72]{1,0:T(2,128)} %gain_ref.6) | copy-start | bytes 1732
  34.4 1.3 %copy-start.2 = (bf16[4,512,512]{2,1,0:T(8,128)(2,1)}, bf16[4,512,512]{2,1,0:T(8,128)(2,1)S(1)}, u32[]{:S(2)}) copy-start(bf16[4,512,512]{2,1,0:T(8,128)(2,1)S(1)} %get-tuple-element.49.weight_ref) | copy-start | bytes 6291460
  41.3 23.5 %copy-start.3 = (bf16[4,512,512]{2,1,0:T(8,128)(2,1)S(1)}, bf16[4,512,512]{2,1,0:T(8,128)(2,1)}, u32[]{:S(2)}) copy-start(bf16[4,512,512]{2,1,0:T(8,128)(2,1)} %copy-done.2) | copy-start | bytes 6291460
  67.7 10.1 %collective-permute-start.3 = (bf16[3,288,128]{2,1,0:T(8,128)(2,1)S(1)}, bf16[3,288,128]{2,1,0:T(8,128)(2,1)S(1)}, u32[]{:S(2)}, u32[]{:S(2)}) collective-permute-start(bf16[3,288,128]{2,1,0:T(8,128)(2,1)S(1)} %get-tuple-element.55), channel_id=1, source_target_pairs={{0,4},{4,0},{8,12},{12,8},{1,5},{5,1},{9,13},{13,9},{2,6},{6,2},{1... | collective-permute-start | bytes 663560 | tf_op jit(solution)/shard_map/ppermute | solution.py:427
  69.6 16.6 %collective-permute-start.4 = (bf16[3,288,128]{2,1,0:T(8,128)(2,1)S(1)}, bf16[3,288,128]{2,1,0:T(8,128)(2,1)S(1)}, u32[]{:S(2)}, u32[]{:S(2)}) collective-permute-start(bf16[3,288,128]{2,1,0:T(8,128)(2,1)S(1)} %get-tuple-element.56), channel_id=1, source_target_pairs={{0,8},{4,12},{8,0},{12,4},{1,9},{5,13},{9,1},{13,5},{2,10},{6,14},... | collective-permute-start | bytes 663560 | tf_op jit(solution)/shard_map/ppermute | solution.py:427
  70.8 20.4 %collective-permute-start.5 = (bf16[3,288,128]{2,1,0:T(8,128)(2,1)S(1)}, bf16[3,288,128]{2,1,0:T(8,128)(2,1)S(1)}, u32[]{:S(2)}, u32[]{:S(2)}) collective-permute-start(bf16[3,288,128]{2,1,0:T(8,128)(2,1)S(1)} %get-tuple-element.57), channel_id=1, source_target_pairs={{0,12},{4,8},{8,4},{12,0},{1,13},{5,9},{9,5},{13,1},{2,14},{6,10},... | collective-permute-start | bytes 663560 | tf_op jit(solution)/shard_map/ppermute | solution.py:427
  77.8 13.4 %collective-permute-start.6 = (bf16[32,1152]{1,0:T(8,128)(2,1)S(1)}, bf16[32,1152]{1,0:T(8,128)(2,1)S(1)}, u32[]{:S(2)}, u32[]{:S(2)}) collective-permute-start(bf16[32,1152]{1,0:T(8,128)(2,1)S(1)} %get-tuple-element.63), channel_id=1, source_target_pairs={{0,1},{1,0},{2,3},{3,2},{4,5},{5,4},{6,7},{7,6},{8,9},{9,8},{10,11... | collective-permute-start | bytes 221192 | tf_op jit(solution)/shard_map/ppermute | solution.py:427
  77.8 13.4 %collective-permute-start.7 = (bf16[32,1152]{1,0:T(8,128)(2,1)S(1)}, bf16[32,1152]{1,0:T(8,128)(2,1)S(1)}, u32[]{:S(2)}, u32[]{:S(2)}) collective-permute-start(bf16[32,1152]{1,0:T(8,128)(2,1)S(1)} %get-tuple-element.64), channel_id=1, source_target_pairs={{0,2},{1,3},{2,0},{3,1},{4,6},{5,7},{6,4},{7,5},{8,10},{9,11},{10,... | collective-permute-start | bytes 221192 | tf_op jit(solution)/shard_map/ppermute | solution.py:427
  78.5 12.7 %collective-permute-start.8 = (bf16[32,1152]{1,0:T(8,128)(2,1)S(1)}, bf16[32,1152]{1,0:T(8,128)(2,1)S(1)}, u32[]{:S(2)}, u32[]{:S(2)}) collective-permute-start(bf16[32,1152]{1,0:T(8,128)(2,1)S(1)} %get-tuple-element.65), channel_id=1, source_target_pairs={{0,3},{1,2},{2,1},{3,0},{4,7},{5,6},{6,5},{7,4},{8,11},{9,10},{10,... | collective-permute-start | bytes 221192 | tf_op jit(solution)/shard_map/ppermute | solution.py:427
